TPU v7x, 32 devices: a whole 2x2x4 slice. The times are simulated.
32 devices in a mesh: dp: 8 (over z, y), tensor: 4 (over x, core).
Axes of the slice: x: 2, y: 2, z: 4, core: 2. Of those that a mesh axis runs over, the one named last changes fastest.
Arguments:
- tokens: bfloat16 [2, 12288, 768], P(None, ('dp', 'tensor')), may hold values from -6 to 6
- qkv_weight: bfloat16 [3, 768, 768], P(None, 'dp', 'tensor'), may hold values from -0.21875 to 0.21875
- out_weight: bfloat16 [768, 768], P('tensor', 'dp'), may hold values from -2.5 to 2.5
- up_weight: bfloat16 [768, 3072], P('dp', 'tensor'), may hold values from -0.21875 to 0.21875
- down_weight: bfloat16 [3072, 768], P('tensor', 'dp'), may hold values from -0.109375 to 0.109375
- qkv_bias: bfloat16 [2, 768], P(None, 'dp'), may hold values from -3 to 3
- out_bias: bfloat16 [768], P('dp'), may hold values from -3 to 3
- up_bias: bfloat16 [3072], P('dp'), may hold values from -3 to 3
- down_bias: bfloat16 [768], P('dp'), may hold values from -3 to 3
- norm_gain: bfloat16 [2, 768], P(None, 'dp'), may hold values from 0.5 to 1.5
- norm_shift: bfloat16 [2, 768], P(None, 'dp'), may hold values from -3 to 3
- proj_weight: bfloat16 [768, 128], P('dp'), may hold values from -0.21875 to 0.21875
- lengths: int32 [2, 8, 2], P(None, 'dp'), may hold values from 0 to 1536, as said below
- cotangent: bfloat16 [2, 12288, 128], P(None, ('dp', 'tensor')), may hold values from -6 to 6
Outputs:
- embeddings: bfloat16 [2, 12288, 128], P(None, ('dp', 'tensor'))
- input_grad: bfloat16 [2, 12288, 768], P(None, ('dp', 'tensor'))
- qkv_weight_grad: float32 [3, 768, 768], P(None, 'dp', 'tensor')
- out_weight_grad: float32 [768, 768], P('tensor', 'dp')
- up_weight_grad: float32 [768, 3072], P('dp', 'tensor')
- down_weight_grad: float32 [3072, 768], P('tensor', 'dp')
- qkv_bias_grad: float32 [2, 768], P(None, 'dp')
- out_bias_grad: float32 [768], P('dp')
- up_bias_grad: float32 [3072], P('dp')
- down_bias_grad: float32 [768], P('dp')
- norm_gain_grad: float32 [2, 768], P(None, 'dp')
- norm_shift_grad: float32 [2, 768], P(None, 'dp')
- proj_weight_grad: float32 [768, 128], P('dp')
Inputs may be any that keep to these rules, and one draw needn't show every extreme that they name: `lengths`: lengths of a pack's 2 sequences in order from its first row; the first is 1024 or more, together at most 1536, the rest of the pack is padding; the first pack of the first micro-batch is one sequence of 1536 rows.
All inputs are finite; a program needn't handle non-finite values.
Results may differ from a plain program's by a relative error of at most 0.024.
Values may be sent and summed in bfloat16 or wider, within the bound.
No kernel may reach another device: no remote copies, remote signals or barrier semaphores. Data moves between devices by JAX's collectives and lax.ppermute only.
A program may use at most 192 MiB of HBM per device.

v0:
```python
import jax
import jax.numpy as jnp
from jax import lax
from jax.sharding import PartitionSpec as P

HD = 64


EPSILON = 1e-06
MASKED = -1e30


def layer_norm(residual, gain_vec, shift_vec):
    center = residual - jnp.mean(residual, axis=-1, keepdims=True)
    variance = jnp.mean(center * center, axis=-1, keepdims=True)
    return center * lax.rsqrt(variance + EPSILON) * gain_vec + shift_vec


def unit_rows(embedding, valid_rows):
    return (
        valid_rows[:, None]
        * embedding
        * lax.rsqrt(jnp.sum(embedding * embedding, axis=-1, keepdims=True) + EPSILON)
    )


def exact_gelu(hidden):
    return jax.nn.gelu(hidden, approximate=False)


def segment_info(length_row, pack_rows):
    positions = lax.iota(jnp.int32, pack_rows)
    bounds = jnp.cumsum(length_row)
    segments = jnp.sum((positions[:, None] >= bounds[None, :]).astype(jnp.int32), axis=1)
    valid_rows = (positions < bounds[-1]).astype(jnp.float32)
    return (segments, valid_rows)


def gather_forward(shards):
    return (
        lax.all_gather(shards[0], "dp", axis=1, tiled=True),
        lax.all_gather(shards[1], "dp", axis=1, tiled=True),
        lax.all_gather(shards[2], "dp", axis=0, tiled=True),
        lax.all_gather(shards[3], "dp", axis=1, tiled=True),
        lax.all_gather(shards[4], "dp", axis=1, tiled=True),
        lax.all_gather(shards[5], "dp", axis=0, tiled=True),
        lax.all_gather(shards[6], "dp", axis=0, tiled=True),
        lax.all_gather(shards[7], "dp", axis=0, tiled=True),
        lax.all_gather(shards[8], "dp", axis=1, tiled=True),
        lax.all_gather(shards[9], "dp", axis=1, tiled=True),
        lax.all_gather(shards[10], "dp", axis=0, tiled=True),
    )


def gather_backward(shards):
    return (
        lax.all_gather(shards[0], "dp", axis=1, tiled=True),
        lax.all_gather(shards[1], "dp", axis=1, tiled=True),
        lax.all_gather(shards[2], "dp", axis=0, tiled=True),
        lax.all_gather(shards[3], "dp", axis=1, tiled=True),
        lax.all_gather(shards[4], "dp", axis=1, tiled=True),
        lax.all_gather(shards[5], "dp", axis=0, tiled=True),
        lax.all_gather(shards[6], "dp", axis=0, tiled=True),
        lax.all_gather(shards[7], "dp", axis=0, tiled=True),
        lax.all_gather(shards[8], "dp", axis=1, tiled=True),
        lax.all_gather(shards[9], "dp", axis=1, tiled=True),
        lax.all_gather(shards[10], "dp", axis=0, tiled=True),
    )


def reduce_grads(totals):
    shared = (
        lax.psum(totals[4].astype(jnp.bfloat16), "tensor").astype(jnp.float32),
        lax.psum(totals[5].astype(jnp.bfloat16), "tensor").astype(jnp.float32),
        lax.psum(totals[6].astype(jnp.bfloat16), "tensor").astype(jnp.float32),
        lax.psum(totals[7].astype(jnp.bfloat16), "tensor").astype(jnp.float32),
        lax.psum(totals[8].astype(jnp.bfloat16), "tensor").astype(jnp.float32),
        lax.psum(totals[9].astype(jnp.bfloat16), "tensor").astype(jnp.float32),
        lax.psum(totals[10].astype(jnp.bfloat16), "tensor").astype(jnp.float32),
    )
    return (
        lax.psum_scatter(totals[0], "dp", scatter_dimension=1, tiled=True),
        lax.psum_scatter(totals[1], "dp", scatter_dimension=1, tiled=True),
        lax.psum_scatter(totals[2], "dp", scatter_dimension=0, tiled=True),
        lax.psum_scatter(totals[3], "dp", scatter_dimension=1, tiled=True),
        lax.psum_scatter(shared[0], "dp", scatter_dimension=1, tiled=True),
        lax.psum_scatter(shared[1], "dp", scatter_dimension=0, tiled=True),
        lax.psum_scatter(shared[2], "dp", scatter_dimension=0, tiled=True),
        lax.psum_scatter(shared[3], "dp", scatter_dimension=0, tiled=True),
        lax.psum_scatter(shared[4], "dp", scatter_dimension=1, tiled=True),
        lax.psum_scatter(shared[5], "dp", scatter_dimension=1, tiled=True),
        lax.psum_scatter(shared[6], "dp", scatter_dimension=0, tiled=True),
    )


def masked_scores(query_block, keys_heads, seg_block, segments, score_scale):
    scores = (
        jnp.einsum("qhd,khd->hqk", query_block, keys_heads, preferred_element_type=jnp.float32)
        * score_scale
    )
    allowed = seg_block[:, None] == segments[None, :]
    return jnp.where(allowed[None], scores, MASKED)


def attend_forward(queries_heads, keys_heads, values_heads, segments, block_rows, score_scale):
    pack_rows = queries_heads.shape[0]

    def one_block(block_index):
        row_start = block_index * block_rows
        query_block = lax.dynamic_slice_in_dim(queries_heads, row_start, block_rows, 0)
        seg_block = lax.dynamic_slice_in_dim(segments, row_start, block_rows, 0)
        scores = masked_scores(query_block, keys_heads, seg_block, segments, score_scale)
        row_max = jnp.max(scores, axis=-1, keepdims=True)
        exp_scores = jnp.exp(scores - row_max)
        row_total = jnp.sum(exp_scores, axis=-1, keepdims=True)
        attn_probs = (exp_scores / row_total).astype(jnp.bfloat16)
        blended = jnp.einsum(
            "hqk,khd->qhd", attn_probs, values_heads, preferred_element_type=jnp.float32
        )
        return (blended.astype(jnp.bfloat16), (row_max + jnp.log(row_total))[..., 0])

    blended, log_sums = lax.map(one_block, jnp.arange(pack_rows // block_rows, dtype=jnp.int32))
    return (blended.reshape(pack_rows, -1), log_sums)


def attend_backward(
    queries_heads, keys_heads, values_heads, grad_heads, log_sums, segments, block_rows, score_scale
):
    pack_rows = queries_heads.shape[0]

    def one_block(carried, block_index):
        d_keys, d_values = carried
        row_start = block_index * block_rows
        query_block = lax.dynamic_slice_in_dim(queries_heads, row_start, block_rows, 0)
        seg_block = lax.dynamic_slice_in_dim(segments, row_start, block_rows, 0)
        grad_block = lax.dynamic_slice_in_dim(grad_heads, row_start, block_rows, 0)
        scores = masked_scores(query_block, keys_heads, seg_block, segments, score_scale)
        attn_probs = jnp.exp(scores - log_sums[block_index][..., None])
        d_probs = jnp.einsum(
            "qhd,khd->hqk", grad_block, values_heads, preferred_element_type=jnp.float32
        )
        inner_sum = jnp.sum(attn_probs * d_probs, axis=-1, keepdims=True)
        d_scores = (attn_probs * (d_probs - inner_sum)).astype(jnp.bfloat16)
        d_query = (
            jnp.einsum("hqk,khd->qhd", d_scores, keys_heads, preferred_element_type=jnp.float32)
            * score_scale
        )
        d_keys = (
            d_keys
            + jnp.einsum("hqk,qhd->khd", d_scores, query_block, preferred_element_type=jnp.float32)
            * score_scale
        )
        d_values = d_values + jnp.einsum(
            "hqk,qhd->khd",
            attn_probs.astype(jnp.bfloat16),
            grad_block,
            preferred_element_type=jnp.float32,
        )
        return ((d_keys, d_values), d_query.astype(jnp.bfloat16))

    empty = jnp.zeros(keys_heads.shape, jnp.float32)
    (d_keys, d_values), d_queries = lax.scan(
        one_block, (empty, empty), jnp.arange(pack_rows // block_rows, dtype=jnp.int32)
    )
    return (
        d_queries.reshape(pack_rows, -1),
        d_keys.reshape(pack_rows, -1).astype(jnp.bfloat16),
        d_values.reshape(pack_rows, -1).astype(jnp.bfloat16),
    )


def per_device(
    tokens,
    qkv_weight,
    out_weight,
    up_weight,
    down_weight,
    qkv_bias,
    out_bias,
    up_bias,
    down_bias,
    norm_gain,
    norm_shift,
    proj_weight,
    lengths,
    cotangent,
):
    shards = (
        qkv_weight,
        out_weight,
        up_weight,
        down_weight,
        qkv_bias,
        out_bias,
        up_bias,
        down_bias,
        norm_gain,
        norm_shift,
        proj_weight,
    )
    tensor_index = lax.axis_index("tensor")
    tensor_count = lax.axis_size("tensor")
    micro_count = tokens.shape[0]
    local_rows = tokens.shape[1]
    pack_rows = local_rows * tensor_count
    head_cols = qkv_weight.shape[2]
    ffn_cols = up_weight.shape[1]
    heads_here = head_cols // HD
    block_rows = min(512, pack_rows)
    score_scale = HD ** (-0.5)
    totals = None
    reduced = None
    embeds = []
    input_grads = []
    for micro_index in range(micro_count):
        gathered = gather_forward(shards)
        qkv_full, out_full, up_full, down_full = (
            gathered[0],
            gathered[1],
            gathered[2],
            gathered[3],
        )
        qkv_bias_here = lax.dynamic_slice_in_dim(
            gathered[4], tensor_index * head_cols, head_cols, 1
        ).astype(jnp.float32)
        out_bias_all = gathered[5].astype(jnp.float32)
        up_bias_here = lax.dynamic_slice_in_dim(
            gathered[6], tensor_index * ffn_cols, ffn_cols, 0
        ).astype(jnp.float32)
        down_bias_all = gathered[7].astype(jnp.float32)
        gains_all = gathered[8].astype(jnp.float32)
        shifts_all = gathered[9].astype(jnp.float32)
        proj_full = gathered[10]
        tokens_here = tokens[micro_index]
        tokens_pack = lax.all_gather(tokens_here, "tensor", axis=0, tiled=True)
        projected = jnp.einsum(
            "pd,sdc->spc", tokens_pack, qkv_full, preferred_element_type=jnp.float32
        )
        queries = (projected[0] + qkv_bias_here[0]).astype(jnp.bfloat16)
        keys_pack = projected[1].astype(jnp.bfloat16)
        values = (projected[2] + qkv_bias_here[1]).astype(jnp.bfloat16)
        segments, valid_rows = segment_info(lengths[micro_index, 0], pack_rows)
        queries_heads = queries.reshape(pack_rows, heads_here, HD)
        keys_heads = keys_pack.reshape(pack_rows, heads_here, HD)
        values_heads = values.reshape(pack_rows, heads_here, HD)
        attended, log_sums = attend_forward(
            queries_heads, keys_heads, values_heads, segments, block_rows, score_scale
        )
        attn_rows = lax.psum_scatter(
            jnp.dot(attended, out_full, preferred_element_type=jnp.float32).astype(jnp.bfloat16),
            "tensor",
            scatter_dimension=0,
            tiled=True,
        ).astype(jnp.float32)
        resid1 = tokens_here.astype(jnp.float32) + attn_rows + out_bias_all
        normed1 = layer_norm(resid1, gains_all[0], shifts_all[0])
        normed_pack = lax.all_gather(normed1.astype(jnp.bfloat16), "tensor", axis=0, tiled=True)
        hidden = jnp.dot(normed_pack, up_full, preferred_element_type=jnp.float32) + up_bias_here
        active = exact_gelu(hidden).astype(jnp.bfloat16)
        ffn_rows = lax.psum_scatter(
            jnp.dot(active, down_full, preferred_element_type=jnp.float32).astype(jnp.bfloat16),
            "tensor",
            scatter_dimension=0,
            tiled=True,
        ).astype(jnp.float32)
        resid2 = normed1 + ffn_rows + down_bias_all
        normed2 = layer_norm(resid2, gains_all[1], shifts_all[1])
        normed2_low = normed2.astype(jnp.bfloat16)
        embedding = jnp.dot(normed2_low, proj_full, preferred_element_type=jnp.float32)
        valid_here = lax.dynamic_slice_in_dim(valid_rows, tensor_index * local_rows, local_rows, 0)
        embeds.append(unit_rows(embedding, valid_here).astype(jnp.bfloat16))
        back_weights = gather_backward(shards)
        qkv_back, out_back, up_back, down_back = (
            back_weights[0],
            back_weights[1],
            back_weights[2],
            back_weights[3],
        )
        gains_back = back_weights[8].astype(jnp.float32)
        shifts_back = back_weights[9].astype(jnp.float32)
        proj_back = back_weights[10]
        cot_here = cotangent[micro_index].astype(jnp.float32)
        d_embed = jax.vjp(lambda vector: unit_rows(vector, valid_here), embedding)[1](cot_here)[0]
        d_embed_low = d_embed.astype(jnp.bfloat16)
        grad_proj = jnp.einsum(
            "pd,pe->de", normed2_low, d_embed_low, preferred_element_type=jnp.float32
        )
        d_normed2 = jnp.einsum(
            "pe,de->pd", d_embed_low, proj_back, preferred_element_type=jnp.float32
        )
        d_resid2, d_gain2, d_shift2 = jax.vjp(layer_norm, resid2, gains_back[1], shifts_back[1])[1](
            d_normed2
        )
        d_ffn_pack = lax.all_gather(d_resid2.astype(jnp.bfloat16), "tensor", axis=0, tiled=True)
        grad_down = jnp.einsum("pf,pd->fd", active, d_ffn_pack, preferred_element_type=jnp.float32)
        d_active = jnp.einsum(
            "pd,fd->pf", d_ffn_pack, down_back, preferred_element_type=jnp.float32
        )
        d_hidden = jax.vjp(exact_gelu, hidden)[1](d_active)[0].astype(jnp.bfloat16)
        grad_up_bias = jnp.sum(d_hidden, axis=0, dtype=jnp.float32)
        grad_up = jnp.einsum("pd,pf->df", normed_pack, d_hidden, preferred_element_type=jnp.float32)
        d_normed1 = d_resid2 + lax.psum_scatter(
            jnp.einsum("pf,df->pd", d_hidden, up_back, preferred_element_type=jnp.float32).astype(
                jnp.bfloat16
            ),
            "tensor",
            scatter_dimension=0,
            tiled=True,
        ).astype(jnp.float32)
        d_resid1, d_gain1, d_shift1 = jax.vjp(layer_norm, resid1, gains_back[0], shifts_back[0])[1](
            d_normed1
        )
        d_attn_pack = lax.all_gather(d_resid1.astype(jnp.bfloat16), "tensor", axis=0, tiled=True)
        grad_out = jnp.einsum(
            "pc,pd->cd", attended, d_attn_pack, preferred_element_type=jnp.float32
        )
        d_attended = jnp.einsum(
            "pd,cd->pc", d_attn_pack, out_back, preferred_element_type=jnp.float32
        ).astype(jnp.bfloat16)
        d_queries, d_keys, d_values = attend_backward(
            queries_heads,
            keys_heads,
            values_heads,
            d_attended.reshape(pack_rows, heads_here, HD),
            log_sums,
            segments,
            block_rows,
            score_scale,
        )
        d_project = jnp.stack([d_queries, d_keys, d_values])
        grad_qkv = jnp.einsum(
            "pd,spc->sdc", tokens_pack, d_project, preferred_element_type=jnp.float32
        )
        grad_qkv_bias_here = jnp.stack(
            [
                jnp.sum(d_queries, axis=0, dtype=jnp.float32),
                jnp.sum(d_values, axis=0, dtype=jnp.float32),
            ]
        )
        d_tokens = d_resid1 + lax.psum_scatter(
            jnp.einsum(
                "spc,sdc->pd", d_project, qkv_back, preferred_element_type=jnp.float32
            ).astype(jnp.bfloat16),
            "tensor",
            scatter_dimension=0,
            tiled=True,
        ).astype(jnp.float32)
        input_grads.append(d_tokens.astype(jnp.bfloat16))
        grad_qkv_bias = lax.dynamic_update_slice_in_dim(
            jnp.zeros((2, head_cols * tensor_count), jnp.float32),
            grad_qkv_bias_here,
            tensor_index * head_cols,
            1,
        )
        grad_up_bias_all = lax.dynamic_update_slice_in_dim(
            jnp.zeros((ffn_cols * tensor_count,), jnp.float32),
            grad_up_bias,
            tensor_index * ffn_cols,
            0,
        )
        micro_grads = (
            grad_qkv,
            grad_out,
            grad_up,
            grad_down,
            grad_qkv_bias,
            jnp.sum(d_resid1, axis=0),
            grad_up_bias_all,
            jnp.sum(d_resid2, axis=0),
            jnp.stack([d_gain1, d_gain2]),
            jnp.stack([d_shift1, d_shift2]),
            grad_proj,
        )
        totals = micro_grads if totals is None else jax.tree.map(jnp.add, totals, micro_grads)
    reduced = reduce_grads(totals)
    return (
        jnp.stack(embeds),
        jnp.stack(input_grads),
        reduced[0],
        reduced[1],
        reduced[2],
        reduced[3],
        reduced[4],
        reduced[5],
        reduced[6],
        reduced[7],
        reduced[8],
        reduced[9],
        reduced[10],
    )


def solution(mesh):
    in_specs = (
        P(None, ("dp", "tensor"), None),
        P(None, "dp", "tensor"),
        P("tensor", "dp"),
        P("dp", "tensor"),
        P("tensor", "dp"),
        P(None, "dp"),
        P("dp"),
        P("dp"),
        P("dp"),
        P(None, "dp"),
        P(None, "dp"),
        P("dp", None),
        P(None, "dp", None),
        P(None, ("dp", "tensor"), None),
    )
    out_specs = (
        P(None, ("dp", "tensor"), None),
        P(None, ("dp", "tensor"), None),
        P(None, "dp", "tensor"),
        P("tensor", "dp"),
        P("dp", "tensor"),
        P("tensor", "dp"),
        P(None, "dp"),
        P("dp"),
        P("dp"),
        P("dp"),
        P(None, "dp"),
        P(None, "dp"),
        P("dp", None),
    )
    return jax.shard_map(
        per_device, mesh=mesh, in_specs=in_specs, out_specs=out_specs, check_vma=False
    )
```

profile of v0, /device:TPU:0, one launch (start us, length us, event | category | flops | bytes accessed | tf_op | source)
XLA Modules:
  0.0 1445.5 jit_solution(15288791335888852047)
XLA Ops:
  11.7 22.1 %all-gather.2 = bf16[8,96,2]{1,2,0:T(2,128)(2,1)S(1)} all-gather(bf16[1,96,2]{1,2,0:T(2,128)(2,1)S(1)} %bitcast.350), channel_id=1, replica_groups=mesh['dp'=8,'tensor'=4] {'dp'}, dimensions={0}, use_global_device_ids=true | all-gather | bytes 3456 | tf_op jit(solution)/shard_map/all_gather | solution.py:45
  35.8 33.1 %all_gather.41 = bf16[192,768]{0,1:T(8,128)(2,1)} all-gather(bf16[192,96]{0,1:T(8,128)(2,1)S(1)} %copy.88), channel_id=1, replica_groups=mesh['dp'=8,'tensor'=4] {'dp'}, dimensions={1}, use_global_device_ids=true | all-gather | bytes 331776 | tf_op jit(solution)/shard_map/all_gather | solution.py:42
  68.9 34.2 %all_gather.38 = bf16[3,768,192]{2,0,1:T(4,128)(2,1)S(1)} all-gather(bf16[3,96,192]{2,0,1:T(4,128)(2,1)S(1)} %copy.84), channel_id=1, replica_groups=mesh['dp'=8,'tensor'=4] {'dp'}, dimensions={1}, use_global_device_ids=true | all-gather | bytes 995328 | tf_op jit(solution)/shard_map/all_gather | solution.py:41
  117.3 36.2 %while.54 = (s32[]{:T(128)}, bf16[3,512,3,64]{1,3,2,0:T(8,128)(2,1)}, f32[3,3,512]{2,1,0:T(4,128)}, s32[3]{0:T(128)}, s32[1536]{0:T(1024)S(1)}, /*index=5*/bf16[...) while((s32[]{:T(128)}, ...), condition=%wide.region_5.6_spmd, body=%wide.region_2.5_spmd.sunk | while | flops 633174528 | bytes 33093832 | solution.py:122
  159.3 30.8 %while.55 = (s32[]{:T(128)}, bf16[3,512,3,64]{1,3,2,0:T(8,128)(2,1)S(1)}, f32[3,3,512]{2,1,0:T(4,128)S(1)}, s32[3]{0:T(128)S(1)}, s32[1536]{0:T(1024)S(1)}, /*in...) while((s32[]{:T(128)}, ...), condition=%wide.region_18.19_spmd, body=%wide.region_15.18_spmd.sunk | while | flops 633174528 | bytes 33102024 | solution.py:122
  194.8 18.6 %all-gather.3 = bf16[8,96,2]{1,2,0:T(2,128)(2,1)S(1)} all-gather(bf16[1,96,2]{1,2,0:T(2,128)(2,1)S(1)} %bitcast.351), channel_id=1, replica_groups=mesh['dp'=8,'tensor'=4] {'dp'}, dimensions={0}, use_global_device_ids=true | all-gather | bytes 3456 | tf_op jit(solution)/shard_map/all_gather | solution.py:49
  213.4 16.2 %all-gather.4 = bf16[8,96,2]{1,2,0:T(2,128)(2,1)S(1)} all-gather(bf16[1,96,2]{1,2,0:T(2,128)(2,1)S(1)} %bitcast.352), channel_id=1, replica_groups=mesh['dp'=8,'tensor'=4] {'dp'}, dimensions={0}, use_global_device_ids=true | all-gather | bytes 3456 | tf_op jit(solution)/shard_map/all_gather | solution.py:50
  231.3 19.1 %all-reduce.6 = (bf16[768]{0:T(1024)(128)(2,1)S(1)}, bf16[768]{0:T(1024)(128)(2,1)S(1)}) all-reduce(bf16[768]{0:T(1024)(128)(2,1)S(1)} %dynamic-update-slice.2, bf16[768]{0:T(1024)(128)(2,1)S(1)} %dynamic-update-slice.3), channel_id=1, replica_groups=mesh['dp'=8,'tensor'=4] {'dp'}, use_global_device_ids=true, to_apply=%add | all-reduce | flops 1536 | bytes 6144
  258.9 26.3 %all-gather.5 = bf16[8,1,384]{2,1,0:T(2,128)(2,1)S(1)} all-gather(bf16[1,1,384]{2,1,0:T(2,128)(2,1)S(1)} %reshape.513), channel_id=1, replica_groups=mesh['dp'=8,'tensor'=4] {'dp'}, dimensions={0}, use_global_device_ids=true | all-gather | bytes 6912 | tf_op jit(solution)/shard_map/all_gather | solution.py:47
  285.3 6.2 fusion.142
  291.5 13.8 all-gather.17.cloned.1.call-done
  305.4 25.2 %multiply_convert_fusion.3 = (bf16[1536,768]{1,0:T(8,128)(2,1)}, f32[1536,768]{1,0:T(8,128)}, bf16[1536,768]{1,0:T(8,128)(2,1)}, f32[1536,768]{1,0:T(8,128)}, f32[1536,768]{1,0:T(8,128)}) fusion(f32[768]{0:T(1024)S(1)} %dynamic-slice_convert_fusion, f32[1536,768]{1,0:T(8,128)} %fusion.142, bf16[1536,768]{1,0:T(8,128)(2,1)} %all-gather.17.cloned.1.call-done, ...), kind=kOutput, calls=%fused_computation.105 | convolution fusion | flops 1967652864 | bytes 27134976 | tf_op jit(solution)/shard_map/dot_general | solution.py:258
  330.6 18.5 %all-gather.21.cloned.1.call-done = bf16[768,768]{0,1:T(8,128)(2,1)} async-done(((bf16[768,96]{0,1:T(8,128)(2,1)}), bf16[768,768]{0,1:T(8,128)(2,1)}) %all-gather.21.cloned.1.call-update) | async-done | bytes 1179664 | tf_op jit(solution)/shard_map/all_gather | solution.py:44
  354.6 5.5 convolution_convert_fusion.2
  362.8 31.0 %all_gather.92 = bf16[768,128]{1,0:T(8,128)(2,1)S(1)} all-gather(bf16[96,128]{1,0:T(8,128)(2,1)} %param.33), channel_id=1, replica_groups=mesh['dp'=8,'tensor'=4] {'dp'}, dimensions={0}, use_global_device_ids=true | all-gather | bytes 221184 | tf_op jit(solution)/shard_map/all_gather | solution.py:51
  395.1 26.7 %reduce-scatter.33.cloned.1.call-done = bf16[384,768]{1,0:T(8,128)(2,1)} async-done(((bf16[1536,768]{1,0:T(8,128)(2,1)}), bf16[384,768]{1,0:T(8,128)(2,1)}) %reduce-scatter.33.cloned.1.call-update) | async-done | bytes 589840 | tf_op jit(solution)/shard_map/reduce_scatter | solution.py:260
  435.7 21.8 %all-gather.25.cloned.1.call-done = bf16[1536,768]{1,0:T(8,128)(2,1)} async-done(((bf16[384,768]{1,0:T(8,128)(2,1)}), bf16[1536,768]{1,0:T(8,128)(2,1)}) %all-gather.25.cloned.1.call-update) | async-done | bytes 2359312 | tf_op jit(solution)/shard_map/all_gather | solution.py:294
  457.6 6.2 fusion.144
  463.8 19.3 %all-gather.29.cloned.1.call-done = bf16[1536,768]{1,0:T(8,128)(2,1)} async-done(((bf16[384,768]{1,0:T(8,128)(2,1)}), bf16[1536,768]{1,0:T(8,128)(2,1)}) %all-gather.29.cloned.1.call-update) | async-done | bytes 2359312 | tf_op jit(solution)/shard_map/all_gather | solution.py:294
  483.1 13.3 convert_reduce_fusion
  507.2 27.3 %reduce-scatter.35.cloned.1.call-done = bf16[384,768]{1,0:T(8,128)(2,1)} async-done(((bf16[1536,768]{1,0:T(8,128)(2,1)}), bf16[384,768]{1,0:T(8,128)(2,1)}) %reduce-scatter.35.cloned.1.call-update) | async-done | bytes 589840 | tf_op jit(solution)/shard_map/reduce_scatter | solution.py:302
  534.5 35.6 %reduce-scatter.39.cloned.1.call-done = bf16[384,768]{1,0:T(8,128)(2,1)} async-done(((bf16[1536,768]{1,0:T(8,128)(2,1)}), bf16[384,768]{1,0:T(8,128)(2,1)}) %reduce-scatter.39.cloned.1.call-update) | async-done | bytes 589840 | tf_op jit(solution)/shard_map/reduce_scatter | solution.py:302
  608.9 101.6 %while.57 = (s32[]{:T(128)}, f32[1536,3,64]{0,2,1:T(8,128)}, f32[1536,3,64]{0,2,1:T(8,128)S(1)}, bf16[3,512,3,64]{1,3,2,0:T(8,128)(2,1)}, s32[3]{0:T(128)S(1)}, ...) while((s32[]{:T(128)}, f32[1536,3,64]{0,2,1:T(8,128)}, ...), condition=%wide.region_44.45_spmd.clone, body=%wide.region_42.44_spmd.clone.sunk | while | flops 1533639168 | bytes 145926704 | solution.py:162
  615.8 7.2 multiply_reduce_fusion.19
  623.0 9.6 multiply_convert_fusion.9
  649.7 7.2 multiply_reduce_fusion.19
  656.9 9.4 multiply_convert_fusion.9
  683.5 7.2 multiply_reduce_fusion.19
  690.7 9.4 multiply_convert_fusion.9
  718.3 98.7 %while.56 = (s32[]{:T(128)}, f32[1536,3,64]{0,2,1:T(8,128)S(1)}, f32[1536,3,64]{0,2,1:T(8,128)S(1)}, bf16[3,512,3,64]{1,3,2,0:T(8,128)(2,1)}, s32[3]{0:T(128)S(1...) while((s32[]{:T(128)}, f32[1536,3,64]{0,2,1:T(8,128)S(1)}, ...), condition=%wide.region_34.35_spmd.clone, body=%wide.region_32.34_spmd.clone.sunk | while | flops 1533639168 | bytes 136489456 | solution.py:162
  725.3 7.2 multiply_reduce_fusion.18
  732.5 9.5 multiply_convert_fusion.8
  758.2 7.2 multiply_reduce_fusion.18
  765.4 9.5 multiply_convert_fusion.8
  791.0 7.2 multiply_reduce_fusion.18
  798.2 9.5 multiply_convert_fusion.8
  819.8 11.1 all-reduce.7
  861.4 5.6 bitcast_convert_fusion
  893.5 37.3 %all-reduce.5 = (f32[768]{0:T(1024)S(1)}, f32[3072]{0:T(1024)S(1)}, f32[768]{0:T(1024)S(1)}) all-reduce(bf16[768]{0:T(1024)(128)(2,1)S(1)} %get-tuple-element.474, bf16[3072]{0:T(1024)(128)(2,1)S(1)} %get-tuple-element.475, bf16[768]{0:T(1024)(128)(2,1)S(1)} %copy-done.103), channel_id=17, replica_groups=mesh['dp'=8,'tensor'=4] {'dp'}, use_global_device_ids=true, to_apply=%region_59.60.clone | all-reduce | flops 4608 | bytes 27648
  934.1 24.0 %reduce-scatter.55.cloned.1.call-done = f32[96,2]{1,0:T(8,128)} async-done(((f32[768,2]{1,0:T(8,128)}), f32[96,2]{1,0:T(8,128)}) %reduce-scatter.55.cloned.1.call-update) | async-done | bytes 784
  959.6 62.7 %reduce-scatter.57.cloned.1.call-done = f32[96,2]{1,0:T(8,128)} async-done(((f32[768,2]{1,0:T(8,128)}), f32[96,2]{1,0:T(8,128)}) %reduce-scatter.57.cloned.1.call-update) | async-done | bytes 784
  1023.7 63.7 %reduce-scatter.51.cloned.1.call-done = f32[96,192]{1,0:T(8,128)} async-done(((f32[768,192]{1,0:T(8,128)}), f32[96,192]{1,0:T(8,128)}) %reduce-scatter.51.cloned.1.call-update) | async-done | bytes 73744
  1089.0 67.5 %reduce-scatter.49.cloned.1.call-done = f32[96,576]{1,0:T(8,128)} async-done(((f32[768,576]{1,0:T(8,128)}), f32[96,576]{1,0:T(8,128)}) %reduce-scatter.49.cloned.1.call-update) | async-done | bytes 221200
  1158.4 32.8 %reduce-scatter.41.cloned.1.call-done = bf16[384,768]{1,0:T(8,128)(2,1)} async-done(((bf16[1536,768]{1,0:T(8,128)(2,1)}), bf16[384,768]{1,0:T(8,128)(2,1)}) %reduce-scatter.41.cloned.1.call-update) | async-done | bytes 589840 | tf_op jit(solution)/shard_map/reduce_scatter | solution.py:340
  1192.5 34.3 %reduce-scatter.37.cloned.1.call-done = bf16[384,768]{1,0:T(8,128)(2,1)} async-done(((bf16[1536,768]{1,0:T(8,128)(2,1)}), bf16[384,768]{1,0:T(8,128)(2,1)}) %reduce-scatter.37.cloned.1.call-update) | async-done | bytes 589840 | tf_op jit(solution)/shard_map/reduce_scatter | solution.py:340
  1229.1 63.3 %reduce-scatter.47.cloned.1.call-done = f32[96,128]{1,0:T(8,128)} async-done(((f32[768,128]{1,0:T(8,128)}), f32[96,128]{1,0:T(8,128)}) %reduce-scatter.47.cloned.1.call-update) | async-done | bytes 49168 | tf_op jit(solution)/shard_map/reduce_scatter | solution.py:92
  1292.5 72.6 %reduce-scatter.45.cloned.1.call-done = f32[768,96]{0,1:T(8,128)} async-done(((f32[768,768]{0,1:T(8,128)}), f32[768,96]{0,1:T(8,128)}) %reduce-scatter.45.cloned.1.call-update) | async-done | bytes 294928 | tf_op jit(solution)/shard_map/reduce_scatter | solution.py:85
  1365.1 72.4 %reduce-scatter.43.cloned.1.call-done = f32[96,768]{1,0:T(8,128)} async-done(((f32[768,768]{1,0:T(8,128)}), f32[96,768]{1,0:T(8,128)}) %reduce-scatter.43.cloned.1.call-update) | async-done | bytes 294928 | tf_op jit(solution)/shard_map/reduce_scatter | solution.py:84
  (621 shorter events, 337.7 us)
Async XLA Ops:
  8.0 27.3 %copy-start.72 = (bf16[192,96]{1,0:T(8,128)(2,1)S(1)}, bf16[192,96]{1,0:T(8,128)(2,1)}, u32[]{:S(2)}) copy-start(bf16[192,96]{1,0:T(8,128)(2,1)} %param.24) | copy-start | bytes 110596
  8.0 27.4 %copy-start.62 = (bf16[3,96,192]{2,1,0:T(8,128)(2,1)S(1)}, bf16[3,96,192]{2,1,0:T(8,128)(2,1)}, u32[]{:S(2)}) copy-start(bf16[3,96,192]{2,1,0:T(8,128)(2,1)} %param.23) | copy-start | bytes 331780
  8.1 95.0 %all-gather.33.cloned.1.call-start = ((), (), s32[]{:S(2)}) async-start(), calls=%async_computation.36 | async-start | bytes 2949120 | tf_op jit(solution)/shard_map/all_gather | solution.py:235
  10.5 98.6 %all-gather.35.cloned.1.call-start = ((), (), s32[]{:S(2)}) async-start(), calls=%async_computation.37 | async-start | bytes 2949120 | tf_op jit(solution)/shard_map/all_gather | solution.py:235
  11.2 240.5 %reduce-scatter.27.cloned.1.call-start = ((), (), s32[]{:S(2)}) async-start(), calls=%async_computation.16 | async-start | bytes 2949120 | tf_op jit(solution)/shard_map/reduce_scatter | solution.py:249
  11.5 96.0 %copy-start.110 = (s32[2,1]{0,1:T(1,128)}, s32[2,1]{0,1:T(1,128)S(1)}, u32[]{:S(2)}) copy-start(s32[2,1]{0,1:T(1,128)S(1)} %reduce-window.9) | copy-start | bytes 28
  11.7 95.8 %copy-start.112 = (s32[2,1]{0,1:T(1,128)}, s32[2,1]{0,1:T(1,128)S(1)}, u32[]{:S(2)}) copy-start(s32[2,1]{0,1:T(1,128)S(1)} %reduce-window.6) | copy-start | bytes 28
  158.9 94.3 %reduce-scatter.31.cloned.1.call-start = ((), (), s32[]{:S(2)}) async-start(), calls=%async_computation.21 | async-start | bytes 2949120 | tf_op jit(solution)/shard_map/reduce_scatter | solution.py:249
  191.8 21.6 %copy-start.109 = (bf16[2,96]{1,0:T(2,128)(2,1)S(1)}, bf16[2,96]{1,0:T(2,128)(2,1)}, u32[]{:S(2)}) copy-start(bf16[2,96]{1,0:T(2,128)(2,1)} %param.32) | copy-start | bytes 1156
  191.8 37.7 %copy-start.104 = (u32[32]{0:T(128)S(1)}, u32[32]{0:T(128)}, u32[]{:S(2)}) copy-start(u32[32]{0:T(128)} %constant.200) | copy-start | bytes 388
  191.8 39.0 %copy-start.118 = (bf16[96]{0:T(256)(128)(2,1)S(1)}, bf16[96]{0:T(256)(128)(2,1)}, u32[]{:S(2)}) copy-start(bf16[96]{0:T(256)(128)(2,1)} %param.28) | copy-start | bytes 580
  191.8 39.2 %copy-start.119 = (bf16[96]{0:T(256)(128)(2,1)S(1)}, bf16[96]{0:T(256)(128)(2,1)}, u32[]{:S(2)}) copy-start(bf16[96]{0:T(256)(128)(2,1)} %param.30) | copy-start | bytes 580
  191.8 60.0 %copy-start.6 = (bf16[2,384,768]{2,1,0:T(8,128)(2,1)S(1)}, bf16[2,384,768]{2,1,0:T(8,128)(2,1)}, u32[]{:S(2)}) copy-start(bf16[2,384,768]{2,1,0:T(8,128)(2,1)} %param.22) | copy-start | bytes 3538948
  194.1 91.2 %all-gather.19.cloned.1.call-start = ((), (), s32[]{:S(2)}) async-start(), calls=%async_computation.18 | async-start | bytes 1327104 | tf_op jit(solution)/shard_map/all_gather | solution.py:43
  194.7 90.6 %all-gather.23.cloned.1.call-start = ((), (), s32[]{:S(2)}) async-start(), calls=%async_computation.22 | async-start | bytes 2949120 | tf_op jit(solution)/shard_map/all_gather | solution.py:257
  257.4 47.9 %all-gather.17.cloned.1.call-start = ((), (), s32[]{:S(2)}) async-start(), calls=%async_computation.17 | async-start | bytes 2949120 | tf_op jit(solution)/shard_map/all_gather | solution.py:257
  258.1 91.1 %all-gather.21.cloned.1.call-start = ((), (), s32[]{:S(2)}) async-start(), calls=%async_computation.19 | async-start | bytes 1327104 | tf_op jit(solution)/shard_map/all_gather | solution.py:44
  258.8 136.3 %reduce-scatter.29.cloned.1.call-start = ((), (), s32[]{:S(2)}) async-start(), calls=%async_computation.20 | async-start | bytes 2949120 | tf_op jit(solution)/shard_map/reduce_scatter | solution.py:260
  285.3 20.0 %copy-start.101 = (f32[768]{0:T(1024)}, f32[768]{0:T(1024)S(1)}, u32[]{:S(2)}) copy-start(f32[768]{0:T(1024)S(1)} %dynamic-slice_convert_fusion) | copy-start | bytes 9220
  354.6 67.3 %reduce-scatter.33.cloned.1.call-start = ((), (), s32[]{:S(2)}) async-start(), calls=%async_computation.23 | async-start | bytes 2949120 | tf_op jit(solution)/shard_map/reduce_scatter | solution.py:260
  360.1 97.5 %all-gather.25.cloned.1.call-start = ((), (), s32[]{:S(2)}) async-start(), calls=%async_computation.24 | async-start | bytes 2949120 | tf_op jit(solution)/shard_map/all_gather | solution.py:294
  433.3 49.8 %all-gather.29.cloned.1.call-start = ((), (), s32[]{:S(2)}) async-start(), calls=%async_computation.28 | async-start | bytes 2949120 | tf_op jit(solution)/shard_map/all_gather | solution.py:294
  433.4 30.4 %copy-start.76 = (f32[384]{0:T(512)}, f32[384]{0:T(512)S(1)}, u32[]{:S(2)}) copy-start(f32[384]{0:T(512)S(1)} %negate_multiply_fusion.3) | copy-start | bytes 4612
  435.7 47.4 %copy-start.102 = (f32[768]{0:T(1024)S(1)}, f32[768]{0:T(1024)}, u32[]{:S(2)}) copy-start(f32[768]{0:T(1024)} %copy-done.101) | copy-start | bytes 9220
  435.7 98.8 %reduce-scatter.35.cloned.1.call-start = ((), (), s32[]{:S(2)}) async-start(), calls=%async_computation.25 | async-start | bytes 2949120 | tf_op jit(solution)/shard_map/reduce_scatter | solution.py:302
  483.1 14.8 %copy-start.117 = (bf16[768,768]{1,0:T(8,128)(2,1)S(1)}, bf16[768,768]{1,0:T(8,128)(2,1)}, u32[]{:S(2)}) copy-start(bf16[768,768]{1,0:T(8,128)(2,1)} %all-gather.19.cloned.1.call-done) | copy-start | bytes 3538948
  501.4 68.7 %reduce-scatter.39.cloned.1.call-start = ((), (), s32[]{:S(2)}) async-start(), calls=%async_computation.29 | async-start | bytes 2949120 | tf_op jit(solution)/shard_map/reduce_scatter | solution.py:302
  507.1 97.4 %all-gather.31.cloned.1.call-start = ((), (), s32[]{:S(2)}) async-start(), calls=%async_computation.30 | async-start | bytes 2949120 | tf_op jit(solution)/shard_map/all_gather | solution.py:313
  534.5 39.9 %copy-start.38 = (bf16[384,768]{1,0:T(8,128)(2,1)S(1)}, bf16[384,768]{1,0:T(8,128)(2,1)}, u32[]{:S(2)}) copy-start(bf16[384,768]{1,0:T(8,128)(2,1)} %reduce-scatter.35.cloned.1.call-done) | copy-start | bytes 1769476
  580.1 133.8 %all-gather.27.cloned.1.call-start = ((), (), s32[]{:S(2)}) async-start(), calls=%async_computation.26 | async-start | bytes 2949120 | tf_op jit(solution)/shard_map/all_gather | solution.py:313
  581.8 290.4 %all-reduce.10.cloned.1.call-start = ((), (), s32[]{:S(2)}) async-start(), calls=%async_computation.34 | async-start | bytes 393216 | tf_op jit(solution)/shard_map/psum | solution.py:79
  585.0 10.7 copy-start.90
  585.6 10.2 copy-start.91
  589.0 19.8 %copy-start.14 = (bf16[1536,3,64]{0,2,1:T(8,128)(2,1)S(1)}, bf16[1536,3,64]{0,2,1:T(8,128)(2,1)}, u32[]{:S(2)}) copy-start(bf16[1536,3,64]{0,2,1:T(8,128)(2,1)} %copy-done.13) | copy-start | bytes 1769476
  589.1 343.6 %reduce-scatter.53.cloned.1.call-start = ((), (), s32[]{:S(2)}) async-start(), calls=%async_computation.40 | async-start | bytes 442368
  831.9 126.2 %reduce-scatter.55.cloned.1.call-start = ((), (), s32[]{:S(2)}) async-start(), calls=%async_computation.41 | async-start | bytes 442368
  832.9 189.4 %reduce-scatter.57.cloned.1.call-start = ((), (), s32[]{:S(2)}) async-start(), calls=%async_computation.42 | async-start | bytes 442368
  833.9 253.5 %reduce-scatter.51.cloned.1.call-start = ((), (), s32[]{:S(2)}) async-start(), calls=%async_computation.39 | async-start | bytes 884736
  840.4 316.1 %reduce-scatter.49.cloned.1.call-start = ((), (), s32[]{:S(2)}) async-start(), calls=%async_computation.38 | async-start | bytes 2211840
  861.4 329.8 %reduce-scatter.41.cloned.1.call-start = ((), (), s32[]{:S(2)}) async-start(), calls=%async_computation.31 | async-start | bytes 2949120 | tf_op jit(solution)/shard_map/reduce_scatter | solution.py:340
  867.1 359.7 %reduce-scatter.37.cloned.1.call-start = ((), (), s32[]{:S(2)}) async-start(), calls=%async_computation.27 | async-start | bytes 2949120 | tf_op jit(solution)/shard_map/reduce_scatter | solution.py:340
  872.1 420.3 %reduce-scatter.47.cloned.1.call-start = ((), (), s32[]{:S(2)}) async-start(), calls=%async_computation.35 | async-start | bytes 442368 | tf_op jit(solution)/shard_map/reduce_scatter | solution.py:92
  874.1 491.0 %reduce-scatter.45.cloned.1.call-start = ((), (), s32[]{:S(2)}) async-start(), calls=%async_computation.33 | async-start | bytes 2654208 | tf_op jit(solution)/shard_map/reduce_scatter | solution.py:85
  882.0 555.4 %reduce-scatter.43.cloned.1.call-start = ((), (), s32[]{:S(2)}) async-start(), calls=%async_computation.32 | async-start | bytes 2654208 | tf_op jit(solution)/shard_map/reduce_scatter | solution.py:84
  891.2 300.0 %copy-start.25 = (f32[384,768]{1,0:T(8,128)S(1)}, f32[384,768]{1,0:T(8,128)}, u32[]{:S(2)}) copy-start(f32[384,768]{1,0:T(8,128)} %copy-done.24) | copy-start | bytes 3538948
  891.2 300.0 %copy-start.84 = (f32[384]{0:T(512)S(1)}, f32[384]{0:T(512)}, u32[]{:S(2)}) copy-start(f32[384]{0:T(512)} %copy-done.83) | copy-start | bytes 4612
  892.7 334.1 %copy-start.23 = (f32[384,768]{1,0:T(8,128)S(1)}, f32[384,768]{1,0:T(8,128)}, u32[]{:S(2)}) copy-start(f32[384,768]{1,0:T(8,128)} %get-tuple-element.488) | copy-start | bytes 3538948
  892.7 334.1 %copy-start.86 = (f32[384]{0:T(512)S(1)}, f32[384]{0:T(512)}, u32[]{:S(2)}) copy-start(f32[384]{0:T(512)} %copy-done.85) | copy-start | bytes 4612
  (124 other events, 428.7 us)
Sparse Core Ops, SparseCore 0:
  11.0 26.7 all-gather.32
  39.4 24.0 all-gather.34
  159.1 32.8 reduce-scatter.26
  194.5 33.0 reduce-scatter.30
  433.4 24.0 all-gather.24
  459.0 24.0 all-gather.28
  580.2 24.2 all-gather.30
  606.1 24.2 all-gather.26
Sparse Core Ops, SparseCore 1:
  196.8 41.1 all-gather.18
  257.5 21.8 all-gather.22
  281.4 23.9 all-gather.16
  307.6 41.5 all-gather.20
  354.6 31.5 reduce-scatter.28
  388.9 33.0 reduce-scatter.32
  501.4 33.0 reduce-scatter.34
  537.0 33.0 reduce-scatter.38
  589.2 46.2 all-reduce.9
  832.0 62.0 reduce-scatter.52
  897.5 60.5 reduce-scatter.54
  961.8 60.5 reduce-scatter.56
  1025.8 61.5 reduce-scatter.50
  1090.9 65.5 reduce-scatter.48
  1159.2 31.9 reduce-scatter.40
  1193.7 32.9 reduce-scatter.36
  1230.9 61.5 reduce-scatter.46
  1297.0 68.0 reduce-scatter.44
  1369.4 68.0 reduce-scatter.42
where the time goes:
time: 1460 us; the launch traced here: 1450 us
  waiting for transfers between devices  663 us (45%)
  matrix products  279 us (19%)
  blocking collectives  249 us (17%)
  other arithmetic  129 us (9%)
  local copies, waits for them, and re-layouts  83 us (6%)
  loops' own time  20.2 us (1%)
  between operations  20 us (1%)
    unnamed x32, waiting for transfers between devices  221 us
    reduce_scatter x1, waiting for transfers between devices, reduce_grads(): lax.psum_scatter(totals[3], 'dp', scatter_dimension=1, tiled=True)  72.6 us
    reduce_scatter x1, waiting for transfers between devices, reduce_grads(): lax.psum_scatter(totals[2], 'dp', scatter_dimension=0, tiled=True)  72.4 us
    reduce_scatter x2, waiting for transfers between devices, per_device(): lax.psum_scatter(jnp.einsum('spc,sdc->pd', d_project, qkv_back, preferred...  67.1 us
    reduce_scatter x1, waiting for transfers between devices, reduce_grads(): lax.psum_scatter(shared[6], 'dp', scatter_dimension=0, tiled=True)  63.3 us
    reduce_scatter x2, waiting for transfers between devices, per_device(): lax.psum_scatter(jnp.einsum('pf,df->pd', d_hidden, up_back, preferred_ele...  62.9 us
    convert_element_type x6, other arithmetic, one_block(): d_scores = (attn_probs * (d_probs - inner_sum)).astype(jnp.bfloat16)  56.8 us
    unnamed x2, blocking collectives  56.4 us
  transfers between devices with their start and end apart: 27, of which 17 were waited for; matrix products, arithmetic and copies ran while one was open for 27% of the time, Pallas kernels for 0%

commit v1 on v0

v1 whole, which is shorter than its diff:
```python
import functools

import jax
import jax.experimental.pallas as pl
import jax.experimental.pallas.tpu as pltpu
import jax.numpy as jnp
from jax import lax
from jax.sharding import PartitionSpec as P

HD = 64
EPSILON = 1e-06
MASKED = -1e30
MASK_ROWS = 16
SQRT_HALF = 0.7071067811865476
INV_SQRT_2PI = 0.3989422804014327
VMEM_BYTES = 60 * 2**20
bf16 = jnp.bfloat16
f32 = jnp.float32
VMEM = pl.BlockSpec(memory_space=pltpu.VMEM)
SMEM = pl.BlockSpec(memory_space=pltpu.SMEM)
ANY = pl.BlockSpec(memory_space=pl.ANY)
FAR, MATE = 2, 1
RELATIVE = (0, FAR, MATE, FAR | MATE)


def mm(left, right, left_dim=1, right_dim=0):
    return lax.dot_general(
        left, right, (((left_dim,), (right_dim,)), ((), ())), preferred_element_type=f32
    )


def kernel_call(body, operands, specs, outs, out_specs, scratch=()):
    return pl.pallas_call(
        body,
        out_shape=outs,
        in_specs=specs,
        out_specs=out_specs,
        scratch_shapes=list(scratch),
        compiler_params=pltpu.CompilerParams(vmem_limit_bytes=VMEM_BYTES),
    )(*operands)


def project_body(count, offs, bias, *refs):
    blocks, rows = refs[:count], refs[count : count + 4]
    qkv, wq, wo, full = refs[count + 4 :]
    height = blocks[0].shape[0]
    for i in range(count):
        full[pl.ds(pl.multiple_of(offs[i], 16), height), :] = blocks[i][...]
    turned = full[...].T
    width = qkv.shape[0]
    wq[...] = turned[:width]
    wo[...] = turned[width:]
    share = rows[0].shape[0]
    ones = jnp.ones((8, share), bf16)
    shift = mm(bias[...], ones, 0, 0)
    for i in range(4):
        got = mm(wq[...], rows[i][...], 1, 1) + shift
        qkv[:, i * share : (i + 1) * share] = got.astype(bf16)


def project(offs, bias, blocks, rows):
    width = bias.shape[1]
    model = rows[0].shape[1]
    outs = (
        jax.ShapeDtypeStruct((width, 4 * rows[0].shape[0]), bf16),
        jax.ShapeDtypeStruct((width, model), bf16),
        jax.ShapeDtypeStruct((model - width, model), bf16),
    )
    operands = (offs, bias, *blocks, *rows)
    return kernel_call(
        functools.partial(project_body, len(blocks)),
        operands,
        [SMEM] + [VMEM] * (len(operands) - 1),
        outs,
        (VMEM,) * 3,
        [pltpu.VMEM((model, model), bf16)],
    )


def attend_body(heads, q_block, qkv, qmask, kmask, near, far, lse, ks, qs):
    rows = qkv.shape[1]
    group = heads * HD
    half = rows // 2
    scale = HD**-0.5

    def head(h, carry):
        top = pl.multiple_of(h * HD, HD)
        ks[...] = jnp.concatenate([qkv[pl.ds(group + top, HD), :], kmask[...]], 0).T
        qs[...] = jnp.concatenate([qkv[pl.ds(top, HD), :] * scale, qmask[...]], 0)
        values = qkv[pl.ds(2 * group + top, HD), :]
        for b in range(rows // q_block):
            at = slice(b * q_block, (b + 1) * q_block)
            scores = mm(ks[...], qs[:, at])
            most = jnp.max(scores, axis=0, keepdims=True)
            weights = jnp.exp(scores - most)
            total = jnp.sum(weights, axis=0, keepdims=True)
            blended = (mm(values, weights.astype(bf16)) / total).astype(bf16)
            cut = min(max(half - b * q_block, 0), q_block)
            if cut:
                near[pl.ds(top, HD), b * q_block : b * q_block + cut] = blended[:, :cut]
            if cut < q_block:
                start = b * q_block + cut - half
                far[pl.ds(top, HD), start : start + q_block - cut] = blended[:, cut:]
            lse[pl.ds(h, 1), at] = most + jnp.log(total)
        return carry

    lax.fori_loop(0, heads, head, 0)


def attend(qkv, qmask, kmask):
    group, rows = qkv.shape[0] // 3, qkv.shape[1]
    half = jax.ShapeDtypeStruct((group, rows // 2), bf16)
    depth = HD + MASK_ROWS
    return kernel_call(
        functools.partial(attend_body, group // HD, rows // 3),
        (qkv, qmask, kmask),
        [VMEM] * 3,
        (half, half, jax.ShapeDtypeStruct((8, rows), f32)),
        (VMEM,) * 3,
        [pltpu.VMEM((rows, depth), bf16), pltpu.VMEM((depth, rows), bf16)],
    )


def attend_back_heads(heads, q_block, k_block, refs, scratch):
    qkv, near, far, d_near, d_far, lse, qmask, kmask, d_qkv = refs
    ks, qs, vs, qn, dt, dn, dks, dvs = scratch
    rows = qkv.shape[1]
    group = heads * HD
    scale = HD**-0.5

    def head(h, carry):
        top = pl.multiple_of(h * HD, HD)
        keys = qkv[pl.ds(group + top, HD), :]
        ks[...] = jnp.concatenate([keys, kmask[...]], 0).T
        queries = qkv[pl.ds(top, HD), :]
        qs[...] = jnp.concatenate([queries * scale, qmask[...]], 0)
        qn[...] = queries.T
        vs[...] = qkv[pl.ds(2 * group + top, HD), :].T
        outer = jnp.concatenate([d_near[pl.ds(top, HD), :], d_far[pl.ds(top, HD), :]], 1)
        blended = jnp.concatenate([near[pl.ds(top, HD), :], far[pl.ds(top, HD), :]], 1)
        dt[...] = outer
        dn[...] = outer.T
        inner = jnp.sum(outer.astype(f32) * blended.astype(f32), axis=0, keepdims=True)
        log_sum = lse[pl.ds(h, 1), :]
        for b in range(rows // q_block):
            at = slice(b * q_block, (b + 1) * q_block)
            d_queries = None
            for k in range(rows // k_block):
                ka = slice(k * k_block, (k + 1) * k_block)
                probs = jnp.exp(mm(ks[ka, :], qs[:, at]) - log_sum[:, at])
                d_probs = mm(vs[ka, :], dt[:, at])
                d_scores = (probs * (d_probs - inner[:, at])).astype(bf16)
                d_values = mm(probs.astype(bf16), dn[at, :])
                d_keys = mm(d_scores, qn[at, :])
                if b == 0:
                    dvs[ka, :] = d_values
                    dks[ka, :] = d_keys
                else:
                    dvs[ka, :] += d_values
                    dks[ka, :] += d_keys
                part = mm(keys[:, ka], d_scores)
                d_queries = part if d_queries is None else d_queries + part
            d_qkv[pl.ds(top, HD), at] = (d_queries * scale).astype(bf16)
        d_qkv[pl.ds(group + top, HD), :] = (dks[...] * scale).astype(bf16).T
        d_qkv[pl.ds(2 * group + top, HD), :] = dvs[...].astype(bf16).T
        return carry

    lax.fori_loop(0, heads, head, 0)


def attend_back_body(last, slots, offs, *refs):
    qkv, near, far, d_near, d_far, lse, qmask, kmask = refs[:8]
    rows_of = refs[8:12]
    refs = refs[12:]
    if last:
        wq, wq_far, d_qkv_far, d_resid = refs[:4]
        refs = refs[4:]
        d_weight, d_bias, d_own, d_mate = refs[:4]
        d_qkv, full = refs[4:6]
        scratch = refs[6:]
    else:
        d_weight, d_bias, d_qkv, full = refs[:4]
        scratch = refs[4:]
    rows = qkv.shape[1]
    heads = qkv.shape[0] // 3 // HD
    attend_back_heads(
        heads,
        rows // 2,
        rows // 3,
        (qkv, near, far, d_near, d_far, lse, qmask, kmask, d_qkv),
        scratch,
    )
    share = rows // 4
    total = None
    for i in range(4):
        part = mm(rows_of[i][...], d_qkv[:, i * share : (i + 1) * share], 0, 1)
        total = part if total is None else total + part
    full[...] = total.astype(bf16)
    n_y, n_z, height, _ = d_weight.shape
    for y in range(n_y):
        for z in range(n_z):
            start = pl.multiple_of(offs[y * n_z + z], 16)
            d_weight[y, z] = full[pl.ds(start, height), :]
    d_bias[...] = mm(jnp.ones((8, rows), bf16), d_qkv[...], 1, 1)
    if last:
        for i in range(4):
            at = slice(i * share, (i + 1) * share)
            part = mm(d_qkv[:, at], wq[...], 0, 0) + mm(d_qkv_far[:, at], wq_far[...], 0, 0)
            if i < 2:
                d_own[at, :] = part + d_resid[at, :]
            else:
                back = slice((i - 2) * share, (i - 1) * share)
                d_mate[back, :] = part.astype(bf16)


def attend_back(offs, slots, saved, tail=()):
    qkv = saved[0]
    width, rows = qkv.shape
    model = saved[8].shape[1]
    n_y, n_z = slots
    outs = [
        jax.ShapeDtypeStruct((n_y, n_z, model // (n_y * n_z), width), bf16),
        jax.ShapeDtypeStruct((8, width), f32),
    ]
    scratch = []
    if tail:
        outs += [
            jax.ShapeDtypeStruct((rows // 2, model), f32),
            jax.ShapeDtypeStruct((rows // 2, model), bf16),
        ]
        scratch.append(pltpu.VMEM((width, rows), bf16))
    else:
        outs.append(jax.ShapeDtypeStruct((width, rows), bf16))
    depth = HD + MASK_ROWS
    scratch += [
        pltpu.VMEM((model, width), bf16),
        pltpu.VMEM((rows, depth), bf16),
        pltpu.VMEM((depth, rows), bf16),
        pltpu.VMEM((rows, HD), bf16),
        pltpu.VMEM((rows, HD), bf16),
        pltpu.VMEM((HD, rows), bf16),
        pltpu.VMEM((rows, HD), bf16),
        pltpu.VMEM((rows, HD), f32),
        pltpu.VMEM((rows, HD), f32),
    ]
    operands = (offs, *saved, *tail)
    return kernel_call(
        functools.partial(attend_back_body, bool(tail), slots),
        operands,
        [SMEM] + [VMEM] * (len(operands) - 1),
        tuple(outs),
        (VMEM,) * len(outs),
        scratch,
    )


def middle_body(slots, offs, *refs):
    n_y, n_z = slots
    n_blocks = 4 * n_y
    toks, refs = refs[:2], refs[2:]
    atts, refs = refs[:4], refs[4:]
    outs_w, refs = refs[:4], refs[4:]
    (proj, vectors, up_bias, valid, cots_a, cots_b), refs = refs[:6], refs[6:]
    ups, refs = refs[:n_blocks], refs[n_blocks:]
    downs, refs = refs[:n_blocks], refs[n_blocks:]
    (
        emb_a,
        emb_b,
        d_resid,
        d_atts_0,
        d_atts_1,
        d_atts_2,
        d_atts_3,
        g_up_keep,
        g_up_mate,
        g_down_keep,
        g_down_mate,
        g_out_keep,
        g_out_mate,
        g_proj,
        g_vec,
        g_up_bias,
    ) = refs[:16]
    d_atts = (d_atts_0, d_atts_1, d_atts_2, d_atts_3)
    (
        up_s,
        down_s,
        att_s,
        out_s,
        low_s,
        branch_s,
        d_hid_s,
        xhat_s,
        rstd_s,
        acc_s,
        act_s,
        slope_s,
        up_stage,
        down_stage,
        in_sem,
        out_sem,
    ) = refs[16:]
    model = proj.shape[0]
    ffn = up_s.shape[2]
    rows = acc_s.shape[0]
    share = toks[0].shape[0]
    group = atts[0].shape[0]
    height = model // (n_y * n_z)
    row_step = share
    chunks = [(i, slice(i * row_step, (i + 1) * row_step)) for i in range(rows // row_step)]

    pending = {}
    index = 0
    for t in range(4):
        for which, (blocks, dest) in enumerate(((ups, up_s), (downs, down_s))):
            for y in range(n_y):
                for z in range(n_z):
                    start = pl.multiple_of(offs[y * n_z + z], 16)
                    copy = pltpu.make_async_copy(
                        blocks[t * n_y + y].at[z],
                        dest.at[t, pl.ds(start, height), :],
                        in_sem.at[index],
                    )
                    copy.start()
                    pending.setdefault((t, which), []).append(copy)
                    index += 1

    for i in range(4):
        att_s[i * group : (i + 1) * group, :] = atts[i][...]
        out_s[i * group : (i + 1) * group, :] = outs_w[i][...]

    gain_1, gain_2 = vectors[8:9, :], vectors[9:10, :]
    shift_1, shift_2 = vectors[10:11, :], vectors[11:12, :]
    out_bias, down_bias = vectors[2:3, :], vectors[7:8, :]

    def normed(value):
        center = value - jnp.mean(value, axis=1, keepdims=True)
        rstd = lax.rsqrt(jnp.mean(center * center, axis=1, keepdims=True) + EPSILON)
        return center * rstd, rstd

    def normed_back(grad, xhat, rstd, gain):
        scaled = grad * gain
        mean = jnp.mean(scaled, axis=1, keepdims=True)
        along = jnp.mean(scaled * xhat, axis=1, keepdims=True)
        return rstd * (scaled - mean - xhat * along)

    def add_up(row, value, first):
        part = jnp.sum(value, axis=0, keepdims=True)
        if first:
            g_vec[row : row + 1, :] = part
        else:
            g_vec[row : row + 1, :] += part

    for i, at in chunks:
        resid = (
            mm(att_s[:, at], out_s[...], 0, 0)
            + toks[i * row_step // share][...].astype(f32)
            + out_bias
        )
        xhat, rstd = normed(resid)
        value = xhat * gain_1 + shift_1
        xhat_s[at, :] = xhat
        rstd_s[at, :] = rstd
        low_s[at, :] = value.astype(bf16)
        acc_s[at, :] = value + down_bias

    for t in range(4):
        for copy in pending[(t, 0)]:
            copy.wait()
        for copy in pending[(t, 1)]:
            copy.wait()
        cols = slice(t * ffn, (t + 1) * ffn)
        for i, at in chunks:
            hidden = mm(low_s[at, :], up_s[t]) + up_bias[t : t + 1, :]
            phi = 0.5 + 0.5 * lax.erf(hidden * SQRT_HALF)
            density = jnp.exp(-0.5 * hidden * hidden) * INV_SQRT_2PI
            active = (hidden * phi).astype(bf16)
            act_s[at, cols] = active
            slope_s[at, cols] = (phi + hidden * density).astype(slope_s.dtype)
            acc_s[at, :] += mm(active, down_s[t], 1, 1)

    for i, at in chunks:
        xhat, rstd = normed(acc_s[at, :])
        low = (xhat * gain_2 + shift_2).astype(bf16)
        embed = mm(low, proj[...])
        unit = lax.rsqrt(jnp.sum(embed * embed, axis=1, keepdims=True) + EPSILON)
        kept = valid[at, :].astype(f32)
        emb = (emb_a, emb_b)[i * row_step // share]
        emb[...] = (kept * embed * unit).astype(bf16)
        cot = (cots_a, cots_b)[i * row_step // share][...].astype(f32)
        along = jnp.sum(cot * embed, axis=1, keepdims=True)
        d_embed = (kept * (unit * cot - unit * unit * unit * embed * along)).astype(bf16)
        part = mm(low, d_embed, 0, 0)
        if i == 0:
            g_proj[...] = part
        else:
            g_proj[...] += part
        d_normed = mm(d_embed, proj[...], 1, 1)
        add_up(1, d_normed * xhat, i == 0)
        add_up(3, d_normed, i == 0)
        d_value = normed_back(d_normed, xhat, rstd, gain_2)
        add_up(5, d_value, i == 0)
        branch_s[at, :] = d_value.astype(bf16)
        acc_s[at, :] = d_value

    sent = {}
    index = 0

    def send(stage, slot, dest, place):
        nonlocal index
        for y in range(n_y):
            for z in range(n_z):
                start = pl.multiple_of(offs[y * n_z + z], 16)
                where = dest.at[y, z] if place is None else dest.at[place, y, z]
                copy = pltpu.make_async_copy(
                    stage.at[slot, pl.ds(start, height), :] if slot is not None else stage.at[pl.ds(start, height), :],
                    where,
                    out_sem.at[index],
                )
                copy.start()
                sent.setdefault((id(stage), slot), []).append(copy)
                index += 1

    def settle(stage, slot):
        for copy in sent.pop((id(stage), slot), []):
            copy.wait()

    for turn, t in enumerate((2, 3, 0, 1)):
        slot = turn % 2
        cols = slice(t * ffn, (t + 1) * ffn)
        for i, at in chunks:
            d_active = mm(branch_s[at, :], down_s[t])
            d_hidden = (d_active * slope_s[at, cols].astype(f32)).astype(bf16)
            d_hid_s[at, :] = d_hidden
            part = jnp.sum(d_hidden.astype(f32), axis=0, keepdims=True)
            if i == 0:
                g_up_bias[t : t + 1, :] = part
            else:
                g_up_bias[t : t + 1, :] += part
            acc_s[at, :] += mm(d_hidden, up_s[t], 1, 1)
        settle(up_stage, slot)
        up_stage[slot] = mm(low_s[...], d_hid_s[...], 0, 0).astype(bf16)
        send(up_stage, slot, g_up_keep if t < 2 else g_up_mate, t % 2)
        settle(down_stage, slot)
        down_stage[slot] = mm(branch_s[...], act_s[:, cols], 0, 0).astype(bf16)
        send(down_stage, slot, g_down_keep if t < 2 else g_down_mate, t % 2)

    for i, at in chunks:
        grad = acc_s[at, :]
        xhat = xhat_s[at, :]
        add_up(0, grad * xhat, i == 0)
        add_up(2, grad, i == 0)
        d_value = normed_back(grad, xhat, rstd_s[at, :], gain_1)
        add_up(4, d_value, i == 0)
        d_resid[at, :] = d_value
        branch_s[at, :] = d_value.astype(bf16)
    for i in range(4):
        rows_of = slice(i * group, (i + 1) * group)
        d_atts[i][...] = mm(out_s[rows_of, :], branch_s[...], 1, 1).astype(bf16)
    for part, dest in ((1, g_out_mate), (0, g_out_keep)):
        slot = part
        settle(up_stage, slot)
        grad = mm(branch_s[...], att_s[part * 2 * group : (part + 1) * 2 * group, :], 0, 1).astype(bf16)
        up_stage[slot, :, : 2 * group] = grad
        for y in range(n_y):
            for z in range(n_z):
                start = pl.multiple_of(offs[y * n_z + z], 16)
                dest[y, z] = up_stage[slot, pl.ds(start, height), : 2 * group]
    for slot in range(2):
        settle(up_stage, slot)
        settle(down_stage, slot)


def middle(offs, slots, toks, atts, outs_w, proj, vectors, up_bias, valid, cots, ups, downs):
    n_y, n_z = slots
    share, model = toks[0].shape
    rows = 2 * share
    group = atts[0].shape[0]
    ffn = ups[0].shape[2]
    emb = proj.shape[1]
    height = model // (n_y * n_z)
    weight = jax.ShapeDtypeStruct((2, n_y, n_z, height, ffn), bf16)
    out_grad = jax.ShapeDtypeStruct((n_y, n_z, height, 2 * group), bf16)
    outs = (
        jax.ShapeDtypeStruct((share, emb), bf16),
        jax.ShapeDtypeStruct((share, emb), bf16),
        jax.ShapeDtypeStruct((rows, model), f32),
        *[jax.ShapeDtypeStruct((group, rows), bf16)] * 4,
        *[weight] * 4,
        *[out_grad] * 2,
        jax.ShapeDtypeStruct((model, emb), f32),
        jax.ShapeDtypeStruct((8, model), f32),
        jax.ShapeDtypeStruct((4, ffn), f32),
    )
    out_specs = (*[VMEM] * 7, *[ANY] * 4, *[VMEM] * 5)
    operands = (offs, *toks, *atts, *outs_w, proj, vectors, up_bias, valid, *cots, *ups, *downs)
    n_blocks = 4 * n_y
    specs = [SMEM] + [VMEM] * (len(operands) - 1 - 2 * n_blocks) + [ANY] * (2 * n_blocks)
    scratch = [
        pltpu.VMEM((4, model, ffn), bf16),
        pltpu.VMEM((4, model, ffn), bf16),
        pltpu.VMEM((4 * group, rows), bf16),
        pltpu.VMEM((4 * group, model), bf16),
        pltpu.VMEM((rows, model), bf16),
        pltpu.VMEM((rows, model), bf16),
        pltpu.VMEM((rows, ffn), bf16),
        pltpu.VMEM((rows, model), f32),
        pltpu.VMEM((rows, 1), f32),
        pltpu.VMEM((rows, model), f32),
        pltpu.VMEM((rows, 4 * ffn), bf16),
        pltpu.VMEM((rows, 4 * ffn), bf16),
        pltpu.VMEM((2, model, ffn), bf16),
        pltpu.VMEM((2, model, ffn), bf16),
        pltpu.SemaphoreType.DMA((8 * n_y * n_z,)),
        pltpu.SemaphoreType.DMA((8 * n_y * n_z,)),
    ]
    return kernel_call(
        functools.partial(middle_body, slots), operands, specs, outs, out_specs, scratch
    )


def swap(value, bit):
    count = lax.axis_size("tensor")
    return lax.ppermute(value, "tensor", [(i, i ^ bit) for i in range(count)])


def swap_y(value):
    count = lax.axis_size("dp")
    return lax.ppermute(value, "dp", [(i, i ^ 1) for i in range(count)])


def pull_z(value, step):
    n_z = lax.axis_size("dp") // 2
    pairs = [(2 * ((z + step) % n_z) + y, 2 * z + y) for z in range(n_z) for y in range(2)]
    return lax.ppermute(value, "dp", pairs)


def push_z(value, step):
    n_z = lax.axis_size("dp") // 2
    pairs = [(2 * z + y, 2 * ((z + step) % n_z) + y) for z in range(n_z) for y in range(2)]
    return lax.ppermute(value, "dp", pairs)


def after(value, *others):
    return lax.optimization_barrier((value, *others))[0]


def scatter_sum(keep, got, slots, far_first=False):
    n_y, n_z = slots

    def both(*at):
        return keep[at].astype(f32) + got[at].astype(f32)

    if n_y == 1:
        rest = both(0) + swap(both(1).astype(bf16), FAR).astype(f32)
        return lax.psum_scatter(rest[0, 0].astype(bf16), "dp", scatter_dimension=0, tiled=True).astype(f32)
    if far_first:
        first = swap(both(1).astype(bf16), FAR)
        second = swap_y((both(0, 1) + first[1].astype(f32)).astype(bf16))
        rest = both(0, 0) + first[0].astype(f32) + second.astype(f32)
    else:
        first = swap_y((keep[:, 1].astype(f32) + got[:, 1].astype(f32)).astype(bf16))
        second = swap((both(1, 0) + first[1].astype(f32)).astype(bf16), FAR)
        rest = both(0, 0) + first[0].astype(f32) + second.astype(f32)
    total = rest[0]
    low = rest.astype(bf16)
    for step in range(1, n_z):
        total = total + push_z(low[step], step).astype(f32)
    return total


def relative_blocks(value, n_z):
    index = lax.axis_index("dp")
    z, y = index // 2, index % 2
    value = value.reshape((n_z, 2) + value.shape[1:])
    value = lax.dynamic_slice_in_dim(jnp.concatenate([value, value]), z, n_z, 0)
    mine = jnp.where(y == 0, value[:, 0], value[:, 1])
    other = jnp.where(y == 0, value[:, 1], value[:, 0])
    return jnp.stack([mine, other])


def share_small(value, slots):
    n_y, n_z = slots
    if n_y == 1:
        total = lax.psum(value.astype(bf16), "tensor")
        return lax.psum_scatter(total, "dp", scatter_dimension=0, tiled=True)[0].astype(f32)
    value = relative_blocks(value, n_z)
    low = value.astype(bf16)
    value = value + swap(low, MATE).astype(f32)
    value = value[0] + swap_y(value[1].astype(bf16)).astype(f32)
    value = value + swap(value.astype(bf16), FAR).astype(f32)
    total = value[0]
    low = value.astype(bf16)
    for step in range(1, n_z):
        total = total + push_z(low[step], step).astype(f32)
    return total


def gather_small(piece, slots):
    n_y, n_z = slots
    if n_y == 1:
        return lax.all_gather(piece, "dp", axis=0)
    mine = jnp.stack([piece] + [pull_z(piece, step) for step in range(1, n_z)])
    other = swap_y(mine)
    index = lax.axis_index("dp")
    z, y = index // 2, index % 2
    both = jnp.stack([jnp.where(y == 0, mine, other), jnp.where(y == 0, other, mine)], 1)
    both = lax.dynamic_slice_in_dim(jnp.concatenate([both, both]), (n_z - z) % n_z, n_z, 0)
    return both.reshape((2 * n_z,) + piece.shape)


def per_device(
    tokens,
    qkv_weight,
    out_weight,
    up_weight,
    down_weight,
    qkv_bias,
    out_bias,
    up_bias,
    down_bias,
    norm_gain,
    norm_shift,
    proj_weight,
    lengths,
    cotangent,
):
    n_dp = lax.axis_size("dp")
    d = lax.axis_index("dp")
    t = lax.axis_index("tensor")
    half = t // 2
    share, model = tokens.shape[1], tokens.shape[2]
    rows = 4 * share
    group = qkv_weight.shape[2]
    height = qkv_weight.shape[1]
    ffn = up_weight.shape[1]
    emb = proj_weight.shape[1]
    ring = n_dp == 8
    slots = (2, n_dp // 2) if ring else (1, 1)
    n_y, n_z = slots
    if ring:
        z, y = d // 2, d % 2
        offs = jnp.stack(
            [height * (2 * ((z + r) % n_z) + (y ^ yy)) for yy in range(2) for r in range(n_z)]
        ).astype(jnp.int32)
    else:
        offs = jnp.zeros((1,), jnp.int32)

    flat = jnp.concatenate(
        [
            qkv_bias.reshape(-1),
            out_bias,
            up_bias,
            down_bias,
            norm_gain.reshape(-1),
            norm_shift.reshape(-1),
        ]
    )
    lines = -(-flat.shape[0] // 128)
    flat = jnp.pad(flat, (0, lines * 128 - flat.shape[0])).reshape(lines, 128)
    extra = -(height + lines) % 16
    small = jnp.concatenate([proj_weight, flat, jnp.zeros((extra, 128), bf16)])
    small_all = gather_small(small, slots)
    proj = small_all[:, :height].reshape(model, emb)
    numbers = small_all[:, height : height + lines].reshape(n_dp, -1).astype(f32)
    pieces = numbers[:, : 12 * height].reshape(n_dp, 12, height)
    vectors = pieces.transpose(1, 0, 2).reshape(12, model)
    up_by_place = pieces[:, 3:7].reshape(4, ffn)
    up_bias_all = jnp.stack(
        [sum(jnp.where((t ^ r) == a, up_by_place[a], 0.0) for a in range(4)) for r in RELATIVE]
    )
    vectors = jnp.concatenate([vectors, jnp.zeros((4, model), f32)])

    swapped = half == 1
    tok_own = jnp.where(swapped, tokens[1], tokens[0])
    tok_far = swap(jnp.where(swapped, tokens[0], tokens[1]), FAR)
    tok_mate = swap(tok_own, MATE)
    tok_far_mate = swap(tok_far, MATE)
    toks = (tok_own, tok_far, tok_mate, tok_far_mate)

    piece_1 = jnp.concatenate([qkv_weight[0], qkv_weight[1], qkv_weight[2], out_weight.T], 1)
    piece_up = up_weight
    piece_down = down_weight.T

    if ring:
        line = [piece_1] + [pull_z(piece_1, step) for step in range(1, n_z)]
        blocks = line + [swap_y(b) for b in line]
        blocks_far = [swap(b, FAR) for b in blocks]
        tie = line[-1]
    else:
        blocks = [lax.all_gather(piece_1, "dp", axis=0, tiled=True)]
        blocks_far = [swap(blocks[0], FAR)]
        tie = blocks[0]

    def gather_ffn(piece):
        if ring:
            own = jnp.stack([piece] + [pull_z(piece, step) for step in range(1, n_z)])
            far = swap(own, FAR)
            near = [own, swap_y(own), far, swap_y(far)]
        else:
            own = lax.all_gather(piece, "dp", axis=0, tiled=True)[None]
            near = [own, swap(own, FAR)]
        return near + [swap(b, MATE) for b in near]

    ups = gather_ffn(after(piece_up, tie))
    downs = gather_ffn(after(piece_down, ups[0]))

    bounds = lengths[:, 0]
    bounds = jnp.where(swapped, bounds[1], bounds[0])
    ends = [jnp.sum(bounds[: j + 1]) for j in range(bounds.shape[0])]
    places = jnp.concatenate([share * (t ^ r) + lax.iota(jnp.int32, share) for r in RELATIVE])
    segment = sum((places >= e).astype(jnp.int32) for e in ends)
    hot = segment[None] == lax.iota(jnp.int32, MASK_ROWS)[:, None]
    qmask = jnp.where(hot, 1.0, 0.0).astype(bf16)
    kmask = jnp.where(hot, 0.0, MASKED).astype(bf16)
    valid = jnp.broadcast_to((places[: rows // 2] < ends[-1])[:, None], (rows // 2, emb)).astype(bf16)

    def bias_of(which):
        start = which * group
        part = lax.dynamic_slice_in_dim(vectors[:2], start, group, 1)
        row = jnp.concatenate([part[0], jnp.zeros((group,), f32), part[1]])
        return jnp.concatenate([row[None], jnp.zeros((7, 3 * group), f32)]).astype(bf16)

    qkv, wq, wo = project(offs, bias_of(t), blocks, toks)
    near, away, lse = attend(qkv, qmask, kmask)
    qkv_far, wq_far, wo_far = project(offs, bias_of(t ^ FAR), blocks_far, toks)
    near_far, away_far, lse_far = attend(qkv_far, qmask, kmask)

    cot_own = jnp.where(swapped, cotangent[1], cotangent[0])
    cot_far = swap(jnp.where(swapped, cotangent[0], cotangent[1]), FAR)
    atts = (near, near_far, swap(away, MATE), swap(away_far, MATE))
    outs_w = (wo, wo_far, swap(wo, MATE), swap(wo_far, MATE))
    (
        emb_own,
        emb_far,
        d_resid,
        d_att,
        d_att_far,
        d_att_mate,
        d_att_far_mate,
        g_up_keep,
        g_up_mate,
        g_down_keep,
        g_down_mate,
        g_out_keep,
        g_out_mate,
        g_proj,
        g_vec,
        g_up_bias,
    ) = middle(
        offs, slots, toks[:2], atts, outs_w, proj, vectors, up_bias_all, valid, (cot_own, cot_far), ups, downs
    )
    d_away = swap(d_att_mate, MATE)
    d_away_far = swap(d_att_far_mate, MATE)

    got_up = swap(g_up_mate, MATE)
    got_down = swap(g_down_mate, MATE)
    got_out = swap(g_out_mate, MATE)
    grad_up = scatter_sum(g_up_keep, got_up, slots)
    grad_down = scatter_sum(g_down_keep, got_down, slots, far_first=True).T

    def split(value):
        return jnp.stack([value[..., :group], value[..., group:]])

    grad_out = scatter_sum(split(g_out_keep), split(got_out), slots).T

    masks = (qmask, kmask)
    g_qkv_far, g_bias_far, d_qkv_far = attend_back(
        offs, slots, (qkv_far, near_far, away_far, d_att_far, d_away_far, lse_far, *masks, *toks)
    )
    g_qkv, g_bias, d_own, d_mate = attend_back(
        offs,
        slots,
        (qkv, near, away, d_att, d_away, lse, *masks, *toks),
        (wq, wq_far, d_qkv_far, d_resid),
    )

    def scatter_pair(own, far):
        if n_y == 1:
            rest = own[0, 0].astype(f32) + swap(far[0, 0], FAR).astype(f32)
            return lax.psum_scatter(rest.astype(bf16), "dp", scatter_dimension=0, tiled=True).astype(f32)
        far_sum = far[0].astype(f32) + swap_y(far[1]).astype(f32)
        got = swap(far_sum.astype(bf16), FAR)
        rest = own[0].astype(f32) + swap_y(own[1]).astype(f32) + got.astype(f32)
        total = rest[0]
        low = rest.astype(bf16)
        for step in range(1, n_z):
            total = total + push_z(low[step], step).astype(f32)
        return total

    grad_qkv = scatter_pair(g_qkv, g_qkv_far)
    grad_qkv = jnp.stack([grad_qkv[:, i * group : (i + 1) * group] for i in range(3)])

    d_input = (d_own + swap(d_mate, MATE).astype(f32)).astype(bf16)
    back = swap(d_input[share:], FAR)
    mine = d_input[:share]
    input_grad = jnp.stack([jnp.where(swapped, back, mine), jnp.where(swapped, mine, back)])
    emb_back = swap(emb_far, FAR)
    embeddings = jnp.stack([jnp.where(swapped, emb_back, emb_own), jnp.where(swapped, emb_own, emb_back)])

    up_by_index = jnp.stack(
        [sum(jnp.where((t ^ r) == a, g_up_bias[i], 0.0) for i, r in enumerate(RELATIVE)) for a in range(4)]
    )
    six = g_vec[:6].reshape(6, n_dp, height).transpose(1, 0, 2).reshape(n_dp, -1)
    early = jnp.concatenate([six, up_by_index.reshape(n_dp, -1)], 1)
    early_lines = -(-early.shape[1] // 128)
    early_lines += -early_lines % 8
    early = jnp.pad(early, ((0, 0), (0, early_lines * 128 - early.shape[1]))).reshape(n_dp, early_lines, 128)
    early = jnp.concatenate([g_proj.reshape(n_dp, height, emb), early], 1)
    early = share_small(early, slots)
    grad_proj = early[:height]
    rest = early[height:].reshape(-1)
    part = [rest[i * height : (i + 1) * height] for i in range(6)]
    grad_up_bias = rest[6 * height : 6 * height + 4 * height]

    late = jnp.zeros((2, model), f32)
    for which, row in ((t, g_bias[0]), (t ^ FAR, g_bias_far[0])):
        pair = jnp.stack([row[:group], row[2 * group :]])
        late = lax.dynamic_update_slice_in_dim(late, pair, which * group, 1)
    late = late.reshape(2, n_dp, height).transpose(1, 0, 2).reshape(n_dp, 2 * height)
    late_lines = -(-(2 * height) // 128)
    late_lines += -late_lines % 8
    late = jnp.pad(late, ((0, 0), (0, late_lines * 128 - 2 * height))).reshape(n_dp, late_lines, 128)
    late = share_small(late, slots).reshape(-1)[: 2 * height].reshape(2, height)

    return (
        embeddings,
        input_grad,
        grad_qkv,
        grad_out,
        grad_up,
        grad_down,
        late,
        part[4],
        grad_up_bias,
        part[5],
        jnp.stack([part[0], part[1]]),
        jnp.stack([part[2], part[3]]),
        grad_proj,
    )


def solution(mesh):
    rows = P(None, ("dp", "tensor"), None)
    shapes = (
        P(None, "dp", "tensor"),
        P("tensor", "dp"),
        P("dp", "tensor"),
        P("tensor", "dp"),
        P(None, "dp"),
        P("dp"),
        P("dp"),
        P("dp"),
        P(None, "dp"),
        P(None, "dp"),
        P("dp", None),
    )
    return jax.shard_map(
        per_device,
        mesh=mesh,
        in_specs=(rows, *shapes, P(None, "dp", None), rows),
        out_specs=(rows, rows, *shapes),
        check_vma=False,
    )
```

time: 1460 us -> 427 us (0.29)
  waiting for transfers between devices: 663 us -> 139 us
  matrix products: 279 us -> 0 us
  blocking collectives: 249 us -> 0 us
  Pallas kernels: 0 us -> 137 us
  other arithmetic: 129 us -> 29.3 us
  starting transfers between devices: 2.23 us -> 82.7 us
  local copies, waits for them, and re-layouts: 83 us -> 28.8 us
  loops' own time: 20.2 us -> 0 us
  between operations: 20 us -> 2.18 us
    reduce_scatter x11 -> x0, waiting for transfers between devices: 365 us -> none  [the longest x1 72.6 us: reduce_grads(): lax.psum_scatter(totals[3], 'dp', scatter_dimension=1, tiled=True)]
    dot_general x72 -> x0, matrix products: 279 us -> none  [the longest x12 55.2 us: masked_scores(): jnp.einsum('qhd,khd->hqk', query_block, keys_heads, preferred_element_typ...]
    unnamed x32 -> x0, waiting for transfers between devices: 221 us -> none
    all_gather x7 -> x0, blocking collectives: 182 us -> none  [the longest x1 34.2 us: gather_forward(): lax.all_gather(shards[0], 'dp', axis=1, tiled=True)]
    ppermute x0 -> x88, waiting for transfers between devices: none -> 139 us  [the longest x42 55.8 us: swap(): return lax.ppermute(value, 'tensor', [(i, i ^ bit) for i in range(count)])]
    pallas_call x0 -> x7, Pallas kernels: none -> 137 us  [kernel_call(): pl.pallas_call(body, out_shape=outs, in_specs=specs, out_specs=out_specs,...]
    ppermute x0 -> x88, starting transfers between devices: none -> 82.7 us  [the longest x18 23.1 us: push_z(): return lax.ppermute(value, 'dp', pairs)]
    all_gather x10 -> x0, waiting for transfers between devices: 77.2 us -> none  [the longest x2 41.2 us: per_device(): lax.all_gather(d_resid2.astype(jnp.bfloat16), 'tensor', axis=0, tiled=True)]
  transfers between devices with their start and end apart: 27 -> 88, of which waited for: 17 -> 32; matrix products, arithmetic and copies ran while one was open for 27% -> 10% of each run, Pallas kernels for 0% -> 23%
where the time goes in v1:
time: 427 us; the launch traced here: 420 us
  waiting for transfers between devices  139 us (33%)
  Pallas kernels  137 us (32%)
  starting transfers between devices  82.7 us (19%)
  other arithmetic  29.3 us (7%)
  local copies, waits for them, and re-layouts  28.8 us (7%)
    pallas_call x7, Pallas kernels, kernel_call(): pl.pallas_call(body, out_shape=outs, in_specs=specs, out_specs=out_specs,...  137 us
    ppermute x42, waiting for transfers between devices, swap(): return lax.ppermute(value, 'tensor', [(i, i ^ bit) for i in range(count)])  55.8 us
    ppermute x16, waiting for transfers between devices, swap_y(): return lax.ppermute(value, 'dp', [(i, i ^ 1) for i in range(count)])  44.8 us
    ppermute x18, waiting for transfers between devices, push_z(): return lax.ppermute(value, 'dp', pairs)  31.8 us
    ppermute x18, starting transfers between devices, push_z(): return lax.ppermute(value, 'dp', pairs)  23.1 us
    ppermute x42, starting transfers between devices, swap(): return lax.ppermute(value, 'tensor', [(i, i ^ bit) for i in range(count)])  22.4 us
    ppermute x12, starting transfers between devices, pull_z(): return lax.ppermute(value, 'dp', pairs)  21.4 us
    ppermute x16, starting transfers between devices, swap_y(): return lax.ppermute(value, 'dp', [(i, i ^ 1) for i in range(count)])  15.8 us
  transfers between devices with their start and end apart: 88, of which 32 were waited for; matrix products, arithmetic and copies ran while one was open for 10% of the time, Pallas kernels for 23%

profile of v1, /device:TPU:0, one launch (start us, length us, event | category | flops | bytes accessed | tf_op | source)
XLA Modules:
  0.0 419.6 jit_solution(14167962073148723912)
XLA Ops:
  3.1 2.1 concatenate.59
  6.0 5.1 %collective-permute-start.1 = (bf16[112,128]{1,0:T(8,128)(2,1)S(1)}, bf16[112,128]{1,0:T(8,128)(2,1)S(1)}, u32[]{:S(2)}, u32[]{:S(2)}) collective-permute-start(bf16[112,128]{1,0:T(8,128)(2,1)S(1)} %maximum_maximum_fusion), channel_id=1, source_target_pairs={{8,0},{12,4},{16,8},{20,12},{24,16},{28,20},{0,24},{4,28},{9,1},{1... | collective-permute-start | bytes 86024 | tf_op jit(solution)/shard_map/ppermute | solution.py:535
  14.0 2.5 collective-permute-start.7
  17.9 1.6 select_bitcast_fusion.10
  22.9 3.2 collective-permute-done.26.refs_15_
  28.2 4.3 %collective-permute-done.4 = bf16[4,112,128]{2,1,0:T(8,128)(2,1)} collective-permute-done((bf16[4,112,128]{2,1,0:T(8,128)(2,1)S(1)}, bf16[4,112,128]{2,1,0:T(8,128)(2,1)}, u32[]{:S(2)}, u32[]{:S(2)}) %collective-permute-start.4) | collective-permute-done | bytes 114720 | tf_op jit(solution)/shard_map/ppermute | solution.py:529
  33.0 3.2 collective-permute-start.27
  36.3 1.9 collective-permute-start.29
  39.4 4.2 %collective-permute-done.11.refs_7_ = bf16[96,768]{1,0:T(8,128)(2,1)} collective-permute-done((bf16[96,768]{1,0:T(8,128)(2,1)S(1)}, bf16[96,768]{1,0:T(8,128)(2,1)}, u32[]{:S(2)}, u32[]{:S(2)}) %collective-permute-start.11) | collective-permute-done | bytes 147488 | tf_op jit(solution)/shard_map/ppermute | solution.py:529
  52.9 3.5 collective-permute-start.37
  58.6 2.5 collective-permute-start.38
  64.6 7.0 %collective-permute-done.38 = bf16[96,768]{1,0:T(8,128)(2,1)} collective-permute-done((bf16[96,768]{1,0:T(8,128)(2,1)S(1)}, bf16[96,768]{1,0:T(8,128)(2,1)}, u32[]{:S(2)}, u32[]{:S(2)}) %collective-permute-start.38) | collective-permute-done | bytes 147488 | tf_op jit(solution)/shard_map/ppermute | solution.py:535
  75.8 5.0 %collective-permute-done.19.refs_5_ = bf16[96,768]{1,0:T(8,128)(2,1)S(1)} collective-permute-done((bf16[96,768]{1,0:T(8,128)(2,1)}, bf16[96,768]{1,0:T(8,128)(2,1)S(1)}, u32[]{:S(2)}, u32[]{:S(2)}) %collective-permute-start.19) | collective-permute-done | bytes 147488 | tf_op jit(solution)/shard_map/ppermute | solution.py:524
  85.8 5.5 %shard_map.239 = (bf16[576,1536]{1,0:T(8,128)(2,1)}, bf16[576,768]{1,0:T(8,128)(2,1)}, bf16[192,768]{1,0:T(8,128)(2,1)}) custom-call(s32[8]{0:T(128)} %stack.189.offs, bf16[8,576]{1,0:T(8,128)(2,1)} %concatenate.67.bias, bf16[96,768]{1,0:T(8,128)(2,1)} %collective-permute-done.14.refs_0_, bf16[96,768]{1,0:T(8,128)(2,1)} %collective-permute-done.15.refs_1_, ...), custom_call_target="tpu_custom_call" | custom-call | tf_op jit(solution)/shard_map/pallas_call | solution.py:33
  91.4 14.5 %shard_map.240 = (bf16[192,768]{1,0:T(8,128)(2,1)}, bf16[192,768]{1,0:T(8,128)(2,1)}, f32[8,1536]{1,0:T(8,128)}) custom-call(bf16[576,1536]{1,0:T(8,128)(2,1)} %get-tuple-element.52.qkv.refs_0_, bf16[16,1536]{1,0:T(8,128)(2,1)} %get-tuple-element.198.qmask.refs_6_, bf16[16,1536]{1,0:T(8,128)(2,1)} %get-tuple-element.197.kmask.refs_7_), custom_call_target="tpu_custom_call" | custom-call | tf_op jit(solution)/shard_map/pallas_call | solution.py:33
  109.2 5.5 %shard_map.237 = (bf16[576,1536]{1,0:T(8,128)(2,1)}, bf16[576,768]{1,0:T(8,128)(2,1)}, bf16[192,768]{1,0:T(8,128)(2,1)}) custom-call(s32[8]{0:T(128)} %stack.189.offs, bf16[8,576]{1,0:T(8,128)(2,1)} %concatenate.63.bias, bf16[96,768]{1,0:T(8,128)(2,1)} %copy-done.19, bf16[96,768]{1,0:T(8,128)(2,1)} %copy-done.33, bf16[96,768]{1,0:T(8,128)(2,1)} %copy-done.34, ...), custom_call_target="tpu_custom_call" | custom-call | tf_op jit(solution)/shard_map/pallas_call | solution.py:33
  114.8 14.5 %shard_map.238 = (bf16[192,768]{1,0:T(8,128)(2,1)}, bf16[192,768]{1,0:T(8,128)(2,1)}, f32[8,1536]{1,0:T(8,128)}) custom-call(bf16[576,1536]{1,0:T(8,128)(2,1)} %get-tuple-element.50.qkv.refs_0_, bf16[16,1536]{1,0:T(8,128)(2,1)} %get-tuple-element.198.qmask.refs_6_, bf16[16,1536]{1,0:T(8,128)(2,1)} %get-tuple-element.197.kmask.refs_7_), custom_call_target="tpu_custom_call" | custom-call | tf_op jit(solution)/shard_map/pallas_call | solution.py:33
  132.1 2.8 collective-permute-done.42.refs_27_
  140.7 40.8 %shard_map.241 = (bf16[384,128]{1,0:T(8,128)(2,1)}, bf16[384,128]{1,0:T(8,128)(2,1)}, f32[768,768]{1,0:T(8,128)}, bf16[192,768]{1,0:T(8,128)(2,1)}, bf16[192,768...) custom-call(s32[8]{0:T(128)} %stack.189.offs, ...), custom_call_target="tpu_custom_call" | custom-call | tf_op jit(solution)/shard_map/pallas_call | solution.py:33
  187.8 4.2 collective-permute-done.47
  194.2 25.6 %shard_map.242 = (bf16[2,4,96,576]{3,2,1,0:T(8,128)(2,1)}, f32[8,576]{1,0:T(8,128)}, bf16[576,1536]{1,0:T(8,128)(2,1)}) custom-call(s32[8]{0:T(128)} %stack.189.offs, bf16[576,1536]{1,0:T(8,128)(2,1)} %get-tuple-element.52.qkv.refs_0_, bf16[192,768]{1,0:T(8,128)(2,1)} %get-tuple-element.53.refs_3_.refs_1_, bf16[192,768]{1,0:T(8,128)(2,1)} %get-tuple-element.55.refs_2_, ...), custom_call_target="tpu_custom_call" | custom-call | tf_op jit(solution)/shard_map/pallas_call | solution.py:33
  221.2 30.9 %shard_map.243 = (bf16[2,4,96,576]{3,2,1,0:T(8,128)(2,1)}, f32[8,576]{1,0:T(8,128)}, f32[768,768]{1,0:T(8,128)}, bf16[768,768]{1,0:T(8,128)(2,1)}) custom-call(s32[8]{0:T(128)} %stack.189.offs, bf16[576,1536]{1,0:T(8,128)(2,1)} %get-tuple-element.50.qkv.refs_0_, bf16[192,768]{1,0:T(8,128)(2,1)} %get-tuple-element.51.refs_2_.refs_1_, ...), custom_call_target="tpu_custom_call" | custom-call | tf_op jit(solution)/shard_map/pallas_call | solution.py:33
  257.7 1.9 slice_bitcast_fusion.5
  262.3 2.0 collective-permute-done.78
  265.6 2.2 collective-permute-start.80
  272.0 3.2 collective-permute-done.84
  276.4 2.7 collective-permute-start.86
  279.1 1.9 collective-permute-start.87
  286.8 26.6 %collective-permute-done.59 = bf16[2,4,96,192]{3,2,1,0:T(8,128)(2,1)S(1)} collective-permute-done((bf16[2,4,96,192]{3,2,1,0:T(8,128)(2,1)S(1)}, bf16[2,4,96,192]{3,2,1,0:T(8,128)(2,1)S(1)}, u32[]{:S(2)}, u32[]{:S(2)}) %collective-permute-start.59) | collective-permute-done | bytes 294944 | tf_op jit(solution)/shard_map/ppermute | solution.py:529
  314.6 4.6 %collective-permute-done.60 = bf16[4,96,192]{2,1,0:T(8,128)(2,1)S(1)} collective-permute-done((bf16[4,96,192]{2,1,0:T(8,128)(2,1)S(1)}, bf16[4,96,192]{2,1,0:T(8,128)(2,1)S(1)}, u32[]{:S(2)}, u32[]{:S(2)}) %collective-permute-start.60) | collective-permute-done | bytes 147488 | tf_op jit(solution)/shard_map/ppermute | solution.py:524
  321.3 3.9 collective-permute-done.61
  326.1 4.1 collective-permute-done.62
  332.1 2.2 collective-permute-done.63
  335.0 1.6 copy.70
  336.7 1.7 fusion.75
  338.4 2.4 collective-permute-start.56
  342.3 1.7 fusion.1
  344.0 2.5 collective-permute-done.55
  346.9 3.9 collective-permute-done.56
  354.5 20.9 %collective-permute-done.71 = bf16[2,4,96,768]{3,2,1,0:T(8,128)(2,1)S(1)} collective-permute-done((bf16[2,4,96,768]{3,2,1,0:T(8,128)(2,1)S(1)}, bf16[2,4,96,768]{3,2,1,0:T(8,128)(2,1)S(1)}, u32[]{:S(2)}, u32[]{:S(2)}) %collective-permute-start.71) | collective-permute-done | bytes 1179680 | tf_op jit(solution)/shard_map/ppermute | solution.py:524
  378.1 8.2 %collective-permute-done.51 = bf16[384,768]{1,0:T(8,128)(2,1)S(1)} collective-permute-done((bf16[384,768]{1,0:T(8,128)(2,1)S(1)}, bf16[384,768]{1,0:T(8,128)(2,1)S(1)}, u32[]{:S(2)}, u32[]{:S(2)}) %collective-permute-start.51) | collective-permute-done | bytes 589856 | tf_op jit(solution)/shard_map/ppermute | solution.py:524
  388.2 3.0 collective-permute-done.72
  392.6 3.2 collective-permute-start.73
  396.7 1.6 collective-permute-start.75
  398.3 1.9 collective-permute-done.66
  401.6 2.8 collective-permute-start.69
  404.4 5.7 %collective-permute-done.74 = bf16[96,768]{1,0:T(8,128)(2,1)S(1)} collective-permute-done((bf16[96,768]{1,0:T(8,128)(2,1)S(1)}, bf16[96,768]{1,0:T(8,128)(2,1)S(1)}, u32[]{:S(2)}, u32[]{:S(2)}) %collective-permute-start.74) | collective-permute-done | bytes 147488 | tf_op jit(solution)/shard_map/ppermute | solution.py:541
  410.9 7.4 %collective-permute-done.68 = bf16[96,768]{1,0:T(8,128)(2,1)S(1)} collective-permute-done((bf16[96,768]{1,0:T(8,128)(2,1)S(1)}, bf16[96,768]{1,0:T(8,128)(2,1)S(1)}, u32[]{:S(2)}, u32[]{:S(2)}) %collective-permute-start.68) | collective-permute-done | bytes 147488 | tf_op jit(solution)/shard_map/ppermute | solution.py:541
  (375 shorter events, 103.2 us)
Async XLA Ops:
  6.0 13.6 %collective-permute-start.1 = (bf16[112,128]{1,0:T(8,128)(2,1)S(1)}, bf16[112,128]{1,0:T(8,128)(2,1)S(1)}, u32[]{:S(2)}, u32[]{:S(2)}) collective-permute-start(bf16[112,128]{1,0:T(8,128)(2,1)S(1)} %maximum_maximum_fusion), channel_id=1, source_target_pairs={{8,0},{12,4},{16,8},{20,12},{24,16},{28,20},{0,24},{4,28},{9,1},{1... | collective-permute-start | bytes 86024 | tf_op jit(solution)/shard_map/ppermute | solution.py:535
  11.1 10.2 %collective-permute-start.3 = (bf16[112,128]{1,0:T(8,128)(2,1)S(1)}, bf16[112,128]{1,0:T(8,128)(2,1)S(1)}, u32[]{:S(2)}, u32[]{:S(2)}) collective-permute-start(bf16[112,128]{1,0:T(8,128)(2,1)S(1)} %maximum_maximum_fusion), channel_id=1, source_target_pairs={{24,0},{28,4},{0,8},{4,12},{8,16},{12,20},{16,24},{20,28},{25,1},{... | collective-permute-start | bytes 86024 | tf_op jit(solution)/shard_map/ppermute | solution.py:535
  14.0 13.6 %collective-permute-start.7 = (bf16[96,768]{1,0:T(8,128)(2,1)S(1)}, bf16[96,768]{1,0:T(8,128)(2,1)S(1)}, u32[]{:S(2)}, u32[]{:S(2)}) collective-permute-start(bf16[96,768]{1,0:T(8,128)(2,1)S(1)} %pad_maximum_fusion.8.refs_0_), channel_id=1, source_target_pairs={{24,0},{28,4},{0,8},{4,12},{8,16},{12,20},{16,24},{20,28},{25,1},{... | collective-permute-start | bytes 442376 | tf_op jit(solution)/shard_map/ppermute | solution.py:535
  16.5 16.5 %collective-permute-start.5 = (bf16[96,768]{1,0:T(8,128)(2,1)S(1)}, bf16[96,768]{1,0:T(8,128)(2,1)S(1)}, u32[]{:S(2)}, u32[]{:S(2)}) collective-permute-start(bf16[96,768]{1,0:T(8,128)(2,1)S(1)} %pad_maximum_fusion.8.refs_0_), channel_id=1, source_target_pairs={{8,0},{12,4},{16,8},{20,12},{24,16},{28,20},{0,24},{4,28},{9,1},{1... | collective-permute-start | bytes 442376 | tf_op jit(solution)/shard_map/ppermute | solution.py:535
  19.6 16.7 %collective-permute-start.6 = (bf16[96,768]{1,0:T(8,128)(2,1)S(1)}, bf16[96,768]{1,0:T(8,128)(2,1)S(1)}, u32[]{:S(2)}, u32[]{:S(2)}) collective-permute-start(bf16[96,768]{1,0:T(8,128)(2,1)S(1)} %pad_maximum_fusion.8.refs_0_), channel_id=1, source_target_pairs={{16,0},{20,4},{24,8},{28,12},{0,16},{4,20},{8,24},{12,28},{17,1},{... | collective-permute-start | bytes 442376 | tf_op jit(solution)/shard_map/ppermute | solution.py:535
  19.8 16.4 %collective-permute-start.8 = (bf16[96,768]{1,0:T(8,128)(2,1)S(1)}, bf16[96,768]{1,0:T(8,128)(2,1)S(1)}, u32[]{:S(2)}, u32[]{:S(2)}) collective-permute-start(bf16[96,768]{1,0:T(8,128)(2,1)S(1)} %pad_maximum_fusion.8.refs_0_), channel_id=1, source_target_pairs={{0,4},{4,0},{8,12},{12,8},{16,20},{20,16},{24,28},{28,24},{1,5},{5... | collective-permute-start | bytes 442376 | tf_op jit(solution)/shard_map/ppermute | solution.py:529
  26.1 12.1 %collective-permute-start.14 = (bf16[96,768]{1,0:T(8,128)(2,1)S(1)}, bf16[96,768]{1,0:T(8,128)(2,1)}, u32[]{:S(2)}, u32[]{:S(2)}) collective-permute-start(bf16[96,768]{1,0:T(8,128)(2,1)S(1)} %pad_maximum_fusion.8.refs_0_), channel_id=1, source_target_pairs={{0,2},{1,3},{2,0},{3,1},{4,6},{5,7},{6,4},{7,5},{8,10},{9,11},{10,... | collective-permute-start | bytes 442376 | tf_op jit(solution)/shard_map/ppermute | solution.py:524
  32.5 30.7 %collective-permute-start = (bf16[384,768]{1,0:T(8,128)(2,1)S(1)}, bf16[384,768]{1,0:T(8,128)(2,1)S(1)}, u32[]{:S(2)}, u32[]{:S(2)}) collective-permute-start(bf16[384,768]{1,0:T(8,128)(2,1)S(1)} %get-tuple-element.146), channel_id=1, source_target_pairs={{0,2},{1,3},{2,0},{3,1},{4,6},{5,7},{6,4},{7,5},{8,10},{9,11},{10,... | collective-permute-start | bytes 1769480 | tf_op jit(solution)/shard_map/ppermute | solution.py:524
  33.0 11.9 %collective-permute-start.27 = (bf16[96,768]{1,0:T(8,128)(2,1)S(1)}, bf16[96,768]{1,0:T(8,128)(2,1)S(1)}, u32[]{:S(2)}, u32[]{:S(2)}) collective-permute-start(bf16[96,768]{1,0:T(8,128)(2,1)S(1)} %copy-done.30), channel_id=1, source_target_pairs={{8,0},{12,4},{16,8},{20,12},{24,16},{28,20},{0,24},{4,28},{9,1},{1... | collective-permute-start | bytes 442376 | tf_op jit(solution)/shard_map/ppermute | solution.py:535
  36.2 9.3 %collective-permute-start.28 = (bf16[96,768]{1,0:T(8,128)(2,1)S(1)}, bf16[96,768]{1,0:T(8,128)(2,1)S(1)}, u32[]{:S(2)}, u32[]{:S(2)}) collective-permute-start(bf16[96,768]{1,0:T(8,128)(2,1)S(1)} %copy-done.30), channel_id=1, source_target_pairs={{16,0},{20,4},{24,8},{28,12},{0,16},{4,20},{8,24},{12,28},{17,1},{... | collective-permute-start | bytes 442376 | tf_op jit(solution)/shard_map/ppermute | solution.py:535
  36.3 10.8 %collective-permute-start.29 = (bf16[96,768]{1,0:T(8,128)(2,1)S(1)}, bf16[96,768]{1,0:T(8,128)(2,1)S(1)}, u32[]{:S(2)}, u32[]{:S(2)}) collective-permute-start(bf16[96,768]{1,0:T(8,128)(2,1)S(1)} %copy-done.30), channel_id=1, source_target_pairs={{24,0},{28,4},{0,8},{4,12},{8,16},{12,20},{16,24},{20,28},{25,1},{... | collective-permute-start | bytes 442376 | tf_op jit(solution)/shard_map/ppermute | solution.py:535
  45.6 10.8 %collective-permute-start.15 = (bf16[96,768]{1,0:T(8,128)(2,1)S(1)}, bf16[96,768]{1,0:T(8,128)(2,1)}, u32[]{:S(2)}, u32[]{:S(2)}) collective-permute-start(bf16[96,768]{1,0:T(8,128)(2,1)S(1)} %collective-permute-done.5.refs_1_), channel_id=1, source_target_pairs={{0,2},{1,3},{2,0},{3,1},{4,6},{5,7},{6,4},{7,5},{8,10},{9,11},{10,... | collective-permute-start | bytes 442376 | tf_op jit(solution)/shard_map/ppermute | solution.py:524
  58.6 23.8 %collective-permute-start.12 = (bf16[384,768]{1,0:T(8,128)(2,1)S(1)}, bf16[384,768]{1,0:T(8,128)(2,1)S(1)}, u32[]{:S(2)}, u32[]{:S(2)}) collective-permute-start(bf16[384,768]{1,0:T(8,128)(2,1)S(1)} %get-tuple-element.147.refs_8_.refs_0_), channel_id=1, source_target_pairs={{0,1},{1,0},{2,3},{3,2},{4,5},{5,4},{6,7},{7,6},{8,9},{9,8},{10,11... | collective-permute-start | bytes 1769480 | tf_op jit(solution)/shard_map/ppermute | solution.py:524
  58.6 13.0 %collective-permute-start.38 = (bf16[96,768]{1,0:T(8,128)(2,1)S(1)}, bf16[96,768]{1,0:T(8,128)(2,1)}, u32[]{:S(2)}, u32[]{:S(2)}) collective-permute-start(bf16[96,768]{1,0:T(8,128)(2,1)S(1)} %bitcast.332), channel_id=1, source_target_pairs={{16,0},{20,4},{24,8},{28,12},{0,16},{4,20},{8,24},{12,28},{17,1},{... | collective-permute-start | bytes 442376 | tf_op jit(solution)/shard_map/ppermute | solution.py:535
  61.7 11.3 %collective-permute-start.39 = (bf16[96,768]{1,0:T(8,128)(2,1)S(1)}, bf16[96,768]{1,0:T(8,128)(2,1)}, u32[]{:S(2)}, u32[]{:S(2)}) collective-permute-start(bf16[96,768]{1,0:T(8,128)(2,1)S(1)} %bitcast.333), channel_id=1, source_target_pairs={{24,0},{28,4},{0,8},{4,12},{8,16},{12,20},{16,24},{20,28},{25,1},{... | collective-permute-start | bytes 442376 | tf_op jit(solution)/shard_map/ppermute | solution.py:535
  61.8 22.0 %collective-permute-start.31 = (bf16[4,96,768]{2,1,0:T(8,128)(2,1)S(1)}, bf16[4,96,768]{2,1,0:T(8,128)(2,1)}, u32[]{:S(2)}, u32[]{:S(2)}) collective-permute-start(bf16[4,96,768]{2,1,0:T(8,128)(2,1)S(1)} %pad_maximum_fusion.1.refs_16_), channel_id=1, source_target_pairs={{0,2},{1,3},{2,0},{3,1},{4,6},{5,7},{6,4},{7,5},{8,10},{9,11},{10,... | collective-permute-start | bytes 1769480 | tf_op jit(solution)/shard_map/ppermute | solution.py:524
  63.2 21.5 %collective-permute-start.13 = (bf16[384,768]{1,0:T(8,128)(2,1)S(1)}, bf16[384,768]{1,0:T(8,128)(2,1)S(1)}, u32[]{:S(2)}, u32[]{:S(2)}) collective-permute-start(bf16[384,768]{1,0:T(8,128)(2,1)S(1)} %collective-permute-done.refs_9_.refs_1_), channel_id=1, source_target_pairs={{0,1},{1,0},{2,3},{3,2},{4,5},{5,4},{6,7},{7,6},{8,9},{9,8},{10,11... | collective-permute-start | bytes 1769480 | tf_op jit(solution)/shard_map/ppermute | solution.py:524
  80.8 25.0 %collective-permute-start.30 = (bf16[4,96,768]{2,1,0:T(8,128)(2,1)S(1)}, bf16[4,96,768]{2,1,0:T(8,128)(2,1)}, u32[]{:S(2)}, u32[]{:S(2)}) collective-permute-start(bf16[4,96,768]{2,1,0:T(8,128)(2,1)S(1)} %pad_maximum_fusion.1.refs_16_), channel_id=1, source_target_pairs={{0,4},{4,0},{8,12},{12,8},{16,20},{20,16},{24,28},{28,24},{1,5},{5... | collective-permute-start | bytes 1769480 | tf_op jit(solution)/shard_map/ppermute | solution.py:529
  82.4 23.9 %collective-permute-start.33 = (bf16[4,96,768]{2,1,0:T(8,128)(2,1)S(1)}, bf16[4,96,768]{2,1,0:T(8,128)(2,1)}, u32[]{:S(2)}, u32[]{:S(2)}) collective-permute-start(bf16[4,96,768]{2,1,0:T(8,128)(2,1)S(1)} %pad_maximum_fusion.1.refs_16_), channel_id=1, source_target_pairs={{0,1},{1,0},{2,3},{3,2},{4,5},{5,4},{6,7},{7,6},{8,9},{9,8},{10,11... | collective-permute-start | bytes 1769480 | tf_op jit(solution)/shard_map/ppermute | solution.py:524
  82.4 24.0 %collective-permute-start.41 = (bf16[4,96,768]{2,1,0:T(8,128)(2,1)S(1)}, bf16[4,96,768]{2,1,0:T(8,128)(2,1)}, u32[]{:S(2)}, u32[]{:S(2)}) collective-permute-start(bf16[4,96,768]{2,1,0:T(8,128)(2,1)S(1)} %pad_maximum_fusion.2.refs_24_), channel_id=1, source_target_pairs={{0,2},{1,3},{2,0},{3,1},{4,6},{5,7},{6,4},{7,5},{8,10},{9,11},{10,... | collective-permute-start | bytes 1769480 | tf_op jit(solution)/shard_map/ppermute | solution.py:524
  83.8 23.8 %collective-permute-start.40 = (bf16[4,96,768]{2,1,0:T(8,128)(2,1)S(1)}, bf16[4,96,768]{2,1,0:T(8,128)(2,1)}, u32[]{:S(2)}, u32[]{:S(2)}) collective-permute-start(bf16[4,96,768]{2,1,0:T(8,128)(2,1)S(1)} %pad_maximum_fusion.2.refs_24_), channel_id=1, source_target_pairs={{0,4},{4,0},{8,12},{12,8},{16,20},{20,16},{24,28},{28,24},{1,5},{5... | collective-permute-start | bytes 1769480 | tf_op jit(solution)/shard_map/ppermute | solution.py:529
  84.6 23.2 %collective-permute-start.43 = (bf16[4,96,768]{2,1,0:T(8,128)(2,1)S(1)}, bf16[4,96,768]{2,1,0:T(8,128)(2,1)}, u32[]{:S(2)}, u32[]{:S(2)}) collective-permute-start(bf16[4,96,768]{2,1,0:T(8,128)(2,1)S(1)} %pad_maximum_fusion.2.refs_24_), channel_id=1, source_target_pairs={{0,1},{1,0},{2,3},{3,2},{4,5},{5,4},{6,7},{7,6},{8,9},{9,8},{10,11... | collective-permute-start | bytes 1769480 | tf_op jit(solution)/shard_map/ppermute | solution.py:524
  105.9 23.4 %collective-permute-start.23 = (bf16[192,768]{1,0:T(8,128)(2,1)}, bf16[192,768]{1,0:T(8,128)(2,1)S(1)}, u32[]{:S(2)}, u32[]{:S(2)}) collective-permute-start(bf16[192,768]{1,0:T(8,128)(2,1)} %get-tuple-element.55.refs_2_), channel_id=1, source_target_pairs={{0,1},{1,0},{2,3},{3,2},{4,5},{5,4},{6,7},{7,6},{8,9},{9,8},{10,11... | collective-permute-start | bytes 884744 | tf_op jit(solution)/shard_map/ppermute | solution.py:524
  106.3 23.0 %collective-permute-start.25 = (bf16[192,768]{1,0:T(8,128)(2,1)S(1)}, bf16[192,768]{1,0:T(8,128)(2,1)S(1)}, u32[]{:S(2)}, u32[]{:S(2)}) collective-permute-start(bf16[192,768]{1,0:T(8,128)(2,1)S(1)} %copy-done.23), channel_id=1, source_target_pairs={{0,1},{1,0},{2,3},{3,2},{4,5},{5,4},{6,7},{7,6},{8,9},{9,8},{10,11... | collective-permute-start | bytes 884744 | tf_op jit(solution)/shard_map/ppermute | solution.py:524
  106.4 25.2 %collective-permute-start.32 = (bf16[4,96,768]{2,1,0:T(8,128)(2,1)}, bf16[4,96,768]{2,1,0:T(8,128)(2,1)S(1)}, u32[]{:S(2)}, u32[]{:S(2)}) collective-permute-start(bf16[4,96,768]{2,1,0:T(8,128)(2,1)} %collective-permute-done.31.refs_18_), channel_id=1, source_target_pairs={{0,4},{4,0},{8,12},{12,8},{16,20},{20,16},{24,28},{28,24},{1,5},{5... | collective-permute-start | bytes 1769480 | tf_op jit(solution)/shard_map/ppermute | solution.py:529
  107.7 24.3 %collective-permute-start.35 = (bf16[4,96,768]{2,1,0:T(8,128)(2,1)}, bf16[4,96,768]{2,1,0:T(8,128)(2,1)S(1)}, u32[]{:S(2)}, u32[]{:S(2)}) collective-permute-start(bf16[4,96,768]{2,1,0:T(8,128)(2,1)} %collective-permute-done.31.refs_18_), channel_id=1, source_target_pairs={{0,1},{1,0},{2,3},{3,2},{4,5},{5,4},{6,7},{7,6},{8,9},{9,8},{10,11... | collective-permute-start | bytes 1769480 | tf_op jit(solution)/shard_map/ppermute | solution.py:524
  107.8 27.1 %collective-permute-start.42 = (bf16[4,96,768]{2,1,0:T(8,128)(2,1)}, bf16[4,96,768]{2,1,0:T(8,128)(2,1)S(1)}, u32[]{:S(2)}, u32[]{:S(2)}) collective-permute-start(bf16[4,96,768]{2,1,0:T(8,128)(2,1)} %collective-permute-done.41.refs_26_), channel_id=1, source_target_pairs={{0,4},{4,0},{8,12},{12,8},{16,20},{20,16},{24,28},{28,24},{1,5},{5... | collective-permute-start | bytes 1769480 | tf_op jit(solution)/shard_map/ppermute | solution.py:529
  186.3 34.2 %collective-permute-start.48 = (bf16[192,768]{1,0:T(8,128)(2,1)}, bf16[192,768]{1,0:T(8,128)(2,1)S(1)}, u32[]{:S(2)}, u32[]{:S(2)}) collective-permute-start(bf16[192,768]{1,0:T(8,128)(2,1)} %get-tuple-element.63), channel_id=1, source_target_pairs={{0,1},{1,0},{2,3},{3,2},{4,5},{5,4},{6,7},{7,6},{8,9},{9,8},{10,11... | collective-permute-start | bytes 884744 | tf_op jit(solution)/shard_map/ppermute | solution.py:524
  186.7 154.1 %collective-permute-start.70 = (bf16[2,2,4,96,768]{4,3,2,1,0:T(8,128)(2,1)}, bf16[2,2,4,96,768]{4,3,2,1,0:T(8,128)(2,1)}, u32[]{:S(2)}, u32[]{:S(2)}) collective-permute-start(bf16[2,2,4,96,768]{4,3,2,1,0:T(8,128)(2,1)} %get-tuple-element.81), channel_id=1, source_target_pairs={{0,1},{1,0},{2,3},{3,2},{4,5},{5,4},{6,7},{7,6},{8,9},{9,8},{10,11... | collective-permute-start | bytes 7077896 | tf_op jit(solution)/shard_map/ppermute | solution.py:524
  191.9 158.9 %collective-permute-start.64 = (bf16[2,2,4,96,768]{4,3,2,1,0:T(8,128)(2,1)}, bf16[2,2,4,96,768]{4,3,2,1,0:T(8,128)(2,1)S(1)}, u32[]{:S(2)}, u32[]{:S(2)}) collective-permute-start(bf16[2,2,4,96,768]{4,3,2,1,0:T(8,128)(2,1)} %get-tuple-element.79), channel_id=1, source_target_pairs={{0,1},{1,0},{2,3},{3,2},{4,5},{5,4},{6,7},{7,6},{8,9},{9,8},{10,11... | collective-permute-start | bytes 7077896 | tf_op jit(solution)/shard_map/ppermute | solution.py:524
  255.5 12.3 %collective-permute-start.83 = (bf16[4,104,128]{2,1,0:T(8,128)(2,1)S(1)}, bf16[4,104,128]{2,1,0:T(8,128)(2,1)S(1)}, u32[]{:S(2)}, u32[]{:S(2)}) collective-permute-start(bf16[4,104,128]{2,1,0:T(8,128)(2,1)S(1)} %fusion.31), channel_id=1, source_target_pairs={{0,4},{4,0},{8,12},{12,8},{16,20},{20,16},{24,28},{28,24},{1,5},{5... | collective-permute-start | bytes 319496 | tf_op jit(solution)/shard_map/ppermute | solution.py:529
  283.3 36.6 %collective-permute-start.53 = (bf16[4,96,576]{2,1,0:T(8,128)(2,1)S(1)}, bf16[4,96,576]{2,1,0:T(8,128)(2,1)S(1)}, u32[]{:S(2)}, u32[]{:S(2)}) collective-permute-start(bf16[4,96,576]{2,1,0:T(8,128)(2,1)S(1)} %copy-done.20), channel_id=1, source_target_pairs={{0,4},{4,0},{8,12},{12,8},{16,20},{20,16},{24,28},{28,24},{1,5},{5... | collective-permute-start | bytes 1327112 | tf_op jit(solution)/shard_map/ppermute | solution.py:529
  284.7 52.0 %collective-permute-start.52 = (bf16[4,96,576]{2,1,0:T(8,128)(2,1)}, bf16[4,96,576]{2,1,0:T(8,128)(2,1)}, u32[]{:S(2)}, u32[]{:S(2)}) collective-permute-start(bf16[4,96,576]{2,1,0:T(8,128)(2,1)} %slice_bitcast_fusion.6), channel_id=1, source_target_pairs={{0,4},{4,0},{8,12},{12,8},{16,20},{20,16},{24,28},{28,24},{1,5},{5... | collective-permute-start | bytes 1327112 | tf_op jit(solution)/shard_map/ppermute | solution.py:529
  285.3 28.0 %collective-permute-start.59 = (bf16[2,4,96,192]{3,2,1,0:T(8,128)(2,1)S(1)}, bf16[2,4,96,192]{3,2,1,0:T(8,128)(2,1)S(1)}, u32[]{:S(2)}, u32[]{:S(2)}) collective-permute-start(bf16[2,4,96,192]{3,2,1,0:T(8,128)(2,1)S(1)} %fusion.11), channel_id=1, source_target_pairs={{0,4},{4,0},{8,12},{12,8},{16,20},{20,16},{24,28},{28,24},{1,5},{5... | collective-permute-start | bytes 884744 | tf_op jit(solution)/shard_map/ppermute | solution.py:529
  320.9 15.8 %collective-permute-start.54 = (bf16[4,96,576]{2,1,0:T(8,128)(2,1)}, bf16[4,96,576]{2,1,0:T(8,128)(2,1)}, u32[]{:S(2)}, u32[]{:S(2)}) collective-permute-start(bf16[4,96,576]{2,1,0:T(8,128)(2,1)} %fusion.6), channel_id=1, source_target_pairs={{0,2},{1,3},{2,0},{3,1},{4,6},{5,7},{6,4},{7,5},{8,10},{9,11},{10,... | collective-permute-start | bytes 1327112 | tf_op jit(solution)/shard_map/ppermute | solution.py:524
  334.4 18.3 %collective-permute-start.50 = (bf16[768,768]{1,0:T(8,128)(2,1)}, bf16[768,768]{1,0:T(8,128)(2,1)S(1)}, u32[]{:S(2)}, u32[]{:S(2)}) collective-permute-start(bf16[768,768]{1,0:T(8,128)(2,1)} %get-tuple-element.73), channel_id=1, source_target_pairs={{0,1},{1,0},{2,3},{3,2},{4,5},{5,4},{6,7},{7,6},{8,9},{9,8},{10,11... | collective-permute-start | bytes 3538952 | tf_op jit(solution)/shard_map/ppermute | solution.py:524
  338.4 12.4 %collective-permute-start.56 = (bf16[96,576]{1,0:T(8,128)(2,1)S(1)}, bf16[96,576]{1,0:T(8,128)(2,1)S(1)}, u32[]{:S(2)}, u32[]{:S(2)}) collective-permute-start(bf16[96,576]{1,0:T(8,128)(2,1)S(1)} %get-tuple-element.161), channel_id=1, source_target_pairs={{0,16},{4,20},{8,24},{12,28},{16,0},{20,4},{24,8},{28,12},{1,17},{... | collective-permute-start | bytes 331784 | tf_op jit(solution)/shard_map/ppermute | solution.py:541
  340.8 10.0 %collective-permute-start.57 = (bf16[96,576]{1,0:T(8,128)(2,1)S(1)}, bf16[96,576]{1,0:T(8,128)(2,1)S(1)}, u32[]{:S(2)}, u32[]{:S(2)}) collective-permute-start(bf16[96,576]{1,0:T(8,128)(2,1)S(1)} %get-tuple-element.160), channel_id=1, source_target_pairs={{0,24},{4,28},{8,0},{12,4},{16,8},{20,12},{24,16},{28,20},{1,25},{... | collective-permute-start | bytes 331784 | tf_op jit(solution)/shard_map/ppermute | solution.py:541
  346.5 28.9 %collective-permute-start.71 = (bf16[2,4,96,768]{3,2,1,0:T(8,128)(2,1)S(1)}, bf16[2,4,96,768]{3,2,1,0:T(8,128)(2,1)S(1)}, u32[]{:S(2)}, u32[]{:S(2)}) collective-permute-start(bf16[2,4,96,768]{3,2,1,0:T(8,128)(2,1)S(1)} %fusion.1), channel_id=1, source_target_pairs={{0,2},{1,3},{2,0},{3,1},{4,6},{5,7},{6,4},{7,5},{8,10},{9,11},{10,... | collective-permute-start | bytes 3538952 | tf_op jit(solution)/shard_map/ppermute | solution.py:524
  351.2 35.1 %collective-permute-start.65 = (bf16[2,4,96,768]{3,2,1,0:T(8,128)(2,1)S(1)}, bf16[2,4,96,768]{3,2,1,0:T(8,128)(2,1)S(1)}, u32[]{:S(2)}, u32[]{:S(2)}) collective-permute-start(bf16[2,4,96,768]{3,2,1,0:T(8,128)(2,1)S(1)} %fusion), channel_id=1, source_target_pairs={{0,4},{4,0},{8,12},{12,8},{16,20},{20,16},{24,28},{28,24},{1,5},{5... | collective-permute-start | bytes 3538952 | tf_op jit(solution)/shard_map/ppermute | solution.py:529
  353.0 33.2 %collective-permute-start.51 = (bf16[384,768]{1,0:T(8,128)(2,1)S(1)}, bf16[384,768]{1,0:T(8,128)(2,1)S(1)}, u32[]{:S(2)}, u32[]{:S(2)}) collective-permute-start(bf16[384,768]{1,0:T(8,128)(2,1)S(1)} %slice.514), channel_id=1, source_target_pairs={{0,2},{1,3},{2,0},{3,1},{4,6},{5,7},{6,4},{7,5},{8,10},{9,11},{10,... | collective-permute-start | bytes 1769480 | tf_op jit(solution)/shard_map/ppermute | solution.py:524
  376.7 14.5 %collective-permute-start.72 = (bf16[4,96,768]{2,1,0:T(8,128)(2,1)S(1)}, bf16[4,96,768]{2,1,0:T(8,128)(2,1)S(1)}, u32[]{:S(2)}, u32[]{:S(2)}) collective-permute-start(bf16[4,96,768]{2,1,0:T(8,128)(2,1)S(1)} %fusion.2), channel_id=1, source_target_pairs={{0,4},{4,0},{8,12},{12,8},{16,20},{20,16},{24,28},{28,24},{1,5},{5... | collective-permute-start | bytes 1769480 | tf_op jit(solution)/shard_map/ppermute | solution.py:529
  386.6 13.6 %collective-permute-start.66 = (bf16[4,96,768]{2,1,0:T(8,128)(2,1)S(1)}, bf16[4,96,768]{2,1,0:T(8,128)(2,1)S(1)}, u32[]{:S(2)}, u32[]{:S(2)}) collective-permute-start(bf16[4,96,768]{2,1,0:T(8,128)(2,1)S(1)} %fusion.4), channel_id=1, source_target_pairs={{0,2},{1,3},{2,0},{3,1},{4,6},{5,7},{6,4},{7,5},{8,10},{9,11},{10,... | collective-permute-start | bytes 1769480 | tf_op jit(solution)/shard_map/ppermute | solution.py:524
  395.8 14.3 %collective-permute-start.74 = (bf16[96,768]{1,0:T(8,128)(2,1)S(1)}, bf16[96,768]{1,0:T(8,128)(2,1)S(1)}, u32[]{:S(2)}, u32[]{:S(2)}) collective-permute-start(bf16[96,768]{1,0:T(8,128)(2,1)S(1)} %get-tuple-element.150), channel_id=1, source_target_pairs={{0,16},{4,20},{8,24},{12,28},{16,0},{20,4},{24,8},{28,12},{1,17},{... | collective-permute-start | bytes 442376 | tf_op jit(solution)/shard_map/ppermute | solution.py:541
  396.7 13.5 %collective-permute-start.75 = (bf16[96,768]{1,0:T(8,128)(2,1)S(1)}, bf16[96,768]{1,0:T(8,128)(2,1)S(1)}, u32[]{:S(2)}, u32[]{:S(2)}) collective-permute-start(bf16[96,768]{1,0:T(8,128)(2,1)S(1)} %get-tuple-element.149), channel_id=1, source_target_pairs={{0,24},{4,28},{8,0},{12,4},{16,8},{20,12},{24,16},{28,20},{1,25},{... | collective-permute-start | bytes 442376 | tf_op jit(solution)/shard_map/ppermute | solution.py:541
  400.5 10.4 %collective-permute-start.67 = (bf16[96,768]{1,0:T(8,128)(2,1)S(1)}, bf16[96,768]{1,0:T(8,128)(2,1)S(1)}, u32[]{:S(2)}, u32[]{:S(2)}) collective-permute-start(bf16[96,768]{1,0:T(8,128)(2,1)S(1)} %get-tuple-element.151), channel_id=1, source_target_pairs={{0,8},{4,12},{8,16},{12,20},{16,24},{20,28},{24,0},{28,4},{1,9},{5... | collective-permute-start | bytes 442376 | tf_op jit(solution)/shard_map/ppermute | solution.py:541
  400.6 17.7 %collective-permute-start.68 = (bf16[96,768]{1,0:T(8,128)(2,1)S(1)}, bf16[96,768]{1,0:T(8,128)(2,1)S(1)}, u32[]{:S(2)}, u32[]{:S(2)}) collective-permute-start(bf16[96,768]{1,0:T(8,128)(2,1)S(1)} %get-tuple-element.153), channel_id=1, source_target_pairs={{0,16},{4,20},{8,24},{12,28},{16,0},{20,4},{24,8},{28,12},{1,17},{... | collective-permute-start | bytes 442376 | tf_op jit(solution)/shard_map/ppermute | solution.py:541
  401.6 16.7 %collective-permute-start.69 = (bf16[96,768]{1,0:T(8,128)(2,1)S(1)}, bf16[96,768]{1,0:T(8,128)(2,1)S(1)}, u32[]{:S(2)}, u32[]{:S(2)}) collective-permute-start(bf16[96,768]{1,0:T(8,128)(2,1)S(1)} %get-tuple-element.152), channel_id=1, source_target_pairs={{0,24},{4,28},{8,0},{12,4},{16,8},{20,12},{24,16},{28,20},{1,25},{... | collective-permute-start | bytes 442376 | tf_op jit(solution)/shard_map/ppermute | solution.py:541
  (95 other events, 817.9 us)

commit v2 on v1

v2 whole, which is shorter than its diff:
```python
import functools

import jax
import jax.experimental.pallas as pl
import jax.experimental.pallas.tpu as pltpu
import jax.numpy as jnp
from jax import lax
from jax.sharding import PartitionSpec as P

HD = 64
EPSILON = 1e-06
MASKED = -1e30
MASK_ROWS = 16
VECTORS = 16
BIAS_COLUMN = 6
SQRT_HALF = 0.7071067811865476
INV_SQRT_2PI = 0.3989422804014327
VMEM_BYTES = 60 * 2**20
bf16 = jnp.bfloat16
f32 = jnp.float32
VMEM = pl.BlockSpec(memory_space=pltpu.VMEM)
SMEM = pl.BlockSpec(memory_space=pltpu.SMEM)
ANY = pl.BlockSpec(memory_space=pl.ANY)
FAR, MATE = 2, 1
RELATIVE = (0, FAR, MATE, FAR | MATE)


def mm(left, right, left_dim=1, right_dim=0):
    return lax.dot_general(
        left, right, (((left_dim,), (right_dim,)), ((), ())), preferred_element_type=f32
    )


def kernel_call(body, operands, specs, outs, out_specs, scratch=(), ties=()):
    first, last = len(operands), len(operands) + len(ties)

    def run(*refs):
        body(*refs[:first], *refs[last:])

    return pl.pallas_call(
        run,
        out_shape=outs,
        in_specs=[*specs, *[ANY] * len(ties)],
        out_specs=out_specs,
        scratch_shapes=list(scratch),
        compiler_params=pltpu.CompilerParams(vmem_limit_bytes=VMEM_BYTES),
    )(*operands, *ties)


def gate(values, ties):
    count = len(values)
    return pl.pallas_call(
        lambda *refs: None,
        out_shape=tuple(jax.ShapeDtypeStruct(v.shape, v.dtype) for v in values),
        in_specs=[ANY] * (count + len(ties)),
        out_specs=(ANY,) * count,
        input_output_aliases={i: i for i in range(count)},
    )(*values, *ties)


def copy_body(source, dest):
    dest[...] = source[...]


def pack_body(left, right, dest):
    width = left.shape[1]
    end = width + right.shape[1]
    dest[:, :width] = left[...]
    dest[:, width:end] = right[...]
    if end < dest.shape[1]:
        dest[:, end:] = jnp.zeros((dest.shape[0], dest.shape[1] - end), dest.dtype)


def pack_first_body(qkv, qkv_bias, out_bias, up_bias, down_bias, gain, shift, dest):
    height, group = qkv.shape[1], qkv.shape[2]
    rows = [qkv_bias[...], out_bias[...], down_bias[...], gain[...], shift[...]]
    rows = jnp.concatenate([r.astype(f32) for r in rows] + [jnp.zeros((8, height), f32)], 0).T
    count = up_bias.shape[1]
    unit = lax.broadcasted_iota(jnp.int32, (height, count), 1) - 4 * lax.broadcasted_iota(jnp.int32, (height, count), 0)
    lane = lax.broadcasted_iota(jnp.int32, rows.shape, 1)
    wide_bias = jnp.concatenate([up_bias[...]] * 8, 0)
    for j in range(4):
        picked = mm(jnp.where(unit == j, 1.0, 0.0).astype(bf16), wide_bias, 1, 1)
        rows = jnp.where(lane == 8 + j, picked[:, :1], rows)
    spare = jnp.zeros((height, dest.shape[1] - 3 * group - rows.shape[1]), bf16)
    dest[...] = jnp.concatenate([qkv[0], qkv[1], qkv[2], rows.astype(bf16), spare], 1)


def staged(body, values, shape, ties):
    return kernel_call(
        body, values, [VMEM] * len(values), jax.ShapeDtypeStruct(shape, values[0].dtype), VMEM, (), ties
    )


def project_body(slots, count, with_vectors, offs, *refs):
    n_y, n_z = slots
    blocks, rows, refs = refs[:count], refs[count : count + 4], refs[count + 4 :]
    qkv, wq = refs[:2]
    if with_vectors:
        vectors, full, shift = refs[2:]
    else:
        full, shift = refs[2:]
    model = full.shape[0]
    width, share = qkv.shape[0], rows[0].shape[0]
    group = width // 3
    height = model // (n_y * n_z)
    place = 0
    if not with_vectors:
        full, blocks = blocks[0], ()
    for block in blocks:
        for i in range(block.shape[0] if len(block.shape) == 3 else 1):
            start = pl.multiple_of(offs[place], 16)
            full[pl.ds(start, height), :] = block[i] if len(block.shape) == 3 else block[...]
            place += 1
    turned = full[...].T
    wq[...] = turned[:width]
    if with_vectors:
        vectors[...] = turned[width : width + VECTORS]
    own = full[pl.ds(pl.multiple_of(offs[n_y * n_z], 16), group), width : width + 2].astype(f32)
    shift[...] = jnp.zeros_like(shift)
    shift[:group, :] = own[:, 0:1]
    shift[2 * group :, :] = own[:, 1:2]
    for i in range(4):
        got = mm(wq[...], rows[i][...], 1, 1) + shift[...]
        qkv[:, i * share : (i + 1) * share] = got.astype(bf16)


def project(offs, slots, blocks, rows, width, with_vectors, ties):
    model = rows[0].shape[1]
    like = jax.ShapeDtypeStruct
    outs = [like((width, 4 * rows[0].shape[0]), bf16), like((width, model), bf16)]
    if with_vectors:
        outs += [like((VECTORS, model), bf16), like((model, blocks[0].shape[-1]), bf16)]
    operands = (offs, *blocks, *rows)
    return kernel_call(
        functools.partial(project_body, slots, len(blocks), with_vectors),
        operands,
        [SMEM] + [VMEM] * (len(operands) - 1),
        tuple(outs),
        (VMEM,) * len(outs),
        [pltpu.VMEM((width, 1), f32)] if with_vectors else [pltpu.VMEM((16, 128), bf16), pltpu.VMEM((width, 1), f32)],
        ties,
    )


def attend_body(heads, q_block, qkv, qmask, kmask, near, far, lse, ks, qs):
    rows = qkv.shape[1]
    group = heads * HD
    half = rows // 2
    scale = HD**-0.5

    def head(h, carry):
        top = pl.multiple_of(h * HD, HD)
        ks[...] = jnp.concatenate([qkv[pl.ds(group + top, HD), :], kmask[...]], 0).T
        qs[...] = jnp.concatenate([qkv[pl.ds(top, HD), :] * scale, qmask[...]], 0)
        values = qkv[pl.ds(2 * group + top, HD), :]
        for b in range(rows // q_block):
            at = slice(b * q_block, (b + 1) * q_block)
            scores = mm(ks[...], qs[:, at])
            most = jnp.max(scores, axis=0, keepdims=True)
            weights = jnp.exp(scores - most)
            total = jnp.sum(weights, axis=0, keepdims=True)
            blended = (mm(values, weights.astype(bf16)) / total).astype(bf16)
            cut = min(max(half - b * q_block, 0), q_block)
            if cut:
                near[pl.ds(top, HD), b * q_block : b * q_block + cut] = blended[:, :cut]
            if cut < q_block:
                start = b * q_block + cut - half
                far[pl.ds(top, HD), start : start + q_block - cut] = blended[:, cut:]
            lse[pl.ds(h, 1), at] = most + jnp.log(total)
        return carry

    lax.fori_loop(0, heads, head, 0)


def attend(qkv, qmask, kmask, ties):
    group, rows = qkv.shape[0] // 3, qkv.shape[1]
    half = jax.ShapeDtypeStruct((group, rows // 2), bf16)
    depth = HD + MASK_ROWS
    return kernel_call(
        functools.partial(attend_body, group // HD, rows // 3),
        (qkv, qmask, kmask),
        [VMEM] * 3,
        (half, half, jax.ShapeDtypeStruct((8, rows), f32)),
        (VMEM,) * 3,
        [pltpu.VMEM((rows, depth), bf16), pltpu.VMEM((depth, rows), bf16)],
        ties,
    )


def attend_back_heads(heads, q_block, k_block, refs, scratch):
    qkv, near, far, d_near, d_far, lse, qmask, kmask, d_qkv = refs
    ks, qs, vs, qn, dt, dn, dks, dvs = scratch
    rows = qkv.shape[1]
    group = heads * HD
    scale = HD**-0.5

    def head(h, carry):
        top = pl.multiple_of(h * HD, HD)
        keys = qkv[pl.ds(group + top, HD), :]
        ks[...] = jnp.concatenate([keys, kmask[...]], 0).T
        queries = qkv[pl.ds(top, HD), :]
        qs[...] = jnp.concatenate([queries * scale, qmask[...]], 0)
        qn[...] = queries.T
        vs[...] = qkv[pl.ds(2 * group + top, HD), :].T
        outer = jnp.concatenate([d_near[pl.ds(top, HD), :], d_far[pl.ds(top, HD), :]], 1)
        blended = jnp.concatenate([near[pl.ds(top, HD), :], far[pl.ds(top, HD), :]], 1)
        dt[...] = outer
        dn[...] = outer.T
        inner = jnp.sum(outer.astype(f32) * blended.astype(f32), axis=0, keepdims=True)
        log_sum = lse[pl.ds(h, 1), :]
        for b in range(rows // q_block):
            at = slice(b * q_block, (b + 1) * q_block)
            d_queries = None
            for k in range(rows // k_block):
                ka = slice(k * k_block, (k + 1) * k_block)
                probs = jnp.exp(mm(ks[ka, :], qs[:, at]) - log_sum[:, at])
                d_probs = mm(vs[ka, :], dt[:, at])
                d_scores = (probs * (d_probs - inner[:, at])).astype(bf16)
                d_values = mm(probs.astype(bf16), dn[at, :])
                d_keys = mm(d_scores, qn[at, :])
                if b == 0:
                    dvs[ka, :] = d_values
                    dks[ka, :] = d_keys
                else:
                    dvs[ka, :] += d_values
                    dks[ka, :] += d_keys
                part = mm(keys[:, ka], d_scores)
                d_queries = part if d_queries is None else d_queries + part
            d_qkv[pl.ds(top, HD), at] = (d_queries * scale).astype(bf16)
        d_qkv[pl.ds(group + top, HD), :] = (dks[...] * scale).astype(bf16).T
        d_qkv[pl.ds(2 * group + top, HD), :] = dvs[...].astype(bf16).T
        return carry

    lax.fori_loop(0, heads, head, 0)


def attend_back_body(where, own, n_blocks, offs, *refs):
    qkv, near, away, d_near, d_pair, lse, qmask, kmask = refs[:8]
    rows_of, g_out, got_out, refs = refs[8:12], refs[12], refs[13], refs[14:]
    if own:
        bias_far, refs = refs[0], refs[1:]
    (keep, send, d_qkv), refs = refs[:3], refs[3:]
    if own:
        bias_s, refs = refs[0], refs[1:]
    else:
        d_bias, refs = refs[0], refs[1:]
    (turned, full), scratch = refs[:2], refs[2:]
    rows = qkv.shape[1]
    width = qkv.shape[0]
    group = width // 3
    attend_back_heads(
        group // HD,
        rows // 2,
        rows // 3,
        (qkv, near, away, d_near, d_pair.at[where], lse, qmask, kmask, d_qkv),
        scratch,
    )
    share = rows // 4
    total = None
    for i in range(4):
        part = mm(d_qkv[:, i * share : (i + 1) * share], rows_of[i][...])
        total = part if total is None else total + part
    turned[:width, :] = total.astype(bf16)
    turned[width:, :] = (g_out[...].astype(f32) + got_out[where].astype(f32)).astype(bf16)
    full[...] = turned[...].T
    lane = lax.broadcasted_iota(jnp.int32, (group, 128), 1)
    bias = jnp.zeros((group, 128), f32)
    for j, column in ((0, BIAS_COLUMN), (2, BIAS_COLUMN + 1)):
        total = jnp.sum(d_qkv[j * group : (j + 1) * group, :].astype(f32), axis=1, keepdims=True)
        bias += jnp.where(lane == column, total, 0.0)
    if own:
        bias_s[...] = jnp.zeros_like(bias_s)
        for start, value in ((offs[n_blocks], bias), (offs[n_blocks + 1], bias_far[...])):
            bias_s[pl.ds(pl.multiple_of(start, 16), group), :] += value
    else:
        d_bias[...] = bias
    places, height = keep.shape[0], keep.shape[1]
    model = full.shape[1]
    for i, dest in enumerate((keep, send)):
        if dest.shape[1] < height:
            continue
        for z in range(places):
            at = pl.ds(pl.multiple_of(offs[i * places + z], 16), height)
            dest[z, :, :model] = full[at, :]
            if own:
                dest[z, :, model:] = bias_s[at, :].astype(bf16)


def attend_back(offs, slots, where, saved, toks, outs_of, bias_far, ties):
    qkv = saved[0]
    width, rows = qkv.shape
    model = toks[0].shape[1]
    depth = HD + MASK_ROWS
    n_y, n_z = slots
    height = model // (n_y * n_z)
    lanes = model + (128 if bias_far else 0)
    like = jax.ShapeDtypeStruct
    outs = [
        like((n_z, height, lanes), bf16),
        like((n_z, height if n_y == 2 else 8, lanes), bf16),
        like((width, rows), bf16),
    ]
    scratch = []
    if bias_far:
        scratch.append(pltpu.VMEM((model, 128), f32))
    else:
        outs.append(like((width // 3, 128), f32))
    scratch += [
        pltpu.VMEM((model, model), bf16),
        pltpu.VMEM((model, model), bf16),
        pltpu.VMEM((rows, depth), bf16),
        pltpu.VMEM((depth, rows), bf16),
        pltpu.VMEM((rows, HD), bf16),
        pltpu.VMEM((rows, HD), bf16),
        pltpu.VMEM((HD, rows), bf16),
        pltpu.VMEM((rows, HD), bf16),
        pltpu.VMEM((rows, HD), f32),
        pltpu.VMEM((rows, HD), f32),
    ]
    operands = (offs, *saved, *toks, *outs_of, *bias_far)
    return kernel_call(
        functools.partial(attend_back_body, where, bool(bias_far), n_y * n_z),
        operands,
        [SMEM] + [VMEM] * (len(operands) - 1),
        tuple(outs),
        (VMEM,) * len(outs),
        scratch,
        ties,
    )


def rows_back_body(d_qkv, d_qkv_far, wq, wq_far, d_resid, d_own, d_mate):
    share = d_resid.shape[0] // 2
    for i in range(4):
        at = slice(i * share, (i + 1) * share)
        part = mm(d_qkv[:, at], wq[...], 0, 0) + mm(d_qkv_far[:, at], wq_far[...], 0, 0)
        if i < 2:
            d_own[at, :] = part + d_resid[at, :]
        else:
            d_mate[(i - 2) * share : (i - 1) * share, :] = part.astype(bf16)


def rows_back(d_qkv, d_qkv_far, wq, wq_far, d_resid, ties):
    outs = (jax.ShapeDtypeStruct(d_resid.shape, f32), jax.ShapeDtypeStruct(d_resid.shape, bf16))
    operands = (d_qkv, d_qkv_far, wq, wq_far, d_resid)
    return kernel_call(rows_back_body, operands, [VMEM] * 5, outs, (VMEM,) * 2, (), ties)


def normed(value):
    center = value - jnp.mean(value, axis=1, keepdims=True)
    rstd = lax.rsqrt(jnp.mean(center * center, axis=1, keepdims=True) + EPSILON)
    return center * rstd, rstd


def normed_back(grad, xhat, rstd, gain):
    scaled = grad * gain
    mean = jnp.mean(scaled, axis=1, keepdims=True)
    along = jnp.mean(scaled * xhat, axis=1, keepdims=True)
    return rstd * (scaled - mean - xhat * along)


def add_row(dest, row, value, first):
    part = jnp.sum(value, axis=0, keepdims=True)
    if first:
        dest[row : row + 1, :] = part
    else:
        dest[row : row + 1, :] += part


def fetch(offs, slots, block, dest, height, sems, index):
    n_y, n_z = slots
    copies = []
    for y in range(n_y):
        for z in range(n_z):
            start = pl.multiple_of(offs[y * n_z + z], 16)
            copy = pltpu.make_async_copy(
                block(y, z), dest.at[pl.ds(start, height), :], sems.at[index]
            )
            copy.start()
            copies.append(copy)
            index += 1
    return copies, index


def block_of(blocks, n_y, t, lanes):
    return lambda y, z: blocks[t * n_y + y].at[z, :, lanes]


def pair_block(blocks, lanes):
    return lambda y, z: blocks.at[z, :, pl.ds(lanes.start + y * lanes.size, lanes.size)]


class Outbox:
    def __init__(self, offs, slots, height, sems):
        self.offs, self.slots, self.height, self.sems = offs, slots, height, sems
        self.index, self.flying = 0, {}

    def send(self, stage, slot, dest, place):
        n_y, n_z = self.slots
        for y in range(n_y):
            for z in range(n_z):
                start = pl.multiple_of(self.offs[y * n_z + z], 16)
                copy = pltpu.make_async_copy(
                    stage.at[slot, pl.ds(start, self.height), :],
                    dest.at[y, z, place],
                    self.sems.at[self.index],
                )
                copy.start()
                self.flying.setdefault(slot, []).append(copy)
                self.index += 1

    def settle(self, slot):
        for copy in self.flying.pop(slot, []):
            copy.wait()


def enter_body(slots, offs, *refs):
    n_y, n_z = slots
    toks, near, away, refs = refs[:2], refs[2:4], refs[4:6], refs[6:]
    vec_in, refs = refs[0], refs[1:]
    ups, downs, outs_in, refs = refs[: 2 * n_y], refs[2 * n_y : 4 * n_y], refs[4 * n_y : 4 * n_y + 2], refs[4 * n_y + 2 :]
    (xhat_s, rstd_s, low_s, acc_s, act, slope, att_s, out_s), refs = refs[:8], refs[8:]
    up_s, down_s, turned, in_sem = refs
    model, ffn = up_s.shape[1], up_s.shape[2]
    rows, share, group = acc_s.shape[0], toks[0].shape[0], near[0].shape[0]
    height = model // (n_y * n_z)
    chunks = [(i, slice(i * share, (i + 1) * share)) for i in range(rows // share)]
    pending, index = {}, 0
    for t in range(4):
        lanes = pl.ds(ffn, out_s.shape[2])
        block = block_of(ups, n_y, t // 2, lanes) if t % 2 == 0 else pair_block(outs_in[t // 2], lanes)
        pending[t, "out"], index = fetch(offs, slots, block, out_s.at[t], height, in_sem, index)
    lanes = pl.ds(0, ffn)
    for t in range(2):
        pending[t, "up"], index = fetch(offs, slots, block_of(ups, n_y, t, lanes), up_s.at[t], height, in_sem, index)
        pending[t, "down"], index = fetch(
            offs, slots, block_of(downs, n_y, t, lanes), down_s.at[t], height, in_sem, index
        )
    for i in range(2):
        att_s[i * group : (i + 1) * group, :] = near[i][...]
        att_s[(2 + i) * group : (3 + i) * group, :] = away[i][...]
    vectors = vec_in[...].astype(f32)
    out_bias, down_bias = vectors[2:3, :], vectors[3:4, :]
    gain_1, shift_1 = vectors[4:5, :], vectors[6:7, :]
    for t in range(4):
        for copy in pending[t, "out"]:
            copy.wait()
    for i, at in chunks:
        resid = toks[i][...].astype(f32) + out_bias
        for t in range(4):
            own = slice(t * group, (t + 1) * group)
            resid += mm(att_s[own, at], out_s[t, :, :group], 0, 1)
        xhat, rstd = normed(resid)
        value = xhat * gain_1 + shift_1
        xhat_s[at, :] = xhat
        rstd_s[at, :] = rstd
        low_s[at, :] = value.astype(bf16)
        acc_s[at, :] = value + down_bias
    first = n_y * n_z + 2
    starts = (offs[first], offs[first + 2])
    hidden_groups(low_s, up_s, down_s, vec_in, starts, turned, chunks, act, slope, acc_s, pending)


def hidden_groups(low_s, up_s, down_s, vec_in, starts, turned, chunks, act, slope, acc_s, pending):
    turned[...] = vec_in[...].astype(f32).T
    span, ffn = turned.shape[0] // 4, up_s.shape[2]
    unit = lax.broadcasted_iota(jnp.int32, (span, ffn), 1) - 4 * lax.broadcasted_iota(jnp.int32, (span, ffn), 0)
    for t in range(2):
        for copy in pending[t, "up"] + pending[t, "down"]:
            copy.wait()
        columns = turned[pl.ds(pl.multiple_of(starts[t], 16), span), :].astype(bf16)
        bias = None
        for j in range(4):
            part = mm(columns, jnp.where(unit == j, 1.0, 0.0).astype(bf16), 0, 0)[8 + j : 9 + j, :]
            bias = part if bias is None else bias + part
        for i, at in chunks:
            hidden = mm(low_s[at, :], up_s[t]) + bias
            phi = 0.5 + 0.5 * lax.erf(hidden * SQRT_HALF)
            density = jnp.exp(-0.5 * hidden * hidden) * INV_SQRT_2PI
            active = (hidden * phi).astype(bf16)
            act[t, at, :] = active
            slope[t, at, :] = (phi + hidden * density).astype(bf16)
            acc_s[at, :] += mm(active, down_s[t], 1, 1)


def enter(offs, slots, ffn, toks, near, away, vectors, ups, downs, outs_in, ties):
    n_y, n_z = slots
    share, model = toks[0].shape
    rows, group = 2 * share, near[0].shape[0]
    like = jax.ShapeDtypeStruct
    outs = (
        like((rows, model), f32),
        like((rows, 1), f32),
        like((rows, model), bf16),
        like((rows, model), f32),
        like((2, rows, ffn), bf16),
        like((2, rows, ffn), bf16),
        like((4 * group, rows), bf16),
        like((4, model, ups[0].shape[-1] - ffn), bf16),
    )
    operands = (offs, *toks, *near, *away, vectors, *ups, *downs, *outs_in)
    n_blocks = len(ups) + len(downs) + len(outs_in)
    specs = [SMEM] + [VMEM] * (len(operands) - 1 - n_blocks) + [ANY] * n_blocks
    scratch = [
        pltpu.VMEM((2, model, ffn), bf16),
        pltpu.VMEM((2, model, ffn), bf16),
        pltpu.VMEM((model, VECTORS), f32),
        pltpu.SemaphoreType.DMA((8 * n_y * n_z,)),
    ]
    return kernel_call(
        functools.partial(enter_body, slots), operands, specs, outs, (VMEM,) * len(outs), scratch, ties
    )


def forward_body(slots, offs, *refs):
    n_y, n_z = slots
    (low_s, acc, act_before), refs = refs[:3], refs[3:]
    (vec_in, valid, cot_own, cot_far), refs = refs[:4], refs[4:]
    ups, downs, projs, refs = refs[: 2 * n_y], refs[2 * n_y : 4 * n_y], refs[4 * n_y : 5 * n_y], refs[5 * n_y :]
    (emb_own, emb_far, branch_s, acc_s, slope, g_keep, g_mate, g_proj, g_vec), refs = refs[:9], refs[9:]
    up_s, down_s, proj_s, act_s, stage, turned, in_sem, out_sem = refs
    model, ffn = up_s.shape[1], up_s.shape[2]
    rows, share = acc_s.shape[0], cot_own.shape[0]
    height = model // (n_y * n_z)
    chunks = [(i, slice(i * share, (i + 1) * share)) for i in range(rows // share)]
    pending, index = {}, 0
    lanes = pl.ds(0, ffn)
    for t in range(2):
        pending[t, "up"], index = fetch(offs, slots, block_of(ups, n_y, t, lanes), up_s.at[t], height, in_sem, index)
        pending[t, "down"], index = fetch(
            offs, slots, block_of(downs, n_y, t, lanes), down_s.at[t], height, in_sem, index
        )
    lanes = pl.ds(ffn, proj_s.shape[1])
    pending["proj"], index = fetch(offs, slots, block_of(projs, n_y, 0, lanes), proj_s, height, in_sem, index)
    vectors = vec_in[...].astype(f32)
    gain_2, shift_2 = vectors[5:6, :], vectors[7:8, :]
    acc_s[...] = acc[...]
    first = n_y * n_z + 2
    starts = (offs[first + 1], offs[first + 3])
    hidden_groups(low_s, up_s, down_s, vec_in, starts, turned, chunks, act_s, slope, acc_s, pending)
    for copy in pending["proj"]:
        copy.wait()
    for i, at in chunks:
        xhat, rstd = normed(acc_s[at, :])
        low = (xhat * gain_2 + shift_2).astype(bf16)
        embed = mm(low, proj_s[...])
        unit = lax.rsqrt(jnp.sum(embed * embed, axis=1, keepdims=True) + EPSILON)
        kept = valid[at, :].astype(f32)
        (emb_own, emb_far)[i][...] = (kept * embed * unit).astype(bf16)
        cot = (cot_own, cot_far)[i][...].astype(f32)
        along = jnp.sum(cot * embed, axis=1, keepdims=True)
        d_embed = (kept * (unit * cot - unit * unit * unit * embed * along)).astype(bf16)
        part = mm(low, d_embed, 0, 0)
        if i == 0:
            g_proj[...] = part
        else:
            g_proj[...] += part
        d_normed = mm(d_embed, proj_s[...], 1, 1)
        add_row(g_vec, 1, d_normed * xhat, i == 0)
        add_row(g_vec, 3, d_normed, i == 0)
        d_value = normed_back(d_normed, xhat, rstd, gain_2)
        add_row(g_vec, 5, d_value, i == 0)
        branch_s[at, :] = d_value.astype(bf16)
        acc_s[at, :] = d_value
    box = Outbox(offs, slots, height, out_sem)
    for turn, t in enumerate((2, 3, 0, 1)):
        slot = turn % 2
        active = act_before if t % 2 == 0 else act_s
        box.settle(slot)
        stage[slot] = mm(branch_s[...], active[t // 2], 0, 0).astype(bf16)
        box.send(stage, slot, g_keep if t < 2 else g_mate, t % 2)
    box.settle(0)
    box.settle(1)


def forward(offs, slots, state, vectors, valid, cots, ups, downs, projs, ties):
    n_y, n_z = slots
    rows, model = state[0].shape
    share, emb = cots[0].shape
    ffn = state[2].shape[2]
    height = model // (n_y * n_z)
    like = jax.ShapeDtypeStruct
    outs = (
        like((share, emb), bf16),
        like((share, emb), bf16),
        like((rows, model), bf16),
        like((rows, model), f32),
        like((2, rows, ffn), bf16),
        like((n_y, n_z, 2, height, ffn), bf16),
        like((n_y, n_z, 2, height, ffn), bf16),
        like((model, emb), f32),
        like((8, model), f32),
    )
    out_specs = (*[VMEM] * 5, ANY, ANY, VMEM, VMEM)
    operands = (offs, *state, vectors, valid, *cots, *ups, *downs, *projs)
    n_blocks = len(ups) + len(downs) + len(projs)
    specs = [SMEM] + [VMEM] * (len(operands) - 1 - n_blocks) + [ANY] * n_blocks
    scratch = [
        pltpu.VMEM((2, model, ffn), bf16),
        pltpu.VMEM((2, model, ffn), bf16),
        pltpu.VMEM((model, emb), bf16),
        pltpu.VMEM((2, rows, ffn), bf16),
        pltpu.VMEM((2, model, ffn), bf16),
        pltpu.VMEM((model, VECTORS), f32),
        pltpu.SemaphoreType.DMA((5 * n_y * n_z,)),
        pltpu.SemaphoreType.DMA((4 * n_y * n_z,)),
    ]
    return kernel_call(
        functools.partial(forward_body, slots), operands, specs, outs, out_specs, scratch, ties
    )


def backward_body(last, slots, offs, *refs):
    n_y, n_z = slots
    (branch, low, slope_a, slope_b, acc), refs = refs[:5], refs[5:]
    slopes = (slope_a, slope_b)
    if last:
        (xhat_s, rstd_s, att_s, out_s, vec_in, vec_before, bias_before, g_proj), refs = refs[:8], refs[8:]
    ups, downs, refs = refs[: 2 * n_y], refs[2 * n_y : 4 * n_y], refs[4 * n_y :]
    g_up, refs = refs[0], refs[1:]
    if last:
        (d_resid, d_near, d_near_far, d_pair, g_out, g_out_far, g_out_pair, small), refs = refs[:8], refs[8:]
    else:
        (acc_out, g_bias), refs = refs[:2], refs[2:]
    up_s, down_s, hid_s, acc_s, stage, in_sem, out_sem = refs[:7]
    if last:
        branch_s, g_bias, g_vec, small_s = refs[7:]
    model, ffn = up_s.shape[1], up_s.shape[2]
    rows = acc.shape[0]
    share = rows // 2
    height = model // (n_y * n_z)
    chunks = [(i, slice(i * share, (i + 1) * share)) for i in range(2)]
    pending, index = {}, 0
    lanes = pl.ds(0, ffn)
    for t in range(2):
        pending[t, "down"], index = fetch(
            offs, slots, block_of(downs, n_y, t, lanes), down_s.at[t], height, in_sem, index
        )
        pending[t, "up"], index = fetch(offs, slots, block_of(ups, n_y, t, lanes), up_s.at[t], height, in_sem, index)
    box = Outbox(offs, slots, height, out_sem)
    g_bias[...] = jnp.zeros_like(g_bias)
    for t in range(2):
        for copy in pending[t, "down"] + pending[t, "up"]:
            copy.wait()
        slope = slopes[t]
        for i, at in chunks:
            d_active = mm(branch[at, :], down_s[t])
            d_hidden = (d_active * slope[1 if not last else 0, at, :].astype(f32)).astype(bf16)
            hid_s[at, :] = d_hidden
            add_row(g_bias, t, d_hidden.astype(f32), i == 0)
            part = mm(d_hidden, up_s[t], 1, 1)
            if t == 0:
                acc_s[at, :] = acc[at, :] + part
            else:
                total = acc_s[at, :] + part
                if last:
                    acc_s[at, :] = total
                else:
                    acc_out[at, :] = total
        stage[t] = mm(low[...], hid_s[...], 0, 0).astype(bf16)
        box.send(stage, t, g_up, t)
    if last:
        group = d_near.shape[0]
        gain_1 = vec_in[...].astype(f32)[4:5, :]
        g_vec[...] = jnp.zeros_like(g_vec)
        g_vec[:8, :] = vec_before[...]
        for i, at in chunks:
            grad = acc_s[at, :]
            xhat = xhat_s[at, :]
            add_row(g_vec, 0, grad * xhat, i == 0)
            add_row(g_vec, 2, grad, i == 0)
            d_value = normed_back(grad, xhat, rstd_s[at, :], gain_1)
            add_row(g_vec, 4, d_value, i == 0)
            d_resid[at, :] = d_value
            branch_s[at, :] = d_value.astype(bf16)
        for i in range(4):
            own = slice(i * group, (i + 1) * group)
            got = mm(out_s[i, :, :group], branch_s[...], 0, 1).astype(bf16)
            grad = mm(att_s[own, :], branch_s[...]).astype(bf16)
            if i < 2:
                (d_near, d_near_far)[i][...] = got
                (g_out, g_out_far)[i][...] = grad
            else:
                d_pair[i - 2] = got
                g_out_pair[i - 2] = grad
        emb = g_proj.shape[1]
        small_s[:, :emb] = g_proj[...]
        small_s[:, emb:] = g_vec[...].T
        biases = jnp.concatenate([g_bias[:2, :], bias_before[:2, :], jnp.zeros((4, ffn), f32)], 0).astype(bf16)
        span = ffn // 4
        lane = lax.broadcasted_iota(jnp.int32, (span, emb), 1)
        unit = lax.broadcasted_iota(jnp.int32, (span, ffn), 1) - 4 * lax.broadcasted_iota(jnp.int32, (span, ffn), 0)
        for j in range(4):
            picked = mm(jnp.where(unit == j, 1.0, 0.0).astype(bf16), biases, 1, 1)
            for i in range(4):
                own = pl.ds(pl.multiple_of(offs[n_y * n_z + 2 + i], 16), span)
                small_s[own, emb:] += jnp.where(lane == 8 + j, picked[:, i : i + 1], 0.0)
        for i in range(n_y * n_z):
            own = pl.ds(pl.multiple_of(offs[i], 16), height)
            for j in range(2):
                small[i // n_z, i % n_z, j] = small_s[own, j * emb : (j + 1) * emb].astype(bf16)
    box.settle(0)
    box.settle(1)


def backward(offs, slots, state, tail, ups, downs, ties):
    n_y, n_z = slots
    rows, model = state[1].shape
    ffn = state[2].shape[2]
    height = model // (n_y * n_z)
    like = jax.ShapeDtypeStruct
    outs = [like((n_y, n_z, 2, height, ffn), bf16)]
    scratch = [
        pltpu.VMEM((2, model, ffn), bf16),
        pltpu.VMEM((2, model, ffn), bf16),
        pltpu.VMEM((rows, ffn), bf16),
        pltpu.VMEM((rows, model), f32),
        pltpu.VMEM((2, model, ffn), bf16),
        pltpu.SemaphoreType.DMA((4 * n_y * n_z,)),
        pltpu.SemaphoreType.DMA((2 * n_y * n_z,)),
    ]
    if tail:
        group = tail[2].shape[0] // 4
        emb = tail[-1].shape[1]
        outs += [
            like((rows, model), f32),
            like((group, rows), bf16),
            like((group, rows), bf16),
            like((2, group, rows), bf16),
            like((group, model), bf16),
            like((group, model), bf16),
            like((2, group, model), bf16),
            like((n_y, n_z, 2, height, emb), bf16),
        ]
        scratch += [
            pltpu.VMEM((rows, model), bf16),
            pltpu.VMEM((8, ffn), f32),
            pltpu.VMEM((emb, model), f32),
            pltpu.VMEM((model, 2 * emb), f32),
        ]
    else:
        outs += [like((rows, model), f32), like((8, ffn), f32)]
    operands = (offs, *state, *tail, *ups, *downs)
    n_blocks = len(ups) + len(downs)
    specs = [SMEM] + [VMEM] * (len(operands) - 1 - n_blocks) + [ANY] * n_blocks
    return kernel_call(
        functools.partial(backward_body, bool(tail), slots),
        operands,
        specs,
        tuple(outs),
        (ANY, *[VMEM] * (len(outs) - 1)),
        scratch,
        ties,
    )


def finish_body(place, offs, d_input, home, emb_own, input_grad, embeddings):
    own = offs[place + 6]
    other = 1 - own
    share, model = input_grad.shape[1:]
    input_grad[own] = d_input[:share, :]
    input_grad[other] = home[:, :model]
    embeddings[own] = emb_own[...]
    embeddings[other] = home[:, model:]


def finish(offs, place, d_input, home, emb_own):
    share, emb = emb_own.shape
    outs = (
        jax.ShapeDtypeStruct((2, share, d_input.shape[1]), bf16),
        jax.ShapeDtypeStruct((2, share, emb), bf16),
    )
    return kernel_call(
        functools.partial(finish_body, place),
        (offs, d_input, home, emb_own),
        [SMEM] + [VMEM] * 3,
        outs,
        (VMEM,) * 2,
    )


def swap(value, bit):
    count = lax.axis_size("tensor")
    return lax.ppermute(value, "tensor", [(i, i ^ bit) for i in range(count)])


def swap_y(value):
    count = lax.axis_size("dp")
    return lax.ppermute(value, "dp", [(i, i ^ 1) for i in range(count)])


def swap_z(value, bits):
    count = lax.axis_size("dp")
    return lax.ppermute(value, "dp", [(i, i ^ (2 * bits)) for i in range(count)])


def low(value):
    return value.astype(bf16)


def wide(value):
    return value.astype(f32)


def scatter_dp(value):
    return wide(lax.psum_scatter(low(value), "dp", scatter_dimension=0, tiled=True))


def gather_z(piece, *after):
    pair = jnp.stack([piece, swap_z(piece, 1)])
    return jnp.concatenate([pair, swap_z(pair, 2)])


def sum_z(value):
    total, narrow = value[0], low(value)
    for step in range(1, value.shape[0]):
        total = total + wide(swap_z(narrow[step], step))
    return total


def per_device(
    tokens,
    qkv_weight,
    out_weight,
    up_weight,
    down_weight,
    qkv_bias,
    out_bias,
    up_bias,
    down_bias,
    norm_gain,
    norm_shift,
    proj_weight,
    lengths,
    cotangent,
):
    n_dp = lax.axis_size("dp")
    d = lax.axis_index("dp")
    t = lax.axis_index("tensor")
    swapped = t // 2 == 1
    share, model = tokens.shape[1], tokens.shape[2]
    rows = 4 * share
    group = qkv_weight.shape[2]
    height = qkv_weight.shape[1]
    ffn = up_weight.shape[1]
    emb = proj_weight.shape[1]
    ring = n_dp == 8
    slots = (2, n_dp // 2) if ring else (1, 1)
    n_y, n_z = slots
    if ring:
        z, y = d // 2, d % 2
        at = [height * (2 * (z ^ r) + (y ^ yy)) for yy in range(2) for r in range(n_z)]
    else:
        at = [0]
    offs = jnp.stack([*at, group * t, group * (t ^ FAR), *[group * (t ^ r) for r in RELATIVE], t // 2]).astype(jnp.int32)
    offs_far = jnp.stack([*at, group * (t ^ FAR), group * t]).astype(jnp.int32)

    width = 3 * group
    lanes = -(-(width + VECTORS) // 128) * 128
    if ring:
        small_operands = (qkv_bias, out_bias[None], up_bias[None], down_bias[None], norm_gain, norm_shift)
        piece_1 = staged(pack_first_body, (qkv_weight, *small_operands), (height, lanes), ())
    else:
        vec = jnp.concatenate(
            [qkv_bias, out_bias[None], down_bias[None], norm_gain, norm_shift, up_bias.reshape(height, 4).T]
        ).T
        spare = jnp.zeros((height, lanes - width - vec.shape[1]), bf16)
        piece_1 = jnp.concatenate([qkv_weight[0], qkv_weight[1], qkv_weight[2], vec, spare], 1)
    up_lanes = -(-(ffn + group) // 128) * 128
    down_lanes = ffn + emb

    tok_own = jnp.where(swapped, tokens[1], tokens[0])
    tok_far = swap(jnp.where(swapped, tokens[0], tokens[1]), FAR)
    toks = (tok_own, tok_far, swap(tok_own, MATE), swap(tok_far, MATE))
    cot_own = jnp.where(swapped, cotangent[1], cotangent[0])
    cot_send = jnp.where(swapped, cotangent[0], cotangent[1])

    bounds = jnp.where(swapped, lengths[1, 0], lengths[0, 0])
    ends = [jnp.sum(bounds[: j + 1]) for j in range(bounds.shape[0])]
    positions = jnp.concatenate([share * (t ^ r) + lax.iota(jnp.int32, share) for r in RELATIVE])
    segment = sum((positions >= e).astype(jnp.int32) for e in ends)
    hot = segment[None] == lax.iota(jnp.int32, MASK_ROWS)[:, None]
    qmask = jnp.where(hot, 1.0, 0.0).astype(bf16)
    kmask = jnp.where(hot, 0.0, MASKED).astype(bf16)
    valid = jnp.broadcast_to((positions[: rows // 2] < ends[-1])[:, None], (rows // 2, emb)).astype(bf16)

    if ring:
        piece_up = staged(pack_body, (up_weight, out_weight.T), (height, up_lanes), (piece_1,))
        piece_down = staged(pack_body, (down_weight.T, proj_weight), (height, down_lanes), (piece_up,))
        line = jnp.stack([piece_1] + [swap_z(piece_1, step) for step in range(1, n_z)])
        pair_up = jnp.stack([piece_up, swap_z(piece_up, 1)])
        pair_down = jnp.stack([piece_down, swap_z(piece_down, 1)])
        other_up = swap_z(pair_up, 2)
        qkv, wq, vectors, whole = project(
            offs, slots, (line, swap_y(line)), toks, width, True, (pair_up, pair_down)
        )
        qkv, wq, vectors, whole, other_up, pair_down = gate((qkv, wq, vectors, whole, other_up, pair_down), ())
        other_down = swap_z(pair_down, 2)
        whole_far = swap(whole, FAR)
        up_own = jnp.concatenate([pair_up, other_up])
        up_y = swap_y(up_own)
        near, away, lse = attend(qkv, qmask, kmask, (up_own, valid))
        near, away, lse, whole_far, up_own, up_y, other_down = gate(
            (near, away, lse, whole_far, up_own, up_y, other_down), ()
        )
        up_far = swap(
            jnp.concatenate([up_own, up_y[:, :, ffn:], cot_send.reshape(n_z, height, emb)], 2), FAR
        )
        down_own = jnp.concatenate([pair_down, other_down])
        down_y = swap_y(down_own)
        qkv_far, wq_far = project(offs_far, slots, (whole_far,), toks, width, False, (near, down_own))
        near_far, away_far, lse_far = attend(qkv_far, qmask, kmask, (down_own,))
        mates = [swap(b, MATE) for b in (up_own, up_y, down_own)]
        near_far, away_far, lse_far, up_far, down_y, away, *mates = gate(
            (near_far, away_far, lse_far, up_far, down_y, away, *mates), ()
        )
        cot_far = up_far[:, :, up_far.shape[2] - emb :].reshape(share, emb)
        up_far_part = up_far[:, :, :ffn]
        ups, downs = [up_own, up_y], [down_own, down_y]
    else:
        piece_up = jnp.pad(jnp.concatenate([up_weight, out_weight.T], 1), ((0, 0), (0, up_lanes - ffn - group)))
        piece_down = jnp.concatenate([down_weight.T, proj_weight], 1)
        whole, up_own, down_own = (
            lax.all_gather(piece, "dp", axis=0, tiled=True)[None] for piece in (piece_1, piece_up, piece_down)
        )
        ups, downs = [up_own], [down_own]
        up_far, down_far = swap(up_own, FAR), swap(down_own, FAR)
        cot_far = swap(cot_send, FAR)
        qkv, wq, vectors, whole = project(offs, slots, (whole,), toks, width, True, ())
        near, away, lse = attend(qkv, qmask, kmask, ())
        qkv_far, wq_far = project(offs_far, slots, (swap(whole, FAR),), toks, width, False, ())
        near_far, away_far, lse_far = attend(qkv_far, qmask, kmask, ())
    if ring:
        ups_mate, downs_mate = mates[:2], [mates[2], swap(down_y, MATE)]
    else:
        ups_mate, downs_mate = [swap(b, MATE) for b in ups], [swap(b, MATE) for b in downs]
    up_far_mate = swap(up_far, MATE)
    outs_in = (up_far, up_far_mate)
    away_got = (swap(away, MATE), swap(away_far, MATE))
    if ring:
        up_far_part, down_own, down_y, up_far_mate, downs_mate[1], *away_got = gate(
            (up_far_part, down_own, down_y, up_far_mate, downs_mate[1], *away_got), ()
        )
        downs, outs_in = [down_own, down_y], (up_far, up_far_mate)
        up_far_y, down_far, down_far_y = swap_y(up_far_part), swap(down_own, FAR), swap(down_y, FAR)
    xhat, rstd, normed_low, acc, act, slope_1, att, out_t = enter(
        offs,
        slots,
        ffn,
        toks[:2],
        (near, near_far),
        away_got,
        vectors,
        ups + ups_mate,
        downs + downs_mate,
        outs_in,
        (),
    )
    if ring:
        xhat, rstd, normed_low, acc, act, slope_1, att, out_t, up_far_y, down_far, down_far_y = gate(
            (xhat, rstd, normed_low, acc, act, slope_1, att, out_t, up_far_y, down_far, down_far_y), ()
        )
        ups_far, downs_far = [up_far, up_far_y], [down_far, down_far_y]
    else:
        ups_far, downs_far = [up_far], [down_far]
    ups_far_mate = [up_far_mate] + [swap(b, MATE) for b in ups_far[1:]]
    downs_far_mate = [swap(b, MATE) for b in downs_far]
    emb_own, emb_far, branch, acc, slope_2, g_down_keep, g_down_mate, g_proj, g_vec = forward(
        offs,
        slots,
        (normed_low, acc, act),
        vectors,
        valid,
        (cot_own, cot_far),
        ups_far + ups_far_mate,
        downs_far + downs_far_mate,
        downs,
        (),
    )
    got_down = swap(g_down_mate, MATE)
    state = (branch, normed_low, slope_1, slope_2)
    g_up_mate, acc, g_bias_mate = backward(
        offs, slots, (*state, acc), (), ups_mate + ups_far_mate, downs_mate + downs_far_mate, ()
    )
    got_up = swap(g_up_mate, MATE)

    def both(keep, got, *at):
        return wide(keep[at]) + wide(got[at])

    ties = ()
    if ring:
        down_y_out = low(both(g_down_keep, got_down, 1))
        down_y_in = swap_y(down_y_out)
        ties = (down_y_out,)
    tail = (xhat, rstd, att, out_t, vectors, g_vec, g_bias_mate, g_proj)
    g_up_keep, d_resid, d_near, d_near_far, d_pair, g_out, g_out_far, g_out_pair, small = backward(
        offs, slots, (*state, acc), tail, ups + ups_far, downs + downs_far, ties
    )
    if ring:
        g_up_keep, d_near_far, d_pair, g_out_pair, small, got_up, down_y_in = gate(
            (g_up_keep, d_near_far, d_pair, g_out_pair, small, got_up, down_y_in), ()
        )
    d_pair = swap(d_pair, MATE)
    got_out = swap(g_out_pair, MATE)
    small_sum = wide(small) + wide(swap(small, MATE))
    if ring:
        down_sum = both(g_down_keep, got_down, 0) + wide(down_y_in)
        down_out = [low(down_sum[step]) for step in range(1, n_z)]
        down_in = [swap_z(down_out[step - 1], step) for step in range(1, n_z)]
        up_y_out = low(jnp.concatenate([both(g_up_keep, got_up, 1), small_sum[1]], 3))
        up_y_in = swap_y(up_y_out)
        ties = (up_y_out, *down_out)
    masks = (qmask, kmask)
    keep_far, send_far, d_qkv_far, bias_far = attend_back(
        offs,
        slots,
        1,
        (qkv_far, near_far, away_far, d_near_far, d_pair, lse_far, *masks),
        toks,
        (g_out_far, got_out),
        (),
        ties,
    )
    if ring:
        keep_far, send_far, bias_far, d_qkv_far, up_y_in, *down_in = gate(
            (keep_far, send_far, bias_far, d_qkv_far, up_y_in, *down_in), ()
        )
        far_y_in = swap_y(send_far)
        up_sum = jnp.concatenate([both(g_up_keep, got_up, 0), small_sum[0]], 3) + wide(up_y_in)
        up_out = [low(up_sum[step]) for step in range(1, n_z)]
        up_in = [swap_z(up_out[step - 1], step) for step in range(1, n_z)]
        down_sum = down_sum[0]
        for part in down_in:
            down_sum = down_sum + wide(part)
        down_x_out = low(down_sum[1])
        down_x_in = swap(down_x_out, FAR)
        ties = (*up_out, down_x_out, d_qkv_far)
    keep, send, d_qkv = attend_back(
        offs, slots, 0, (qkv, near, away, d_near, d_pair, lse, *masks), toks, (g_out, got_out), (bias_far,), ties
    )
    if ring:
        keep, send, d_qkv, far_y_in, down_x_in, *up_in = gate((keep, send, d_qkv, far_y_in, down_x_in, *up_in), ())
        own_y_in = swap_y(send)
        far_x_out = low(wide(keep_far) + wide(far_y_in))
        far_x_in = swap(far_x_out, FAR)
        ties = (far_x_out,)
    d_own, d_mate = rows_back(d_qkv, d_qkv_far, wq, wq_far, d_resid, ties)
    if ring:
        d_own, d_mate, far_x_in, own_y_in, *up_in = gate((d_own, d_mate, far_x_in, own_y_in, *up_in), ())
        up_sum = up_sum[0]
        for part in up_in:
            up_sum = up_sum + wide(part)
        up_x_out = low(jnp.concatenate([up_sum[1, :, :ffn], up_sum[0, :, ffn:], up_sum[1, :, ffn:]], 1))
    d_input = low(d_own + wide(swap(d_mate, MATE)))
    home = jnp.concatenate([d_input[share:], emb_far], 1)
    if ring:
        home, keep, own_y_in, up_x_out = gate((home, keep, own_y_in, up_x_out), ())
        home = swap(home, FAR)
        far_x_in = jnp.pad(wide(far_x_in), ((0, 0), (0, 0), (0, keep.shape[2] - model)))
        grad_1 = wide(keep) + wide(own_y_in) + far_x_in
        low_1 = low(grad_1)
        parts = [swap_z(low_1[step], step) for step in range(1, n_z)]
        up_x_in = swap(up_x_out, FAR)
        *parts, down_sum, down_x_in, up_sum = gate((*parts, down_sum, down_x_in, up_sum), ())
        grad_1 = grad_1[0]
        for part in parts:
            grad_1 = grad_1 + wide(part)
        ffn_total = jnp.concatenate(
            [up_sum[0, :, :ffn], down_sum[0], up_sum[0, :, ffn:], up_sum[1, :, ffn:]], 1
        ) + wide(jnp.concatenate([up_x_in[:, :ffn], down_x_in, up_x_in[:, ffn:]], 1))
        late = grad_1[:, model:]
        late = late + wide(swap(low(late), MATE))
        late = late + wide(swap(low(late), FAR))
    else:
        home = swap(home, FAR)
        got = jnp.pad(wide(swap(keep_far[0], FAR)), ((0, 0), (0, keep.shape[2] - model)))
        grad_1 = scatter_dp(wide(keep[0]) + got)
        pieces = []
        for mine, got in ((g_up_keep, got_up), (g_down_keep, got_down)):
            pieces.append(scatter_dp(both(mine, got, 0, 0, 0) + wide(swap(low(both(mine, got, 0, 0, 1)), FAR))))
        small_sum = jnp.concatenate([small_sum[0, 0, 0], small_sum[0, 0, 1]], 1)
        small_sum = small_sum + wide(swap(low(small_sum), FAR))
        ffn_total = jnp.concatenate([*pieces, scatter_dp(small_sum)], 1)
        late = lax.psum(low(grad_1[:, model:]), "tensor").astype(f32)
    grad_up, grad_down, small_grad = ffn_total[:, :ffn], ffn_total[:, ffn : 2 * ffn].T, ffn_total[:, 2 * ffn :]
    grad_qkv = jnp.stack([grad_1[:, i * group : (i + 1) * group] for i in range(3)])
    grad_out = grad_1[:, width:model].T

    input_grad, embeddings = finish(offs, n_y * n_z, d_input, home, emb_own)
    grad_proj, vec_grad = small_grad[:, :emb], small_grad[:, emb : emb + VECTORS].T
    grad_up_bias = small_grad[:, emb + 8 : emb + 12].reshape(-1)
    late = late[:, BIAS_COLUMN : BIAS_COLUMN + 2].T

    return (
        embeddings,
        input_grad,
        grad_qkv,
        grad_out,
        grad_up,
        grad_down,
        late,
        vec_grad[4],
        grad_up_bias,
        vec_grad[5],
        vec_grad[0:2],
        vec_grad[2:4],
        grad_proj,
    )


def solution(mesh):
    rows = P(None, ("dp", "tensor"), None)
    shapes = (
        P(None, "dp", "tensor"),
        P("tensor", "dp"),
        P("dp", "tensor"),
        P("tensor", "dp"),
        P(None, "dp"),
        P("dp"),
        P("dp"),
        P("dp"),
        P(None, "dp"),
        P(None, "dp"),
        P("dp", None),
    )
    return jax.shard_map(
        per_device,
        mesh=mesh,
        in_specs=(rows, *shapes, P(None, "dp", None), rows),
        out_specs=(rows, rows, *shapes),
        check_vma=False,
    )
```

time: 427 us -> 353 us (0.83)
  waiting for transfers between devices: 139 us -> 59.1 us
  Pallas kernels: 137 us -> 179 us
  starting transfers between devices: 82.7 us -> 42 us
  other arithmetic: 29.3 us -> 38.2 us
    pallas_call x7 -> x26, Pallas kernels: 137 us -> 179 us  [the longest x15 179 us: kernel_call(): pl.pallas_call(run, out_shape=outs, in_specs=[*specs, *[ANY] * len(ties)]...]
    ppermute x16 -> x8, waiting for transfers between devices: 44.8 us -> 11.5 us  [swap_y(): return lax.ppermute(value, 'dp', [(i, i ^ 1) for i in range(count)])]
    ppermute x42 -> x29, waiting for transfers between devices: 55.8 us -> 28.8 us  [swap(): return lax.ppermute(value, 'tensor', [(i, i ^ bit) for i in range(count)])]
    ppermute x30 -> x16, starting transfers between devices: 44.5 us -> 21.1 us  [swap_z(): return lax.ppermute(value, 'dp', [(i, i ^ 2 * bits) for i in range(count)])]
    ppermute x30 -> x16, waiting for transfers between devices: 38.8 us -> 18.8 us  [swap_z(): return lax.ppermute(value, 'dp', [(i, i ^ 2 * bits) for i in range(count)])]
    unnamed x115 -> x138, local copies, waits for them, and re-layouts: 6.05 us -> 17.1 us
    ppermute x16 -> x8, starting transfers between devices: 15.8 us -> 5.85 us  [swap_y(): return lax.ppermute(value, 'dp', [(i, i ^ 1) for i in range(count)])]
    ppermute x42 -> x29, starting transfers between devices: 22.4 us -> 15.1 us  [swap(): return lax.ppermute(value, 'tensor', [(i, i ^ bit) for i in range(count)])]
  transfers between devices with their start and end apart: 88 -> 53, of which waited for: 32 -> 18; matrix products, arithmetic and copies ran while one was open for 10% -> 11% of each run, Pallas kernels for 23% -> 44%
where the time goes in v2:
time: 353 us; the launch traced here: 349 us
  Pallas kernels  179 us (51%)
  waiting for transfers between devices  59.1 us (17%)
  starting transfers between devices  42 us (12%)
  other arithmetic  38.2 us (11%)
  local copies, waits for them, and re-layouts  28.6 us (8%)
    pallas_call x15, Pallas kernels, kernel_call(): pl.pallas_call(run, out_shape=outs, in_specs=[*specs, *[ANY] * len(ties)]...  179 us
    ppermute x29, waiting for transfers between devices, swap(): return lax.ppermute(value, 'tensor', [(i, i ^ bit) for i in range(count)])  28.8 us
    ppermute x16, starting transfers between devices, swap_z(): return lax.ppermute(value, 'dp', [(i, i ^ 2 * bits) for i in range(count)])  21.1 us
    ppermute x16, waiting for transfers between devices, swap_z(): return lax.ppermute(value, 'dp', [(i, i ^ 2 * bits) for i in range(count)])  18.8 us
    unnamed x138, local copies, waits for them, and re-layouts  17.1 us
    ppermute x29, starting transfers between devices, swap(): return lax.ppermute(value, 'tensor', [(i, i ^ bit) for i in range(count)])  15.1 us
    ppermute x8, waiting for transfers between devices, swap_y(): return lax.ppermute(value, 'dp', [(i, i ^ 1) for i in range(count)])  11.5 us
    another operation x3, other arithmetic  9.35 us
  transfers between devices with their start and end apart: 53, of which 18 were waited for; matrix products, arithmetic and copies ran while one was open for 11% of the time, Pallas kernels for 44%

profile of v2, /device:TPU:0, one launch (start us, length us, event | category | flops | bytes accessed | tf_op | source)
XLA Modules:
  0.0 348.6 jit_solution(4824224033450748835)
XLA Ops:
  2.0 3.0 collective-permute-start.4
  5.6 2.0 shard_map.237.refs_2_
  7.6 1.6 collective-permute-start
  9.2 2.6 collective-permute-start.1
  12.7 1.6 shard_map.238.refs_2_
  15.0 1.6 shard_map.239
  16.6 4.8 %collective-permute-done.1 = bf16[96,640]{1,0:T(8,128)(2,1)S(1)} collective-permute-done((bf16[96,640]{1,0:T(8,128)(2,1)}, bf16[96,640]{1,0:T(8,128)(2,1)S(1)}, u32[]{:S(2)}, u32[]{:S(2)}) %collective-permute-start.1) | collective-permute-done | bytes 122912 | tf_op jit(solution)/shard_map/ppermute | solution.py:795
  22.7 1.6 collective-permute-start.3
  24.7 1.7 pad_maximum_fusion.5.refs_7_
  26.4 2.6 collective-permute-start.9
  30.3 1.8 pad_maximum_fusion.6.refs_8_.refs_5_
  32.0 4.3 %collective-permute-done.3.refs_2_ = bf16[4,96,640]{2,1,0:T(8,128)(2,1)} collective-permute-done((bf16[4,96,640]{2,1,0:T(8,128)(2,1)S(1)}, bf16[4,96,640]{2,1,0:T(8,128)(2,1)}, u32[]{:S(2)}, u32[]{:S(2)}) %collective-permute-start.3) | collective-permute-done | bytes 491552 | tf_op jit(solution)/shard_map/ppermute | solution.py:790
  37.2 5.3 %shard_map.240 = (bf16[576,1536]{1,0:T(8,128)(2,1)}, bf16[576,768]{1,0:T(8,128)(2,1)}, bf16[16,768]{1,0:T(8,128)(2,1)}, bf16[768,640]{1,0:T(8,128)(2,1)}) custom-call(s32[15]{0:T(128)} %stack.115.refs_0_, bf16[4,96,640]{2,1,0:T(8,128)(2,1)} %copy-done.41, bf16[4,96,640]{2,1,0:T(8,128)(2,1)} %collective-permute-done.3.refs_2_, bf16[384,768]{1,0:T(8,128)(2,1)} %copy-done.4, ...), custom_call_target="tpu_custom_call" | custom-call | tf_op jit(solution)/shard_map/pallas_call | solution.py:40
  42.5 4.4 %collective-permute-done.9.refs_4_ = bf16[2,96,1024]{2,1,0:T(8,128)(2,1)S(1)} collective-permute-done((bf16[2,96,1024]{2,1,0:T(8,128)(2,1)}, bf16[2,96,1024]{2,1,0:T(8,128)(2,1)S(1)}, u32[]{:S(2)}, u32[]{:S(2)}) %collective-permute-start.9) | collective-permute-done | bytes 393248 | tf_op jit(solution)/shard_map/ppermute | solution.py:795
  53.4 14.8 %shard_map.242 = (bf16[192,768]{1,0:T(8,128)(2,1)}, bf16[192,768]{1,0:T(8,128)(2,1)}, f32[8,1536]{1,0:T(8,128)}) custom-call(bf16[576,1536]{1,0:T(8,128)(2,1)} %get-tuple-element.149.refs_0_.refs_1_, bf16[16,1536]{1,0:T(8,128)(2,1)} %get-tuple-element.345.refs_1_.refs_7_, bf16[16,1536]{1,0:T(8,128)(2,1)} %get-tuple-element.344.refs_2_.refs_8_, ...), custom_call_target="tpu_custom_call" | custom-call | tf_op jit(solution)/shard_map/pallas_call | solution.py:40
  68.6 2.1 collective-permute-done.10.refs_3_
  72.7 2.2 pad_maximum_fusion.1
  77.1 5.2 %shard_map.244 = (bf16[576,1536]{1,0:T(8,128)(2,1)}, bf16[576,768]{1,0:T(8,128)(2,1)}) custom-call(s32[10]{0:T(128)} %stack.127.refs_0_, bf16[768,640]{1,0:T(8,128)(2,1)} %get-tuple-element.157.refs_1_, bf16[384,768]{1,0:T(8,128)(2,1)} %copy-done.4, bf16[384,768]{1,0:T(8,128)(2,1)} %copy-done.7, bf16[384,768]{1,0:T(8,128)(2,1)} %copy-done.8, ...), custom_call_target="tpu_custom_call" | custom-call | tf_op jit(solution)/shard_map/pallas_call | solution.py:40
  82.3 14.5 %shard_map.245 = (bf16[192,768]{1,0:T(8,128)(2,1)}, bf16[192,768]{1,0:T(8,128)(2,1)}, f32[8,1536]{1,0:T(8,128)}) custom-call(bf16[576,1536]{1,0:T(8,128)(2,1)} %get-tuple-element.159.refs_0_.refs_1_, bf16[16,1536]{1,0:T(8,128)(2,1)} %get-tuple-element.345.refs_1_.refs_7_, bf16[16,1536]{1,0:T(8,128)(2,1)} %get-tuple-element.344.refs_2_.refs_8_, ...), custom_call_target="tpu_custom_call" | custom-call | tf_op jit(solution)/shard_map/pallas_call | solution.py:40
  96.8 2.4 collective-permute-done.13.refs_3_
  101.2 1.9 slice.204.refs_0_
  109.2 14.3 %shard_map.248 = (f32[768,768]{1,0:T(8,128)}, f32[768,1]{1,0:T(8,128)}, bf16[768,768]{1,0:T(8,128)(2,1)}, f32[768,768]{1,0:T(8,128)}, bf16[2,768,768]{2,1,0:T(8,...) custom-call(s32[15]{0:T(128)} %stack.115.refs_0_, ...), custom_call_target="tpu_custom_call" | custom-call | tf_op jit(solution)/shard_map/pallas_call | solution.py:40
  125.3 13.9 %collective-permute-done.24.refs_10_ = bf16[4,96,896]{2,1,0:T(8,128)(2,1)S(1)} collective-permute-done((bf16[4,96,896]{2,1,0:T(8,128)(2,1)}, bf16[4,96,896]{2,1,0:T(8,128)(2,1)S(1)}, u32[]{:S(2)}, u32[]{:S(2)}) %collective-permute-start.24) | collective-permute-done | bytes 688160 | tf_op jit(solution)/shard_map/ppermute | solution.py:785
  140.6 1.5 slice.205
  142.2 2.1 collective-permute-done.25.refs_11_.refs_9_
  145.6 22.2 %shard_map.250 = (bf16[384,128]{1,0:T(8,128)(2,1)}, bf16[384,128]{1,0:T(8,128)(2,1)}, bf16[768,768]{1,0:T(8,128)(2,1)}, f32[768,768]{1,0:T(8,128)}, bf16[2,768,7...) custom-call(s32[15]{0:T(128)} %stack.115.refs_0_, ...), custom_call_target="tpu_custom_call" | custom-call | tf_op jit(solution)/shard_map/pallas_call | solution.py:40
  168.0 15.1 %shard_map.251 = (bf16[2,4,2,96,768]{4,3,2,1,0:T(8,128)(2,1)}, f32[768,768]{1,0:T(8,128)}, f32[8,768]{1,0:T(8,128)}) custom-call(s32[15]{0:T(128)} %stack.115.refs_0_, bf16[768,768]{1,0:T(8,128)(2,1)} %get-tuple-element.196.refs_1_, bf16[768,768]{1,0:T(8,128)(2,1)} %get-tuple-element.190.refs_1_.refs_2_, bf16[2,768,768]{2,1,0:T(8,128)(2,1)} %get-tuple-element.197.refs_3_, ...), custom_call_target="tpu_custom_call" | custom-call | tf_op jit(solution)/shard_map/pallas_call | solution.py:40
  183.6 1.9 fusion.refs_22_
  186.6 20.7 %shard_map.252 = (bf16[2,4,2,96,768]{4,3,2,1,0:T(8,128)(2,1)}, f32[768,768]{1,0:T(8,128)}, bf16[192,768]{1,0:T(8,128)(2,1)}, bf16[192,768]{1,0:T(8,128)(2,1)}, b...) custom-call(s32[15]{0:T(128)} %stack.115.refs_0_, ...), custom_call_target="tpu_custom_call" | custom-call | tf_op jit(solution)/shard_map/pallas_call | solution.py:40
  207.3 6.4 %collective-permute-done.30.refs_6_ = bf16[4,2,96,768]{3,2,1,0:T(8,128)(2,1)} collective-permute-done((bf16[4,2,96,768]{3,2,1,0:T(8,128)(2,1)S(1)}, bf16[4,2,96,768]{3,2,1,0:T(8,128)(2,1)}, u32[]{:S(2)}, u32[]{:S(2)}) %collective-permute-start.30) | collective-permute-done | bytes 1179680 | tf_op jit(solution)/shard_map/ppermute | solution.py:790
  213.7 3.0 add_bitcast_fusion
  219.2 3.4 fusion.20
  224.1 2.0 collective-permute-start.36
  226.1 1.9 collective-permute-start.37
  228.9 25.3 %shard_map.254 = (bf16[4,96,768]{2,1,0:T(8,128)(2,1)}, bf16[4,96,768]{2,1,0:T(8,128)(2,1)}, bf16[576,1536]{1,0:T(8,128)(2,1)}, f32[192,128]{1,0:T(8,128)}) custom-call(s32[15]{0:T(128)} %stack.115.refs_0_, bf16[576,1536]{1,0:T(8,128)(2,1)} %get-tuple-element.159.refs_0_.refs_1_, bf16[192,768]{1,0:T(8,128)(2,1)} %get-tuple-element.167.refs_4_.refs_2_, ...), custom_call_target="tpu_custom_call" | custom-call | tf_op jit(solution)/shard_map/pallas_call | solution.py:40
  255.2 3.3 fusion.19
  258.7 2.7 collective-permute-start.41
  261.4 1.7 collective-permute-start.42
  267.0 25.6 %shard_map.256 = (bf16[4,96,896]{2,1,0:T(8,128)(2,1)}, bf16[4,96,896]{2,1,0:T(8,128)(2,1)}, bf16[576,1536]{1,0:T(8,128)(2,1)}) custom-call(s32[15]{0:T(128)} %stack.115.refs_0_, bf16[576,1536]{1,0:T(8,128)(2,1)} %get-tuple-element.149.refs_0_.refs_1_, bf16[192,768]{1,0:T(8,128)(2,1)} %get-tuple-element.156.refs_6_.refs_3_.refs_2_, ...), custom_call_target="tpu_custom_call" | custom-call | tf_op jit(solution)/shard_map/pallas_call | solution.py:40
  297.3 8.1 %shard_map.258 = (f32[768,768]{1,0:T(8,128)}, bf16[768,768]{1,0:T(8,128)(2,1)}) custom-call(bf16[576,1536]{1,0:T(8,128)(2,1)} %get-tuple-element.242.refs_0_, bf16[576,1536]{1,0:T(8,128)(2,1)} %get-tuple-element.237.refs_20_.refs_1_, bf16[576,768]{1,0:T(8,128)(2,1)} %get-tuple-element.243.refs_2_, bf16[576,768]{1,0:T(8,128)(2,1)} %get-tuple-element.244.refs_3_, ...), custom_call_target="tpu_custom_call" | custom-call | tf_op jit(solution)/shard_map/pallas_call | solution.py:40
  305.4 4.0 %collective-permute-done.43.refs_2_ = bf16[4,96,768]{2,1,0:T(8,128)(2,1)S(1)} collective-permute-done((bf16[4,96,768]{2,1,0:T(8,128)(2,1)S(1)}, bf16[4,96,768]{2,1,0:T(8,128)(2,1)S(1)}, u32[]{:S(2)}, u32[]{:S(2)}) %collective-permute-start.43) | collective-permute-done | bytes 589856 | tf_op jit(solution)/shard_map/ppermute | solution.py:785
  310.4 2.6 fusion.17
  316.0 2.7 fusion.16
  318.8 2.6 collective-permute-start.48
  321.4 1.8 collective-permute-start.49
  325.2 3.5 collective-permute-done.47.refs_0_
  328.7 5.7 %collective-permute-done.48.refs_1_ = bf16[96,896]{1,0:T(8,128)(2,1)S(1)} collective-permute-done((bf16[96,896]{1,0:T(8,128)(2,1)S(1)}, bf16[96,896]{1,0:T(8,128)(2,1)S(1)}, u32[]{:S(2)}, u32[]{:S(2)}) %collective-permute-start.48) | collective-permute-done | bytes 172064 | tf_op jit(solution)/shard_map/ppermute | solution.py:795
  345.7 2.7 shard_map.261
  (284 shorter events, 64.3 us)
Async XLA Ops:
  2.0 19.4 %collective-permute-start.4 = (bf16[384,768]{1,0:T(8,128)(2,1)S(1)}, bf16[384,768]{1,0:T(8,128)(2,1)S(1)}, u32[]{:S(2)}, u32[]{:S(2)}) collective-permute-start(bf16[384,768]{1,0:T(8,128)(2,1)S(1)} %get-tuple-element.325), channel_id=1, source_target_pairs={{0,2},{1,3},{2,0},{3,1},{4,6},{5,7},{6,4},{7,5},{8,10},{9,11},{10,... | collective-permute-start | bytes 1769480 | tf_op jit(solution)/shard_map/ppermute | solution.py:785
  7.6 9.0 %collective-permute-start = (bf16[96,640]{1,0:T(8,128)(2,1)}, bf16[96,640]{1,0:T(8,128)(2,1)S(1)}, u32[]{:S(2)}, u32[]{:S(2)}) collective-permute-start(bf16[96,640]{1,0:T(8,128)(2,1)} %shard_map.237.refs_2_), channel_id=1, source_target_pairs={{0,8},{4,12},{8,0},{12,4},{16,24},{20,28},{24,16},{28,20},{1,9},{5... | collective-permute-start | bytes 368648 | tf_op jit(solution)/shard_map/ppermute | solution.py:795
  9.2 12.3 %collective-permute-start.1 = (bf16[96,640]{1,0:T(8,128)(2,1)}, bf16[96,640]{1,0:T(8,128)(2,1)S(1)}, u32[]{:S(2)}, u32[]{:S(2)}) collective-permute-start(bf16[96,640]{1,0:T(8,128)(2,1)} %shard_map.237.refs_2_), channel_id=1, source_target_pairs={{0,16},{4,20},{8,24},{12,28},{16,0},{20,4},{24,8},{28,12},{1,17},{... | collective-permute-start | bytes 368648 | tf_op jit(solution)/shard_map/ppermute | solution.py:795
  11.8 9.8 %collective-permute-start.2 = (bf16[96,640]{1,0:T(8,128)(2,1)}, bf16[96,640]{1,0:T(8,128)(2,1)S(1)}, u32[]{:S(2)}, u32[]{:S(2)}) collective-permute-start(bf16[96,640]{1,0:T(8,128)(2,1)} %shard_map.237.refs_2_), channel_id=1, source_target_pairs={{0,24},{4,28},{8,16},{12,20},{16,8},{20,12},{24,0},{28,4},{1,25},{... | collective-permute-start | bytes 368648 | tf_op jit(solution)/shard_map/ppermute | solution.py:795
  14.3 10.3 %collective-permute-start.7 = (bf16[96,1024]{1,0:T(8,128)(2,1)}, bf16[96,1024]{1,0:T(8,128)(2,1)S(1)}, u32[]{:S(2)}, u32[]{:S(2)}) collective-permute-start(bf16[96,1024]{1,0:T(8,128)(2,1)} %shard_map.238.refs_2_), channel_id=1, source_target_pairs={{0,8},{4,12},{8,0},{12,4},{16,24},{20,28},{24,16},{28,20},{1,9},{5... | collective-permute-start | bytes 589832 | tf_op jit(solution)/shard_map/ppermute | solution.py:795
  16.6 15.4 %collective-permute-start.5 = (bf16[384,768]{1,0:T(8,128)(2,1)S(1)}, bf16[384,768]{1,0:T(8,128)(2,1)S(1)}, u32[]{:S(2)}, u32[]{:S(2)}) collective-permute-start(bf16[384,768]{1,0:T(8,128)(2,1)S(1)} %get-tuple-element.326.refs_3_.refs_2_.refs_1_.refs_9_), channel_id=1, source_target_pairs={{0,1},{1,0},{2,3},{3,2},{4,5},{5,4},{6,7},{7,6},{8,9},{9,8},{10,11... | collective-permute-start | bytes 1769480 | tf_op jit(solution)/shard_map/ppermute | solution.py:785
  21.4 8.8 %collective-permute-start.8 = (bf16[96,896]{1,0:T(8,128)(2,1)}, bf16[96,896]{1,0:T(8,128)(2,1)}, u32[]{:S(2)}, u32[]{:S(2)}) collective-permute-start(bf16[96,896]{1,0:T(8,128)(2,1)} %shard_map.239), channel_id=1, source_target_pairs={{0,8},{4,12},{8,0},{12,4},{16,24},{20,28},{24,16},{28,20},{1,9},{5... | collective-permute-start | bytes 516104 | tf_op jit(solution)/shard_map/ppermute | solution.py:795
  21.5 14.9 %collective-permute-start.6 = (bf16[384,768]{1,0:T(8,128)(2,1)S(1)}, bf16[384,768]{1,0:T(8,128)(2,1)S(1)}, u32[]{:S(2)}, u32[]{:S(2)}) collective-permute-start(bf16[384,768]{1,0:T(8,128)(2,1)S(1)} %collective-permute-done.4.refs_4_.refs_3_.refs_2_.refs_10_), channel_id=1, source_target_pairs={{0,1},{1,0},{2,3},{3,2},{4,5},{5,4},{6,7},{7,6},{8,9},{9,8},{10,11... | collective-permute-start | bytes 1769480 | tf_op jit(solution)/shard_map/ppermute | solution.py:785
  22.7 13.7 %collective-permute-start.3 = (bf16[4,96,640]{2,1,0:T(8,128)(2,1)S(1)}, bf16[4,96,640]{2,1,0:T(8,128)(2,1)}, u32[]{:S(2)}, u32[]{:S(2)}) collective-permute-start(bf16[4,96,640]{2,1,0:T(8,128)(2,1)S(1)} %pad_maximum_fusion.4.refs_1_), channel_id=1, source_target_pairs={{0,4},{4,0},{8,12},{12,8},{16,20},{20,16},{24,28},{28,24},{1,5},{5... | collective-permute-start | bytes 1474568 | tf_op jit(solution)/shard_map/ppermute | solution.py:790
  26.4 20.6 %collective-permute-start.9 = (bf16[2,96,1024]{2,1,0:T(8,128)(2,1)}, bf16[2,96,1024]{2,1,0:T(8,128)(2,1)S(1)}, u32[]{:S(2)}, u32[]{:S(2)}) collective-permute-start(bf16[2,96,1024]{2,1,0:T(8,128)(2,1)} %pad_maximum_fusion.5.refs_7_), channel_id=1, source_target_pairs={{0,16},{4,20},{8,24},{12,28},{16,0},{20,4},{24,8},{28,12},{1,17},{... | collective-permute-start | bytes 1179656 | tf_op jit(solution)/shard_map/ppermute | solution.py:795
  47.7 23.0 %collective-permute-start.10 = (bf16[768,640]{1,0:T(8,128)(2,1)}, bf16[768,640]{1,0:T(8,128)(2,1)S(1)}, u32[]{:S(2)}, u32[]{:S(2)}) collective-permute-start(bf16[768,640]{1,0:T(8,128)(2,1)} %get-tuple-element.154), channel_id=1, source_target_pairs={{0,2},{1,3},{2,0},{3,1},{4,6},{5,7},{6,4},{7,5},{8,10},{9,11},{10,... | collective-permute-start | bytes 2949128 | tf_op jit(solution)/shard_map/ppermute | solution.py:785
  50.0 18.6 %collective-permute-start.11 = (bf16[4,96,1024]{2,1,0:T(8,128)(2,1)S(1)}, bf16[4,96,1024]{2,1,0:T(8,128)(2,1)}, u32[]{:S(2)}, u32[]{:S(2)}) collective-permute-start(bf16[4,96,1024]{2,1,0:T(8,128)(2,1)S(1)} %pad_maximum_fusion.2.refs_3_.refs_4_), channel_id=1, source_target_pairs={{0,4},{4,0},{8,12},{12,8},{16,20},{20,16},{24,28},{28,24},{1,5},{5... | collective-permute-start | bytes 2359304 | tf_op jit(solution)/shard_map/ppermute | solution.py:790
  51.9 16.3 %collective-permute-start.12 = (bf16[2,96,896]{2,1,0:T(8,128)(2,1)S(1)}, bf16[2,96,896]{2,1,0:T(8,128)(2,1)S(1)}, u32[]{:S(2)}, u32[]{:S(2)}) collective-permute-start(bf16[2,96,896]{2,1,0:T(8,128)(2,1)S(1)} %copy-done.17), channel_id=1, source_target_pairs={{0,16},{4,20},{8,24},{12,28},{16,0},{20,4},{24,8},{28,12},{1,17},{... | collective-permute-start | bytes 1032200 | tf_op jit(solution)/shard_map/ppermute | solution.py:795
  74.9 24.2 %collective-permute-start.13 = (bf16[4,96,1408]{2,1,0:T(8,128)(2,1)}, bf16[4,96,1408]{2,1,0:T(8,128)(2,1)S(1)}, u32[]{:S(2)}, u32[]{:S(2)}) collective-permute-start(bf16[4,96,1408]{2,1,0:T(8,128)(2,1)} %pad_maximum_fusion.1), channel_id=1, source_target_pairs={{0,2},{1,3},{2,0},{3,1},{4,6},{5,7},{6,4},{7,5},{8,10},{9,11},{10,... | collective-permute-start | bytes 3244040 | tf_op jit(solution)/shard_map/ppermute | solution.py:785
  75.6 21.1 %collective-permute-start.15 = (bf16[4,96,1024]{2,1,0:T(8,128)(2,1)S(1)}, bf16[4,96,1024]{2,1,0:T(8,128)(2,1)}, u32[]{:S(2)}, u32[]{:S(2)}) collective-permute-start(bf16[4,96,1024]{2,1,0:T(8,128)(2,1)S(1)} %copy-done.2), channel_id=1, source_target_pairs={{0,1},{1,0},{2,3},{3,2},{4,5},{5,4},{6,7},{7,6},{8,9},{9,8},{10,11... | collective-permute-start | bytes 2359304 | tf_op jit(solution)/shard_map/ppermute | solution.py:785
  75.7 21.0 %collective-permute-start.16 = (bf16[4,96,1024]{2,1,0:T(8,128)(2,1)}, bf16[4,96,1024]{2,1,0:T(8,128)(2,1)}, u32[]{:S(2)}, u32[]{:S(2)}) collective-permute-start(bf16[4,96,1024]{2,1,0:T(8,128)(2,1)} %get-tuple-element.164.refs_9_.refs_15_), channel_id=1, source_target_pairs={{0,1},{1,0},{2,3},{3,2},{4,5},{5,4},{6,7},{7,6},{8,9},{9,8},{10,11... | collective-permute-start | bytes 2359304 | tf_op jit(solution)/shard_map/ppermute | solution.py:785
  76.3 20.5 %collective-permute-start.14 = (bf16[4,96,896]{2,1,0:T(8,128)(2,1)S(1)}, bf16[4,96,896]{2,1,0:T(8,128)(2,1)S(1)}, u32[]{:S(2)}, u32[]{:S(2)}) collective-permute-start(bf16[4,96,896]{2,1,0:T(8,128)(2,1)S(1)} %constant_dynamic-update-slice_fusion.refs_7_.refs_3_.refs_1_), channel_id=1, source_target_pairs={{0,4},{4,0},{8,12},{12,8},{16,20},{20,16},{24,28},{28,24},{1,5},{5... | collective-permute-start | bytes 2064392 | tf_op jit(solution)/shard_map/ppermute | solution.py:790
  76.4 20.3 %collective-permute-start.17 = (bf16[4,96,896]{2,1,0:T(8,128)(2,1)S(1)}, bf16[4,96,896]{2,1,0:T(8,128)(2,1)}, u32[]{:S(2)}, u32[]{:S(2)}) collective-permute-start(bf16[4,96,896]{2,1,0:T(8,128)(2,1)S(1)} %constant_dynamic-update-slice_fusion.refs_7_.refs_3_.refs_1_), channel_id=1, source_target_pairs={{0,1},{1,0},{2,3},{3,2},{4,5},{5,4},{6,7},{7,6},{8,9},{9,8},{10,11... | collective-permute-start | bytes 2064392 | tf_op jit(solution)/shard_map/ppermute | solution.py:785
  100.1 4.8 %collective-permute-start.18 = (bf16[4,96,1408]{2,1,0:T(8,128)(2,1)}, bf16[4,96,1408]{2,1,0:T(8,128)(2,1)S(1)}, u32[]{:S(2)}, u32[]{:S(2)}) collective-permute-start(bf16[4,96,1408]{2,1,0:T(8,128)(2,1)} %get-tuple-element.168.refs_16_.refs_8_), channel_id=1, source_target_pairs={{0,1},{1,0},{2,3},{3,2},{4,5},{5,4},{6,7},{7,6},{8,9},{9,8},{10,11... | collective-permute-start | bytes 3244040 | tf_op jit(solution)/shard_map/ppermute | solution.py:785
  100.1 4.7 %collective-permute-start.19 = (bf16[4,96,896]{2,1,0:T(8,128)(2,1)}, bf16[4,96,896]{2,1,0:T(8,128)(2,1)S(1)}, u32[]{:S(2)}, u32[]{:S(2)}) collective-permute-start(bf16[4,96,896]{2,1,0:T(8,128)(2,1)} %get-tuple-element.169.refs_2_), channel_id=1, source_target_pairs={{0,1},{1,0},{2,3},{3,2},{4,5},{5,4},{6,7},{7,6},{8,9},{9,8},{10,11... | collective-permute-start | bytes 2064392 | tf_op jit(solution)/shard_map/ppermute | solution.py:785
  100.6 4.2 %collective-permute-start.21 = (bf16[192,768]{1,0:T(8,128)(2,1)}, bf16[192,768]{1,0:T(8,128)(2,1)S(1)}, u32[]{:S(2)}, u32[]{:S(2)}) collective-permute-start(bf16[192,768]{1,0:T(8,128)(2,1)} %get-tuple-element.170.refs_3_), channel_id=1, source_target_pairs={{0,1},{1,0},{2,3},{3,2},{4,5},{5,4},{6,7},{7,6},{8,9},{9,8},{10,11... | collective-permute-start | bytes 884744 | tf_op jit(solution)/shard_map/ppermute | solution.py:785
  106.8 18.5 %collective-permute-start.23 = (bf16[4,96,896]{2,1,0:T(8,128)(2,1)}, bf16[4,96,896]{2,1,0:T(8,128)(2,1)S(1)}, u32[]{:S(2)}, u32[]{:S(2)}) collective-permute-start(bf16[4,96,896]{2,1,0:T(8,128)(2,1)} %get-tuple-element.176.refs_12_.refs_16_.refs_18_), channel_id=1, source_target_pairs={{0,2},{1,3},{2,0},{3,1},{4,6},{5,7},{6,4},{7,5},{8,10},{9,11},{10,... | collective-permute-start | bytes 2064392 | tf_op jit(solution)/shard_map/ppermute | solution.py:785
  107.7 31.5 %collective-permute-start.24 = (bf16[4,96,896]{2,1,0:T(8,128)(2,1)}, bf16[4,96,896]{2,1,0:T(8,128)(2,1)S(1)}, u32[]{:S(2)}, u32[]{:S(2)}) collective-permute-start(bf16[4,96,896]{2,1,0:T(8,128)(2,1)} %get-tuple-element.177.refs_13_.refs_17_.refs_19_), channel_id=1, source_target_pairs={{0,2},{1,3},{2,0},{3,1},{4,6},{5,7},{6,4},{7,5},{8,10},{9,11},{10,... | collective-permute-start | bytes 2064392 | tf_op jit(solution)/shard_map/ppermute | solution.py:785
  108.8 15.0 %collective-permute-start.22 = (bf16[4,96,768]{2,1,0:T(8,128)(2,1)}, bf16[4,96,768]{2,1,0:T(8,128)(2,1)S(1)}, u32[]{:S(2)}, u32[]{:S(2)}) collective-permute-start(bf16[4,96,768]{2,1,0:T(8,128)(2,1)} %get-tuple-element.189), channel_id=1, source_target_pairs={{0,4},{4,0},{8,12},{12,8},{16,20},{20,16},{24,28},{28,24},{1,5},{5... | collective-permute-start | bytes 1769480 | tf_op jit(solution)/shard_map/ppermute | solution.py:790
  140.1 4.2 %collective-permute-start.26 = (bf16[4,96,896]{2,1,0:T(8,128)(2,1)}, bf16[4,96,896]{2,1,0:T(8,128)(2,1)S(1)}, u32[]{:S(2)}, u32[]{:S(2)}) collective-permute-start(bf16[4,96,896]{2,1,0:T(8,128)(2,1)} %get-tuple-element.194.refs_12_.refs_20_), channel_id=1, source_target_pairs={{0,1},{1,0},{2,3},{3,2},{4,5},{5,4},{6,7},{7,6},{8,9},{9,8},{10,11... | collective-permute-start | bytes 2064392 | tf_op jit(solution)/shard_map/ppermute | solution.py:785
  140.1 4.2 %collective-permute-start.27 = (bf16[4,96,896]{2,1,0:T(8,128)(2,1)}, bf16[4,96,896]{2,1,0:T(8,128)(2,1)S(1)}, u32[]{:S(2)}, u32[]{:S(2)}) collective-permute-start(bf16[4,96,896]{2,1,0:T(8,128)(2,1)} %get-tuple-element.195.refs_13_.refs_21_), channel_id=1, source_target_pairs={{0,1},{1,0},{2,3},{3,2},{4,5},{5,4},{6,7},{7,6},{8,9},{9,8},{10,11... | collective-permute-start | bytes 2064392 | tf_op jit(solution)/shard_map/ppermute | solution.py:785
  167.8 15.8 %collective-permute-start.28 = (bf16[2,4,2,96,768]{4,3,2,1,0:T(8,128)(2,1)}, bf16[2,4,2,96,768]{4,3,2,1,0:T(8,128)(2,1)}, u32[]{:S(2)}, u32[]{:S(2)}) collective-permute-start(bf16[2,4,2,96,768]{4,3,2,1,0:T(8,128)(2,1)} %get-tuple-element.209), channel_id=1, source_target_pairs={{0,1},{1,0},{2,3},{3,2},{4,5},{5,4},{6,7},{7,6},{8,9},{9,8},{10,11... | collective-permute-start | bytes 7077896 | tf_op jit(solution)/shard_map/ppermute | solution.py:785
  183.2 24.1 %collective-permute-start.29 = (bf16[2,4,2,96,768]{4,3,2,1,0:T(8,128)(2,1)}, bf16[2,4,2,96,768]{4,3,2,1,0:T(8,128)(2,1)S(1)}, u32[]{:S(2)}, u32[]{:S(2)}) collective-permute-start(bf16[2,4,2,96,768]{4,3,2,1,0:T(8,128)(2,1)} %get-tuple-element.216), channel_id=1, source_target_pairs={{0,1},{1,0},{2,3},{3,2},{4,5},{5,4},{6,7},{7,6},{8,9},{9,8},{10,11... | collective-permute-start | bytes 7077896 | tf_op jit(solution)/shard_map/ppermute | solution.py:785
  185.5 28.2 %collective-permute-start.30 = (bf16[4,2,96,768]{3,2,1,0:T(8,128)(2,1)S(1)}, bf16[4,2,96,768]{3,2,1,0:T(8,128)(2,1)}, u32[]{:S(2)}, u32[]{:S(2)}) collective-permute-start(bf16[4,2,96,768]{3,2,1,0:T(8,128)(2,1)S(1)} %fusion.refs_22_), channel_id=1, source_target_pairs={{0,4},{4,0},{8,12},{12,8},{16,20},{20,16},{24,28},{28,24},{1,5},{5... | collective-permute-start | bytes 3538952 | tf_op jit(solution)/shard_map/ppermute | solution.py:790
  218.1 36.1 %collective-permute-start.34 = (bf16[4,2,96,896]{3,2,1,0:T(8,128)(2,1)}, bf16[4,2,96,896]{3,2,1,0:T(8,128)(2,1)}, u32[]{:S(2)}, u32[]{:S(2)}) collective-permute-start(bf16[4,2,96,896]{3,2,1,0:T(8,128)(2,1)} %pad_maximum_fusion.refs_15_), channel_id=1, source_target_pairs={{0,4},{4,0},{8,12},{12,8},{16,20},{20,16},{24,28},{28,24},{1,5},{5... | collective-permute-start | bytes 4128776 | tf_op jit(solution)/shard_map/ppermute | solution.py:790
  218.5 7.7 %collective-permute-start.31 = (bf16[2,192,768]{2,1,0:T(8,128)(2,1)S(1)}, bf16[2,192,768]{2,1,0:T(8,128)(2,1)S(1)}, u32[]{:S(2)}, u32[]{:S(2)}) collective-permute-start(bf16[2,192,768]{2,1,0:T(8,128)(2,1)S(1)} %copy-done.58), channel_id=1, source_target_pairs={{0,1},{1,0},{2,3},{3,2},{4,5},{5,4},{6,7},{7,6},{8,9},{9,8},{10,11... | collective-permute-start | bytes 1769480 | tf_op jit(solution)/shard_map/ppermute | solution.py:785
  218.7 10.2 %collective-permute-start.32 = (bf16[2,192,768]{2,1,0:T(8,128)(2,1)S(1)}, bf16[2,192,768]{2,1,0:T(8,128)(2,1)}, u32[]{:S(2)}, u32[]{:S(2)}) collective-permute-start(bf16[2,192,768]{2,1,0:T(8,128)(2,1)S(1)} %copy-done.59), channel_id=1, source_target_pairs={{0,1},{1,0},{2,3},{3,2},{4,5},{5,4},{6,7},{7,6},{8,9},{9,8},{10,11... | collective-permute-start | bytes 1769480 | tf_op jit(solution)/shard_map/ppermute | solution.py:785
  223.4 30.7 %collective-permute-start.35 = (bf16[2,96,768]{2,1,0:T(8,128)(2,1)}, bf16[2,96,768]{2,1,0:T(8,128)(2,1)}, u32[]{:S(2)}, u32[]{:S(2)}) collective-permute-start(bf16[2,96,768]{2,1,0:T(8,128)(2,1)} %get-tuple-element.324.refs_16_), channel_id=1, source_target_pairs={{0,8},{4,12},{8,0},{12,4},{16,24},{20,28},{24,16},{28,20},{1,9},{5... | collective-permute-start | bytes 884744 | tf_op jit(solution)/shard_map/ppermute | solution.py:795
  224.1 30.0 %collective-permute-start.36 = (bf16[2,96,768]{2,1,0:T(8,128)(2,1)S(1)}, bf16[2,96,768]{2,1,0:T(8,128)(2,1)}, u32[]{:S(2)}, u32[]{:S(2)}) collective-permute-start(bf16[2,96,768]{2,1,0:T(8,128)(2,1)S(1)} %get-tuple-element.323.refs_17_), channel_id=1, source_target_pairs={{0,16},{4,20},{8,24},{12,28},{16,0},{20,4},{24,8},{28,12},{1,17},{... | collective-permute-start | bytes 884744 | tf_op jit(solution)/shard_map/ppermute | solution.py:795
  226.1 28.1 %collective-permute-start.37 = (bf16[2,96,768]{2,1,0:T(8,128)(2,1)S(1)}, bf16[2,96,768]{2,1,0:T(8,128)(2,1)}, u32[]{:S(2)}, u32[]{:S(2)}) collective-permute-start(bf16[2,96,768]{2,1,0:T(8,128)(2,1)S(1)} %get-tuple-element.322.refs_18_), channel_id=1, source_target_pairs={{0,24},{4,28},{8,16},{12,20},{16,8},{20,12},{24,0},{28,4},{1,25},{... | collective-permute-start | bytes 884744 | tf_op jit(solution)/shard_map/ppermute | solution.py:795
  258.6 34.0 %collective-permute-start.40 = (bf16[2,96,896]{2,1,0:T(8,128)(2,1)S(1)}, bf16[2,96,896]{2,1,0:T(8,128)(2,1)S(1)}, u32[]{:S(2)}, u32[]{:S(2)}) collective-permute-start(bf16[2,96,896]{2,1,0:T(8,128)(2,1)S(1)} %get-tuple-element.321.refs_16_), channel_id=1, source_target_pairs={{0,8},{4,12},{8,0},{12,4},{16,24},{20,28},{24,16},{28,20},{1,9},{5... | collective-permute-start | bytes 1032200 | tf_op jit(solution)/shard_map/ppermute | solution.py:795
  258.7 33.9 %collective-permute-start.41 = (bf16[2,96,896]{2,1,0:T(8,128)(2,1)S(1)}, bf16[2,96,896]{2,1,0:T(8,128)(2,1)S(1)}, u32[]{:S(2)}, u32[]{:S(2)}) collective-permute-start(bf16[2,96,896]{2,1,0:T(8,128)(2,1)S(1)} %get-tuple-element.320.refs_17_), channel_id=1, source_target_pairs={{0,16},{4,20},{8,24},{12,28},{16,0},{20,4},{24,8},{28,12},{1,17},{... | collective-permute-start | bytes 1032200 | tf_op jit(solution)/shard_map/ppermute | solution.py:795
  261.4 31.2 %collective-permute-start.42 = (bf16[2,96,896]{2,1,0:T(8,128)(2,1)S(1)}, bf16[2,96,896]{2,1,0:T(8,128)(2,1)S(1)}, u32[]{:S(2)}, u32[]{:S(2)}) collective-permute-start(bf16[2,96,896]{2,1,0:T(8,128)(2,1)S(1)} %get-tuple-element.319.refs_18_), channel_id=1, source_target_pairs={{0,24},{4,28},{8,16},{12,20},{16,8},{20,12},{24,0},{28,4},{1,25},{... | collective-permute-start | bytes 1032200 | tf_op jit(solution)/shard_map/ppermute | solution.py:795
  263.1 29.6 %collective-permute-start.38 = (bf16[4,96,768]{2,1,0:T(8,128)(2,1)}, bf16[4,96,768]{2,1,0:T(8,128)(2,1)S(1)}, u32[]{:S(2)}, u32[]{:S(2)}) collective-permute-start(bf16[4,96,768]{2,1,0:T(8,128)(2,1)} %get-tuple-element.241), channel_id=1, source_target_pairs={{0,4},{4,0},{8,12},{12,8},{16,20},{20,16},{24,28},{28,24},{1,5},{5... | collective-permute-start | bytes 1769480 | tf_op jit(solution)/shard_map/ppermute | solution.py:790
  266.0 26.6 %collective-permute-start.39 = (bf16[96,768]{1,0:T(8,128)(2,1)S(1)}, bf16[96,768]{1,0:T(8,128)(2,1)S(1)}, u32[]{:S(2)}, u32[]{:S(2)}) collective-permute-start(bf16[96,768]{1,0:T(8,128)(2,1)S(1)} %fusion.12.refs_19_), channel_id=1, source_target_pairs={{0,2},{1,3},{2,0},{3,1},{4,6},{5,7},{6,4},{7,5},{8,10},{9,11},{10,... | collective-permute-start | bytes 442376 | tf_op jit(solution)/shard_map/ppermute | solution.py:785
  293.8 15.6 %collective-permute-start.44 = (bf16[4,96,896]{2,1,0:T(8,128)(2,1)}, bf16[4,96,896]{2,1,0:T(8,128)(2,1)S(1)}, u32[]{:S(2)}, u32[]{:S(2)}) collective-permute-start(bf16[4,96,896]{2,1,0:T(8,128)(2,1)} %get-tuple-element.250), channel_id=1, source_target_pairs={{0,4},{4,0},{8,12},{12,8},{16,20},{20,16},{24,28},{28,24},{1,5},{5... | collective-permute-start | bytes 2064392 | tf_op jit(solution)/shard_map/ppermute | solution.py:790
  296.1 13.3 %collective-permute-start.43 = (bf16[4,96,768]{2,1,0:T(8,128)(2,1)S(1)}, bf16[4,96,768]{2,1,0:T(8,128)(2,1)S(1)}, u32[]{:S(2)}, u32[]{:S(2)}) collective-permute-start(bf16[4,96,768]{2,1,0:T(8,128)(2,1)S(1)} %add_convert_fusion.3.refs_5_), channel_id=1, source_target_pairs={{0,2},{1,3},{2,0},{3,1},{4,6},{5,7},{6,4},{7,5},{8,10},{9,11},{10,... | collective-permute-start | bytes 1769480 | tf_op jit(solution)/shard_map/ppermute | solution.py:785
  318.7 9.9 %collective-permute-start.47 = (bf16[96,896]{1,0:T(8,128)(2,1)S(1)}, bf16[96,896]{1,0:T(8,128)(2,1)S(1)}, u32[]{:S(2)}, u32[]{:S(2)}) collective-permute-start(bf16[96,896]{1,0:T(8,128)(2,1)S(1)} %get-tuple-element.333), channel_id=1, source_target_pairs={{0,8},{4,12},{8,0},{12,4},{16,24},{20,28},{24,16},{28,20},{1,9},{5... | collective-permute-start | bytes 516104 | tf_op jit(solution)/shard_map/ppermute | solution.py:795
  318.8 15.6 %collective-permute-start.48 = (bf16[96,896]{1,0:T(8,128)(2,1)S(1)}, bf16[96,896]{1,0:T(8,128)(2,1)S(1)}, u32[]{:S(2)}, u32[]{:S(2)}) collective-permute-start(bf16[96,896]{1,0:T(8,128)(2,1)S(1)} %get-tuple-element.332), channel_id=1, source_target_pairs={{0,16},{4,20},{8,24},{12,28},{16,0},{20,4},{24,8},{28,12},{1,17},{... | collective-permute-start | bytes 516104 | tf_op jit(solution)/shard_map/ppermute | solution.py:795
  321.4 12.9 %collective-permute-start.49 = (bf16[96,896]{1,0:T(8,128)(2,1)S(1)}, bf16[96,896]{1,0:T(8,128)(2,1)S(1)}, u32[]{:S(2)}, u32[]{:S(2)}) collective-permute-start(bf16[96,896]{1,0:T(8,128)(2,1)S(1)} %get-tuple-element.331), channel_id=1, source_target_pairs={{0,24},{4,28},{8,16},{12,20},{16,8},{20,12},{24,0},{28,4},{1,25},{... | collective-permute-start | bytes 516104 | tf_op jit(solution)/shard_map/ppermute | solution.py:795
  323.2 15.1 %collective-permute-start.50 = (bf16[96,1024]{1,0:T(8,128)(2,1)S(1)}, bf16[96,1024]{1,0:T(8,128)(2,1)S(1)}, u32[]{:S(2)}, u32[]{:S(2)}) collective-permute-start(bf16[96,1024]{1,0:T(8,128)(2,1)S(1)} %copy-done.54), channel_id=1, source_target_pairs={{0,2},{1,3},{2,0},{3,1},{4,6},{5,7},{6,4},{7,5},{8,10},{9,11},{10,... | collective-permute-start | bytes 589832 | tf_op jit(solution)/shard_map/ppermute | solution.py:785
  324.3 21.3 %collective-permute-start.46 = (bf16[384,896]{1,0:T(8,128)(2,1)S(1)}, bf16[384,896]{1,0:T(8,128)(2,1)}, u32[]{:S(2)}, u32[]{:S(2)}) collective-permute-start(bf16[384,896]{1,0:T(8,128)(2,1)S(1)} %copy-done.32), channel_id=1, source_target_pairs={{0,2},{1,3},{2,0},{3,1},{4,6},{5,7},{6,4},{7,5},{8,10},{9,11},{10,... | collective-permute-start | bytes 2064392 | tf_op jit(solution)/shard_map/ppermute | solution.py:785
  340.7 4.2 %collective-permute-start.52 = (bf16[96,128]{1,0:T(8,128)(2,1)S(1)}, bf16[96,128]{1,0:T(8,128)(2,1)S(1)}, u32[]{:S(2)}, u32[]{:S(2)}) collective-permute-start(bf16[96,128]{1,0:T(8,128)(2,1)S(1)} %get-tuple-element.305), channel_id=1, source_target_pairs={{0,2},{1,3},{2,0},{3,1},{4,6},{5,7},{6,4},{7,5},{8,10},{9,11},{10,... | collective-permute-start | bytes 73736 | tf_op jit(solution)/shard_map/ppermute | solution.py:785
  (71 other events, 317.9 us)
